TPU v7x, 256 devices: a whole 4x4x8 slice. The times are simulated.
256 devices in a mesh: dp: 8 (over z), seq: 32 (over y, x, core).
Axes of the slice: x: 4, y: 4, z: 8, core: 2. Of those that a mesh axis runs over, the one named last changes fastest.
Arguments:
- projected: bfloat16 [8, 4096, 6144], P('dp', 'seq'), may hold values from -6 to 6
- conv_weight: float32 [4, 6144], replicated, may hold values from -3 to 3
- initial_memory: float32 [16, 128, 128], replicated, may hold values from -3 to 3
- log_forget: float32 [8, 16, 4096], P('dp', None, 'seq'), as said below
- log_momentum: float32 [8, 16, 4096], P('dp', None, 'seq'), as said below
- learn_rate: float32 [8, 16, 4096], P('dp', None, 'seq'), as said below
- cotangent: bfloat16 [8, 4096, 2048], P('dp', 'seq'), may hold values from -6 to 6
Outputs:
- output: bfloat16 [8, 4096, 2048], P('dp', 'seq')
- projected_grad: bfloat16 [8, 4096, 6144], P('dp', 'seq')
- conv_grad: float32 [4, 6144], replicated
- memory_grad: float32 [16, 128, 128], P(None, 'seq')
Inputs may be any that keep to these rules, and one draw needn't show every extreme that they name: `log_forget`: never positive. `log_momentum`: never positive. `learn_rate`: positive.
All inputs are finite; a program needn't handle non-finite values.
Results may differ from a plain program's by a relative error of at most 0.0056.
Values may be sent and summed in bfloat16 or wider, within the bound.
No kernel may reach another device: no remote copies, remote signals or barrier semaphores. Data moves between devices by JAX's collectives and lax.ppermute only.
A program may use at most 256 MiB of HBM per device.

v0:
```python
import jax
import jax.numpy as jnp
from jax import lax
from jax.sharding import PartitionSpec as P

DK = 128


def from_behind(value, axis, by):
    size = lax.axis_size(axis)
    pairs = [(i, i + by) for i in range(size) if 0 <= i + by < size]
    return lax.ppermute(value, axis, pairs)


def carried_in(value, axis, join, neutral, backward):
    count, mine = (lax.axis_size(axis), lax.axis_index(axis))
    pieces = jax.tree.map(lambda part: lax.all_gather(part, axis), value)
    if backward:
        pieces = jax.tree.map(lambda part: part[::-1], pieces)
        mine = count - 1 - mine
    running = jax.tree.map(
        lambda part, zero: jnp.full_like(part, 0) + jnp.asarray(zero, part.dtype), value, neutral
    )

    def step(position, running):
        longer = join(running, jax.tree.map(lambda part: part[position], pieces))
        return jax.tree.map(lambda new, old: jnp.where(position < mine, new, old), longer, running)

    return lax.fori_loop(0, count - 1, step, running)


def from_root(value, axis, source):
    kept = jnp.where(lax.axis_index(axis) == source, value, 0).astype(value.dtype)
    return lax.psum(kept, axis)


def features(extended, weights):
    kernel_width = weights.shape[0]
    length = extended.shape[0] - kernel_width + 1
    convolved = weights[0] * extended[0:length]
    for offset in range(1, kernel_width):
        convolved = convolved + weights[offset] * extended[offset : offset + length]
    active = jax.nn.silu(convolved)
    group_width = active.shape[1] // 3
    head_count = group_width // DK

    def normalize(section):
        shaped = section.reshape(length, head_count, DK)
        return shaped * lax.rsqrt(jnp.sum(shaped * shaped, axis=2, keepdims=True) + 1e-06)

    probe_vectors = normalize(active[:, :group_width]).astype(jnp.bfloat16)
    memory_keys = normalize(active[:, group_width : 2 * group_width]).astype(jnp.bfloat16)
    values = active[:, 2 * group_width :].reshape(length, head_count, DK).astype(jnp.bfloat16)
    return (probe_vectors, memory_keys, values)


def tables(forget, momentum):
    cum_forget = jnp.cumsum(forget, axis=1)
    cum_moment = jnp.cumsum(momentum, axis=1)
    positions = jnp.arange(forget.shape[1])
    causal = (positions[:, None] >= positions[None, :]).astype(jnp.float32)

    def decay_map(running):
        differences = running[:, :, None] - running[:, None, :]
        return jnp.exp(jnp.minimum(differences, 0.0)) * causal

    forget_map = decay_map(cum_forget)
    moment_map = decay_map(cum_moment)
    coupling = jnp.einsum("htr,hrs->hts", forget_map, moment_map, precision=lax.Precision.HIGHEST)
    start_forget = jnp.exp(cum_forget)
    start_moment = jnp.exp(cum_moment)
    carry_moment = jnp.einsum(
        "htr,hr->ht", forget_map, start_moment, precision=lax.Precision.HIGHEST
    )
    return (coupling, moment_map[:, -1, :], start_forget, start_moment, carry_moment)


def local_part(query_f, key_f, value_f, decay_tables, rates):
    coupling, moment_tail, start_forget, start_moment, carry_moment = decay_tables
    highest = lax.Precision.HIGHEST
    weighted = key_f * jnp.transpose(rates)[:, :, None]
    scores = jnp.einsum("thd,shd->hts", query_f, weighted, precision=highest)
    inside = jnp.einsum("hts,she->the", scores * coupling, value_f, precision=highest)
    memory_local = jnp.einsum(
        "shd,she->hde",
        weighted * jnp.transpose(coupling[:, -1, :])[:, :, None],
        value_f,
        precision=highest,
    )
    moment_local = jnp.einsum(
        "shd,she->hde",
        weighted * jnp.transpose(moment_tail)[:, :, None],
        value_f,
        precision=highest,
    )
    return (inside, memory_local, moment_local)


def expand_heads(scalars):
    return scalars[:, None, None]


def compose_forward(preceding, after_map):
    forget_one, carry_one, moment_one, memory_one, state_one = preceding
    forget_two, carry_second, moment_two, memory_two, state_two = after_map
    return (
        forget_two * forget_one,
        forget_two * carry_one + carry_second * moment_one,
        moment_two * moment_one,
        expand_heads(forget_two) * memory_one + expand_heads(carry_second) * state_one + memory_two,
        expand_heads(moment_two) * state_one + state_two,
    )


def compose_adjoint(preceding, after_map):
    forget_one, carry_one, moment_one, memory_one, state_one = preceding
    forget_two, carry_second, moment_two, memory_two, state_two = after_map
    return (
        forget_two * forget_one,
        carry_second * forget_one + moment_two * carry_one,
        moment_two * moment_one,
        expand_heads(forget_two) * memory_one + memory_two,
        expand_heads(carry_second) * memory_one + expand_heads(moment_two) * state_one + state_two,
    )


def own_rows(full_grad):
    row_count = full_grad.shape[1] // lax.axis_size("seq")
    return lax.dynamic_slice_in_dim(full_grad, lax.axis_index("seq") * row_count, row_count, 1)


def local(projected, conv_weight, initial_memory, log_forget, log_momentum, learn_rate, cotangent):
    highest = lax.Precision.HIGHEST
    row_block = projected[0]
    token_count = row_block.shape[0]
    kernel_width = conv_weight.shape[0]
    head_count = initial_memory.shape[0]
    rim_rows = row_block[token_count - (kernel_width - 1) :]
    borrowed = from_behind(rim_rows, "seq", 1)
    extended = jnp.concatenate([borrowed, row_block], axis=0).astype(jnp.float32)
    (probe_vectors, memory_keys, values), feature_pull = jax.vjp(features, extended, conv_weight)
    forget = log_forget[0]
    momentum = log_momentum[0]
    rates = learn_rate[0]
    decay_tables = tables(forget, momentum)
    coupling, moment_tail, start_forget, start_moment, carry_moment = decay_tables
    query_f = probe_vectors.astype(jnp.float32)
    key_f = memory_keys.astype(jnp.float32)
    value_f = values.astype(jnp.float32)

    def local_only(query_in, key_in, value_in):
        return local_part(query_in, key_in, value_in, decay_tables, rates)

    (inside, memory_local, moment_local), local_pull = jax.vjp(local_only, query_f, key_f, value_f)
    keep_forget = start_forget[:, -1]
    keep_moment = start_moment[:, -1]
    carry_last = carry_moment[:, -1]
    ones_heads = jnp.ones((head_count,), jnp.float32)
    zeros_heads = jnp.zeros((head_count,), jnp.float32)
    blank_matrix = jnp.zeros_like(memory_local)
    identity = (ones_heads, zeros_heads, ones_heads, blank_matrix, blank_matrix)
    element = (keep_forget, carry_last, keep_moment, memory_local, moment_local)
    before_maps = carried_in(element, "seq", compose_forward, identity, False)
    memory_in = expand_heads(before_maps[0]) * initial_memory + before_maps[3]
    moment_in = before_maps[4]
    forget_rows = jnp.transpose(start_forget)[:, :, None]
    moment_rows = jnp.transpose(carry_moment)[:, :, None]
    from_memory = jnp.einsum("thd,hde->the", query_f, memory_in, precision=highest)
    from_moment = jnp.einsum("thd,hde->the", query_f, moment_in, precision=highest)
    readout = inside + forget_rows * from_memory + moment_rows * from_moment
    output = readout.reshape(token_count, -1).astype(jnp.bfloat16)[None]
    upstream = cotangent[0].astype(jnp.float32).reshape(token_count, head_count, -1)
    recall_straight_route = jnp.einsum(
        "thd,the->hde", query_f * forget_rows, upstream, precision=highest
    )
    direct_moment = jnp.einsum("thd,the->hde", query_f * moment_rows, upstream, precision=highest)
    adjoint_element = (keep_forget, carry_last, keep_moment, recall_straight_route, direct_moment)
    after_maps = carried_in(adjoint_element, "seq", compose_adjoint, identity, True)
    memory_sense = after_maps[3]
    moment_sense = after_maps[4]
    grad_query, grad_key, grad_value = local_pull((upstream, memory_sense, moment_sense))
    grad_query = grad_query + forget_rows * jnp.einsum(
        "the,hde->thd", upstream, memory_in, precision=highest
    )
    grad_query = grad_query + moment_rows * jnp.einsum(
        "the,hde->thd", upstream, moment_in, precision=highest
    )
    extended_grad, weight_grad = feature_pull(
        (
            grad_query.astype(jnp.bfloat16),
            grad_key.astype(jnp.bfloat16),
            grad_value.astype(jnp.bfloat16),
        )
    )
    returned = from_behind(
        extended_grad[: kernel_width - 1].astype(jnp.bfloat16), "seq", -1
    ).astype(jnp.float32)
    own_grad = extended_grad[kernel_width - 1 :]
    split_at = token_count - (kernel_width - 1)
    own_grad = jnp.concatenate([own_grad[:split_at], own_grad[split_at:] + returned], axis=0)
    projected_grad = own_grad.astype(jnp.bfloat16)[None]
    conv_grad = lax.psum(weight_grad, ("dp", "seq"))
    at_start = expand_heads(keep_forget) * memory_sense + recall_straight_route
    grouped = lax.psum(at_start, "dp")
    full_grad = from_root(grouped, "seq", 0)
    memory_grad = own_rows(full_grad)
    return (output, projected_grad, conv_grad, memory_grad)


def solution(mesh):
    in_specs = (
        P("dp", "seq", None),
        P(),
        P(),
        P("dp", None, "seq"),
        P("dp", None, "seq"),
        P("dp", None, "seq"),
        P("dp", "seq", None),
    )
    out_specs = (P("dp", "seq", None), P("dp", "seq", None), P(), P(None, "seq", None))
    return jax.shard_map(local, mesh=mesh, in_specs=in_specs, out_specs=out_specs, check_vma=False)
```

profile of v0, /device:TPU:1, one launch (start us, length us, event | category | flops | bytes accessed | tf_op | source)
XLA Modules:
  0.0 1316.7 jit_solution(5410503335986429474)
XLA Ops:
  8.1 4.5 collective-permute-start
  46.2 64.9 %all-reduce.14 = (f32[512]{0:T(512)}, f32[512]{0:T(512)}, f32[512]{0:T(512)}) all-reduce(f32[512]{0:T(512)S(1)} %dynamic-update-slice, f32[512]{0:T(512)S(1)} %fusion.71, f32[512]{0:T(512)S(1)} %dynamic-update-slice.2), channel_id=2, replica_groups=mesh['dp'=8,'seq'=32] {'seq'}, use_global_device_ids=true, to_apply=%add.11 | all-reduce | flops 1536 | bytes 12288
  131.3 28.6 %all-gather.18.cloned.1.call-done = f32[512,128,128]{2,1,0:T(8,128)} async-done(((f32[16,128,128]{2,1,0:T(8,128)}), f32[512,128,128]{2,1,0:T(8,128)}) %all-gather.18.cloned.1.call-update) | async-done | bytes 33554448 | tf_op jit(solution)/shard_map/all_gather | solution.py:17
  159.9 23.4 %rev.19 = f32[32,16,128,128]{3,2,1,0:T(8,128)} reverse(f32[32,16,128,128]{3,2,1,0:T(8,128)} %bitcast.191), dimensions={0} | reverse | bytes 67108864 | tf_op jit(solution)/shard_map/rev | solution.py:19
  183.4 96.9 %all-gather.16.cloned.1.call-done = f32[512,128,128]{2,1,0:T(8,128)} async-done(((f32[16,128,128]{2,1,0:T(8,128)}), f32[512,128,128]{2,1,0:T(8,128)}) %all-gather.16.cloned.1.call-update) | async-done | bytes 33554448 | tf_op jit(solution)/shard_map/all_gather | solution.py:17
  280.3 23.0 %rev.16 = f32[32,16,128,128]{3,2,1,0:T(8,128)} reverse(f32[32,16,128,128]{3,2,1,0:T(8,128)} %bitcast.192), dimensions={0} | reverse | bytes 67108864 | tf_op jit(solution)/shard_map/rev | solution.py:19
  303.3 164.5 %while.35 = (s32[]{:T(128)}, f32[16,128,128]{2,1,0:T(8,128)}, f32[16,128,128]{2,1,0:T(8,128)}, s32[]{:T(128)}, f32[32,16]{1,0:T(8,128)}, /*index=5*/f32[32,16,12...) while((s32[]{:T(128)}, f32[16,128,128]{2,1,0:T(8,128)}, ...), condition=%wide.region_7.8_spmd.clone, body=%wide.region_6.7_spmd.clone.sunk | while | flops 2621444 | bytes 6292173 | solution.py:29
  309.3 3.9 fusion.115
  314.7 3.9 fusion.115
  320.0 4.0 fusion.115
  325.3 3.9 fusion.115
  330.6 3.9 fusion.115
  336.0 3.9 fusion.115
  341.3 3.9 fusion.115
  346.6 3.9 fusion.115
  351.9 3.9 fusion.115
  357.2 3.9 fusion.115
  362.6 3.9 fusion.115
  367.9 3.9 fusion.115
  373.2 3.9 fusion.115
  378.5 3.9 fusion.115
  383.8 3.9 fusion.115
  389.1 3.9 fusion.115
  394.5 3.9 fusion.115
  399.8 3.9 fusion.115
  405.1 4.0 fusion.115
  410.5 3.9 fusion.115
  415.8 3.9 fusion.115
  421.2 3.9 fusion.115
  426.5 3.9 fusion.115
  431.8 3.9 fusion.115
  437.1 3.9 fusion.115
  442.5 3.9 fusion.115
  447.8 3.9 fusion.115
  453.1 3.9 fusion.115
  458.4 3.9 fusion.115
  463.8 3.9 fusion.115
  476.3 65.1 %all-reduce.21.cloned.1.call-done = f32[16,128,128]{2,1,0:T(8,128)} async-done(((f32[16,128,128]{2,1,0:T(8,128)}), f32[16,128,128]{2,1,0:T(8,128)}) %all-reduce.21.cloned.1.call-update) | async-done | bytes 1048592 | tf_op jit(solution)/shard_map/psum | solution.py:204
  568.2 93.8 %all-reduce.23.cloned.1.call-done = f32[16,128,128]{2,1,0:T(8,128)} async-done(((f32[16,128,128]{2,1,0:T(8,128)}), f32[16,128,128]{2,1,0:T(8,128)}) %all-reduce.23.cloned.1.call-update) | async-done | bytes 1048592 | tf_op jit(solution)/shard_map/psum | solution.py:34
  663.5 120.4 %all-gather.14.cloned.1.call-done = f32[512,128,128]{2,1,0:T(8,128)} async-done(((f32[16,128,128]{2,1,0:T(8,128)}), f32[512,128,128]{2,1,0:T(8,128)}) %all-gather.14.cloned.1.call-update) | async-done | bytes 33554448 | tf_op jit(solution)/shard_map/all_gather | solution.py:17
  783.9 121.0 %all-gather.12.cloned.1.call-done = f32[512,128,128]{2,1,0:T(8,128)} async-done(((f32[16,128,128]{2,1,0:T(8,128)}), f32[512,128,128]{2,1,0:T(8,128)}) %all-gather.12.cloned.1.call-update) | async-done | bytes 33554448 | tf_op jit(solution)/shard_map/all_gather | solution.py:17
  904.9 142.2 %while.34 = (s32[]{:T(128)}, f32[16]{0:T(128)S(1)}, f32[16,128,128]{2,1,0:T(8,128)}, f32[16,128,128]{2,1,0:T(8,128)}, s32[]{:T(128)}, /*index=5*/f32[32,16]{1,0:...) while((s32[]{:T(128)}, f32[16]{0:T(128)S(1)}, ...), condition=%wide.region_5.6_spmd.clone, body=%wide.region_4.5_spmd.clone.sunk | while | flops 2621492 | bytes 6292311 | solution.py:29
  914.2 3.9 fusion.112
  969.6 3.9 fusion.112
  988.0 3.9 fusion.112
  1043.2 3.9 fusion.112
  1057.2 4.6 multiply_reduce_fusion.3
  1078.9 229.4 %all-reduce.19.cloned.1.call-done = f32[4,6144]{1,0:T(4,128)} async-done(((f32[4,6144]{1,0:T(4,128)}), f32[4,6144]{1,0:T(4,128)}) %all-reduce.19.cloned.1.call-update) | async-done | bytes 98320 | tf_op jit(solution)/shard_map/psum | solution.py:202
  (314 shorter events, 291.8 us)
Async XLA Ops:
  7.2 152.8 %all-gather.18.cloned.1.call-start = ((), (), s32[]{:S(2)}) async-start(), calls=%async_computation.6 | async-start | bytes 34603008 | tf_op jit(solution)/shard_map/all_gather | solution.py:17
  8.1 11.7 collective-permute-start
  14.9 7.4 copy-start.29
  15.8 21.9 %copy-start.28 = (f32[16,128]{1,0:T(8,128)}, f32[16,128]{1,0:T(8,128)S(1)}, u32[]{:S(2)}) copy-start(f32[16,128]{1,0:T(8,128)S(1)} %reduce_window_sum.17) | copy-start | bytes 24580
  19.8 0.6 copy-start.27
  25.3 1.6 copy-start.15
  32.3 8.9 copy-start.25
  32.3 5.4 copy-start.23
  33.7 0.8 copy-start.8
  37.7 242.6 %all-gather.16.cloned.1.call-start = ((), (), s32[]{:S(2)}) async-start(), calls=%async_computation.5 | async-start | bytes 34603008 | tf_op jit(solution)/shard_map/all_gather | solution.py:17
  41.2 500.2 %all-reduce.21.cloned.1.call-start = ((), (), s32[]{:S(2)}) async-start(), calls=%async_computation.1 | async-start | bytes 2097152 | tf_op jit(solution)/shard_map/psum | solution.py:204
  44.1 67.1 %copy-start.30 = (f32[16]{0:T(128)}, f32[16]{0:T(128)S(1)}, u32[]{:S(2)}) copy-start(f32[16]{0:T(128)S(1)} %slice_reduce_fusion.1) | copy-start | bytes 196
  120.5 1.0 copy-start.20
  303.3 164.5 %copy-start.31 = (f32[16]{0:T(128)S(1)}, f32[16]{0:T(128)}, u32[]{:S(2)}) copy-start(f32[16]{0:T(128)} %copy-done.30) | copy-start | bytes 196
  470.4 191.6 %all-reduce.23.cloned.1.call-start = ((), (), s32[]{:S(2)}) async-start(), calls=%async_computation.2 | async-start | bytes 2097152 | tf_op jit(solution)/shard_map/psum | solution.py:34
  470.7 2.2 copy-start
  470.7 3.9 copy-start.9
  470.7 3.9 copy-start.16
  470.7 3.9 copy-start.19
  470.7 3.9 copy-start.22
  542.5 241.4 %all-gather.14.cloned.1.call-start = ((), (), s32[]{:S(2)}) async-start(), calls=%async_computation.4 | async-start | bytes 34603008 | tf_op jit(solution)/shard_map/all_gather | solution.py:17
  542.6 3.5 copy-start.7
  545.3 0.8 copy-start.12
  548.3 356.5 %all-gather.12.cloned.1.call-start = ((), (), s32[]{:S(2)}) async-start(), calls=%async_computation.3 | async-start | bytes 34603008 | tf_op jit(solution)/shard_map/all_gather | solution.py:17
  551.8 756.6 %all-reduce.19.cloned.1.call-start = ((), (), s32[]{:S(2)}) async-start(), calls=%async_computation | async-start | bytes 196608 | tf_op jit(solution)/shard_map/psum | solution.py:202
  551.9 2.5 copy-start.11
  551.9 3.5 copy-start.2
  551.9 3.5 copy-start.13
  554.4 1.0 copy-start.18
  554.4 2.8 copy-start.1
  1047.1 2.2 copy-start.4
  1047.1 2.2 copy-start.21
  1047.1 4.0 copy-start.6
  1047.1 4.0 copy-start.14
  1047.1 4.0 copy-start.17
  1051.1 2.4 copy-start.26
  1051.1 2.4 copy-start.24
  1066.0 4.5 copy-start.5
  1066.0 4.5 copy-start.10
  1067.6 5.6 copy-start.3
  1068.4 6.9 collective-permute-start.1
Sparse Core Ops, SparseCore 0:
  37.8 122.0 all-gather.17
  162.5 117.7 all-gather.15
  470.5 70.8 all-reduce.20
  544.5 117.4 all-reduce.22
  664.8 119.0 all-gather.13
  786.6 118.1 all-gather.11
  1068.5 239.8 all-reduce.18
where the time goes:
time: 1320 us
  waiting for transfers between devices  755 us (57%)
  other arithmetic  273 us (21%)
  local copies, waits for them, and re-layouts  155 us (12%)
  blocking collectives  64.9 us (5%)
  matrix products  46.2 us (4%)
  between operations  15.4 us (1%)
    all_gather x4, waiting for transfers between devices, carried_in(): pieces = jax.tree.map(lambda part: lax.all_gather(part, axis), value)  367 us
    select_n x93, other arithmetic, step(): jnp.where(position < mine, new, old)  242 us
    psum x1, waiting for transfers between devices, local(): conv_grad = lax.psum(weight_grad, ('dp', 'seq'))  229 us
    psum x1, waiting for transfers between devices, from_root(): return lax.psum(kept, axis)  93.8 us
    psum x1, waiting for transfers between devices, local(): grouped = lax.psum(at_start, 'dp')  65.1 us
    unnamed x1, blocking collectives  64.9 us
    rev x5, local copies, waits for them, and re-layouts, carried_in(): pieces = jax.tree.map(lambda part: part[::-1], pieces)  49.6 us
  transfers between devices with their start and end apart: 9, of which 7 were waited for; matrix products, arithmetic and copies ran while one was open for 7% of the time, Pallas kernels for 0%

commit v1 on v0

v1 whole, which is shorter than its diff:
```python
import functools

import jax
import jax.numpy as jnp
from jax import lax
from jax.experimental import pallas as pl
from jax.experimental.pallas import tpu as pltpu
from jax.sharding import PartitionSpec as P

DK = 128
BF = jnp.bfloat16
F32 = jnp.float32
PARAMS = pltpu.CompilerParams(vmem_limit_bytes=60 * 1024 * 1024)
SHARED = pltpu.CompilerParams(vmem_limit_bytes=32 * 1024 * 1024)
CHIPS = 16
HALF = 8
EXTRA = 16
PIECE = 4 * 64 + EXTRA


def dot(a, b, contract):
    return lax.dot_general(a, b, ((contract[:1], contract[1:]), ((), ())), preferred_element_type=F32)


def to_column(row, eye):
    return jnp.sum(jnp.where(eye, row, 0.0), axis=1, keepdims=True)


def tables_kernel(forget_ref, momentum_ref, rate_ref, coupling_ref, column_ref, coef_ref):
    heads, tokens = forget_ref.shape
    rows = lax.broadcasted_iota(jnp.int32, (tokens, tokens), 0)
    lanes = lax.broadcasted_iota(jnp.int32, (tokens, tokens), 1)
    eye = rows == lanes
    causal = rows >= lanes
    upper = (rows <= lanes).astype(F32)
    exact = functools.partial(
        lax.dot_general,
        dimension_numbers=(((1,), (0,)), ((), ())),
        precision=lax.Precision.HIGHEST,
        preferred_element_type=F32,
    )
    cum_forget = exact(forget_ref[...], upper)
    cum_moment = exact(momentum_ref[...], upper)
    narrow = lax.broadcasted_iota(jnp.int32, (tokens, 8), 1)
    last = tokens - 1
    for h in range(heads):
        forget_row = cum_forget[h : h + 1, :]
        moment_row = cum_moment[h : h + 1, :]
        rate_row = rate_ref[h : h + 1, :]
        forget_col = to_column(forget_row, eye)
        moment_col = to_column(moment_row, eye)
        rate_col = to_column(rate_row, eye)
        forget_map = jnp.where(causal, jnp.exp(jnp.minimum(forget_col - forget_row, 0.0)), 0.0)
        moment_map = jnp.where(causal, jnp.exp(jnp.minimum(moment_col - moment_row, 0.0)), 0.0)
        coupling = dot(forget_map.astype(BF), moment_map.astype(BF), (1, 0))
        carry = coupling[:, 0:1] * jnp.exp(moment_row[:, 0:1])
        rated = coupling * rate_row
        coupling_ref[h] = rated
        memory_col = to_column(rated[last : last + 1, :], eye)
        tail_col = rate_col * jnp.exp(jnp.minimum(moment_row[:, last:] - moment_col, 0.0))
        quad = jnp.where(
            narrow % 4 == 0,
            memory_col,
            jnp.where(narrow % 4 == 1, tail_col, jnp.where(narrow % 4 == 2, jnp.exp(forget_col), carry)),
        )
        if h % 2 == 0:
            first_quad = quad
        else:
            column_ref[h // 2] = jnp.where(narrow < 4, first_quad, quad)
        spread = functools.partial(jnp.broadcast_to, shape=(1, tokens))
        coef_ref[h : h + 1, :] = spread(jnp.exp(forget_row[:, last:]))
        coef_ref[heads + h : heads + h + 1, :] = spread(carry[last : last + 1, :])
        coef_ref[2 * heads + h : 2 * heads + h + 1, :] = spread(jnp.exp(moment_row[:, last:]))


def extend(ext_ref, slot, halo, own):
    cols = slice(slot * DK, (slot + 1) * DK)
    ext_ref[0:8, cols] = halo
    ext_ref[8 : 8 + own.shape[0], cols] = own.astype(F32)


def convolve(ext_ref, slot, weights, tokens):
    cols = slice(slot * DK, (slot + 1) * DK)
    total = weights[0:1] * ext_ref[5 : 5 + tokens, cols]
    for tap in range(1, 4):
        total = total + weights[tap : tap + 1] * ext_ref[5 + tap : 5 + tap + tokens, cols]
    return total


def element_kernel(
    base_ref, q_ref, k_ref, v_ref, u_ref, halo_ref, weight_ref, column_ref, element_ref, ext_ref
):
    tokens, width = q_ref.shape
    section = halo_ref.shape[1] // 3
    block = base_ref[0] + pl.program_id(0)
    for side in range(width // DK):
        cols = slice(side * DK, (side + 1) * DK)
        made = []
        for part, ref in enumerate((q_ref, k_ref, v_ref)):
            at = pl.ds(pl.multiple_of(part * section + block * width + side * DK, DK), DK)
            slot = side * 3 + part
            extend(ext_ref, slot, halo_ref[:, at], ref[:, cols])
            conv = convolve(ext_ref, slot, weight_ref[:, at], tokens)
            active = conv * (0.5 + 0.5 * jnp.tanh(0.5 * conv))
            if part < 2:
                active = active * lax.rsqrt(
                    jnp.sum(active * active, axis=1, keepdims=True) + 1e-06
                )
            made.append(active.astype(BF))
        query, key, value = made
        column = column_ref[0, :, 4 * side : 4 * side + 4]
        query = query.astype(F32)
        key = key.astype(F32)
        left = jnp.concatenate(
            [(key * column[:, 0:1]).astype(BF), (key * column[:, 1:2]).astype(BF)], axis=1
        )
        element_ref[side, 0 : 2 * DK] = dot(left, value, (0, 0)).astype(BF)
        left = jnp.concatenate(
            [(query * column[:, 2:3]).astype(BF), (query * column[:, 3:4]).astype(BF)], axis=1
        )
        element_ref[side, 2 * DK : 4 * DK] = dot(left, u_ref[:, cols], (0, 0)).astype(BF)


def compose_kernel(place_ref, own_ref, other_ref, own_coef_ref, other_coef_ref, out_ref):
    core = place_ref[0]
    first_core = core == 0
    heads = own_coef_ref.shape[0] // 3
    for j in range(own_ref.shape[0]):
        head = core * HALF + pl.program_id(0) * own_ref.shape[0] + j

        def coef(which):
            mine = own_coef_ref[pl.ds(which * heads + head, 1), :]
            theirs = other_coef_ref[pl.ds(which * heads + head, 1), :]
            return jnp.where(first_core, mine, theirs), jnp.where(first_core, theirs, mine)

        def matrix(which):
            at = slice(which * DK, (which + 1) * DK)
            mine = own_ref[j, at].astype(F32)
            theirs = other_ref[j, at].astype(F32)
            return jnp.where(first_core, mine, theirs), jnp.where(first_core, theirs, mine)

        forget_a, forget_b = coef(0)
        carry_a, carry_b = coef(1)
        moment_a, moment_b = coef(2)
        memory_a, memory_b = matrix(0)
        state_a, state_b = matrix(1)
        recall_a, recall_b = matrix(2)
        direct_a, direct_b = matrix(3)
        joined = (
            forget_b * memory_a + carry_b * state_a + memory_b,
            moment_b * state_a + state_b,
            forget_a * recall_b + recall_a,
            carry_a * recall_b + moment_a * direct_b + direct_a,
        )
        scalars = []
        for value in (
            forget_a * forget_b,
            forget_b * carry_a + carry_b * moment_a,
            moment_a * moment_b,
        ):
            for term in range(3):
                kept = value.astype(BF).astype(F32)
                scalars.append(kept)
                value = value - kept
        scalars.append(jnp.zeros((EXTRA - len(scalars), DK), F32))
        tail = jnp.concatenate(scalars, axis=0).astype(BF)
        for half in range(2):
            for which, full in enumerate(joined):
                out_ref[2 * j + half, which * 64 : (which + 1) * 64] = full[
                    half * 64 : (half + 1) * 64
                ].astype(BF)
            out_ref[2 * j + half, 256:PIECE] = tail


def scan_kernel(got_ref, start_ref, out_ref):
    count = got_ref.shape[0]

    def coefs(c):
        rows = got_ref[c, 256:PIECE].astype(F32)
        return tuple(
            (rows[3 * i : 3 * i + 1] + rows[3 * i + 1 : 3 * i + 2]) + rows[3 * i + 2 : 3 * i + 3]
            for i in range(3)
        )

    scalars = [coefs(c) for c in range(count)]
    memory = start_ref[...]
    state = jnp.zeros_like(memory)
    for c in range(count):
        out_ref[c, 0:64] = memory.astype(BF)
        out_ref[c, 64:128] = state.astype(BF)
        forget, carry, moment = scalars[c]
        memory = forget * memory + carry * state + got_ref[c, 0:64].astype(F32)
        state = moment * state + got_ref[c, 64:128].astype(F32)
    memory = jnp.zeros_like(state)
    state = jnp.zeros_like(state)
    for c in reversed(range(count)):
        out_ref[c, 128:192] = memory.astype(BF)
        out_ref[c, 192:256] = state.astype(BF)
        forget, carry, moment = scalars[c]
        state = carry * memory + moment * state + got_ref[c, 192:256].astype(F32)
        memory = forget * memory + got_ref[c, 128:192].astype(F32)
    for c in range(count):
        rows = memory[8 * (c % 8) : 8 * (c % 8) + 8]
        high = rows.astype(BF).astype(F32)
        out_ref[c, 256:PIECE] = jnp.concatenate([high, rows - high], axis=0).astype(BF)


def spread_kernel(
    place_ref, got_ref, own_ref, other_ref, own_coef_ref, other_coef_ref, keep_ref, send_ref, start_ref
):
    core = place_ref[0]
    side = place_ref[1]
    first_core = core == 0
    heads = own_coef_ref.shape[0] // 3
    for j in range(own_ref.shape[0]):
        head = core * HALF + pl.program_id(0) * own_ref.shape[0] + j

        def coef(which):
            mine = own_coef_ref[pl.ds(which * heads + head, 1), :]
            theirs = other_coef_ref[pl.ds(which * heads + head, 1), :]
            return jnp.where(first_core, mine, theirs), jnp.where(first_core, theirs, mine)

        def local(which):
            at = slice(which * DK, (which + 1) * DK)
            mine = own_ref[j, at].astype(F32)
            theirs = other_ref[j, at].astype(F32)
            return jnp.where(first_core, mine, theirs), jnp.where(first_core, theirs, mine)

        def entering(which):
            at = slice(which * 64, (which + 1) * 64)
            return jnp.concatenate([got_ref[2 * j, at], got_ref[2 * j + 1, at]], axis=0).astype(F32)

        forget_a, forget_b = coef(0)
        carry_a, carry_b = coef(1)
        moment_a, moment_b = coef(2)
        memory, state = entering(0), entering(1)
        memory_end, state_end = entering(2), entering(3)
        one = (
            memory,
            state,
            forget_b * memory_end + local(2)[1],
            carry_b * memory_end + moment_b * state_end + local(3)[1],
        )
        two = (
            forget_a * memory + carry_a * state + local(0)[0],
            moment_a * state + local(1)[0],
            memory_end,
            state_end,
        )
        for which in range(4):
            at = slice(which * DK, (which + 1) * DK)
            keep_ref[j, at] = jnp.where(first_core, one[which], two[which]).astype(BF)
            send_ref[j, at] = jnp.where(first_core, two[which], one[which]).astype(BF)
        rows = got_ref[2 * j + side, 256:PIECE].astype(F32)
        start_ref[j] = rows[0:8] + rows[8:16]


def inner_kernel(
    q_ref, k_ref, v_ref, u_ref, halo_ref, weight_ref, coupling_ref, out_ref, read_ref, ext_ref
):
    tokens, width = q_ref.shape
    section = halo_ref.shape[1] // 3
    block = pl.program_id(0)
    for side in range(width // DK):
        cols = slice(side * DK, (side + 1) * DK)
        made, slopes, units = [], [], []
        for part, ref in enumerate((q_ref, k_ref, v_ref)):
            at = pl.ds(pl.multiple_of(part * section + block * width + side * DK, DK), DK)
            slot = side * 3 + part
            extend(ext_ref, slot, halo_ref[:, at], ref[:, cols])
            conv = convolve(ext_ref, slot, weight_ref[:, at], tokens)
            gate = 0.5 + 0.5 * jnp.tanh(0.5 * conv)
            active = conv * gate
            slope = gate * (1.0 + conv * (1.0 - gate))
            slopes.append(slope)
            if part < 2:
                scale = lax.rsqrt(jnp.sum(active * active, axis=1, keepdims=True) + 1e-06)
                active = active * scale
                slope = slope * scale
                slopes[part] = slope
                units.append(active)
            active = active.astype(BF)
            made.append(active)
            out_ref[0, part, :, cols] = active
            out_ref[0, 4 + part, :, cols] = slope.astype(BF)
            out_ref[0, 10 + part, :, cols] = ref[:, cols]
        query, key, value = made
        upstream = u_ref[:, cols]
        out_ref[0, 3, :, cols] = upstream
        coupling = coupling_ref[side]
        scores = (dot(query, key, (1, 1)) * coupling).astype(BF)
        sense = (dot(upstream, value, (1, 1)) * coupling).astype(BF)
        grads = (
            dot(sense, key, (1, 0)),
            dot(sense, query, (0, 0)),
            dot(scores, upstream, (0, 0)),
        )
        for part, grad in enumerate(grads):
            if part < 2:
                unit = units[part]
                grad = grad - unit * jnp.sum(unit * grad, axis=1, keepdims=True)
            out_ref[0, 7 + part, :, cols] = (grad * slopes[part]).astype(BF)
        read_ref[0, 0, :, cols] = query
        read_ref[0, 1, :, cols] = dot(scores, value, (1, 0)).astype(BF)


def along_rows(left, pair):
    return dot(left, pair[:DK], (1, 0)), dot(left, pair[DK:], (1, 0))


def along_lanes(left, pair):
    both = dot(left, pair, (1, 1))
    return both[:, :DK], both[:, DK:]


def sense_kernel(
    base_ref, in_ref, halo_ref, weight_ref, column_ref, state_ref, before_ref,
    conv_ref, rim_ref, tap_ref, pad_ref, ext_ref,
):
    tokens = in_ref.shape[2]
    width = in_ref.shape[3]
    section = halo_ref.shape[1] // 3
    block = base_ref[0] + pl.program_id(0)

    @pl.when(pl.program_id(0) == 0)
    def _():
        pad_ref[0:8] = jnp.zeros((8, pad_ref.shape[1]), F32)
        pad_ref[8 + tokens :] = jnp.zeros((8, pad_ref.shape[1]), F32)

    rim_ref[0] = before_ref[1]
    for side in range(width // DK):
        cols = slice(side * DK, (side + 1) * DK)
        query, key, value, upstream = (in_ref[0, i, :, cols] for i in range(4))
        column = column_ref[0, :, 4 * side : 4 * side + 4]
        memory_col, tail_col, forget_col, carry_col = (column[:, i : i + 1] for i in range(4))
        forward, adjoint = state_ref[side, : 2 * DK], state_ref[side, 2 * DK :]
        grads = []
        a, b = along_lanes(upstream, forward)
        grads.append(forget_col * a + carry_col * b)
        a, b = along_lanes(value, adjoint)
        grads.append(memory_col * a + tail_col * b)
        a, b = along_rows(key, adjoint)
        grads.append(memory_col * a + tail_col * b)
        for part in range(3):
            grad = grads[part]
            if part < 2:
                unit = (query, key)[part].astype(F32)
                grad = grad - unit * jnp.sum(unit * grad, axis=1, keepdims=True)
            grad = grad * in_ref[0, 4 + part, :, cols].astype(F32)
            grad = grad + in_ref[0, 7 + part, :, cols].astype(F32)
            conv_ref[0, part, :, cols] = grad
            slot = side * 3 + part
            there = slice(slot * DK, (slot + 1) * DK)
            pad_ref[8 : 8 + tokens, there] = grad
            at = pl.ds(pl.multiple_of(part * section + block * width + side * DK, DK), DK)
            extend(ext_ref, slot, halo_ref[:, at], in_ref[0, 10 + part, :, cols])
            rows = ext_ref[:, there]
            weights = weight_ref[:, at]
            rim = None
            for tap in range(4):
                moved = pad_ref[3 - tap : 3 - tap + 8 + tokens, there]
                slot_row = 12 * (2 * pl.program_id(0) + side) + 4 * part + tap
                tap_ref[pl.ds(slot_row, 1), :] = jnp.sum(moved * rows, axis=0, keepdims=True)
                lead = moved[0:8] * weights[tap : tap + 1]
                rim = lead if rim is None else rim + lead
            rim_ref[1, :, part * width + side * DK : part * width + (side + 1) * DK] = jnp.concatenate(
                [jnp.zeros_like(rim), rim], axis=0
            ).astype(BF)


def readout_kernel(place_ref, read_ref, column_ref, own_ref, other_ref, output_ref):
    width = read_ref.shape[3]
    owned = (pl.program_id(0) // (pl.num_programs(0) // 2)) == place_ref[0]
    for side in range(width // DK):
        cols = slice(side * DK, (side + 1) * DK)
        column = column_ref[0, :, 4 * side : 4 * side + 4]
        states = jnp.where(owned, own_ref[side], other_ref[side])
        from_memory, from_moment = along_rows(read_ref[0, 0, :, cols], states)
        readout = read_ref[0, 1, :, cols].astype(F32) + column[:, 2:3] * from_memory + column[:, 3:4] * from_moment
        output_ref[:, cols] = readout.astype(BF)


def unroll_kernel(
    place_ref, conv_own_ref, conv_other_ref, weight_ref, rim_own_ref, rim_other_ref, grad_ref, pad_ref
):
    tokens, width = conv_own_ref.shape[2:]
    section = weight_ref.shape[1] // 3
    block = pl.program_id(0)
    owned = (block // (pl.num_programs(0) // 2)) == place_ref[0]

    @pl.when(block == 0)
    def _():
        pad_ref[tokens:] = jnp.zeros((8, pad_ref.shape[1]), F32)

    for side in range(width // DK):
        cols = slice(side * DK, (side + 1) * DK)
        for part in range(3):
            at = pl.ds(pl.multiple_of(part * section + block * width + side * DK, DK), DK)
            slot = side * 3 + part
            there = slice(slot * DK, (slot + 1) * DK)
            grad = jnp.where(owned, conv_own_ref[0, part, :, cols], conv_other_ref[0, part, :, cols])
            weights = weight_ref[:, at]
            pad_ref[0:tokens, there] = grad
            total = grad * weights[3:4]
            for tap in range(3):
                total = total + pad_ref[3 - tap : 3 - tap + tokens, there] * weights[tap : tap + 1]
            near = slice(part * width + side * DK, part * width + (side + 1) * DK)
            rim = jnp.where(owned, rim_own_ref[0, :, near], rim_other_ref[0, :, near]).astype(F32)
            total = jnp.concatenate([total[: tokens - 16], total[tokens - 16 :] + rim], axis=0)
            grad_ref[:, at] = total.astype(BF)


def assemble_kernel(place_ref, own_ref, other_ref, out_ref):
    section = out_ref.shape[1] // 3
    for h in range(section // DK):
        for part in range(3):
            first = 12 * (h % HALF) + 4 * part
            rows = slice(first, first + 4)
            at = part * section + h * DK
            out_ref[:, at : at + DK] = jnp.where(
                place_ref[0] == h // HALF, own_ref[rows], other_ref[rows]
            )


def whole(*shape):
    return pl.BlockSpec(shape, lambda *_: (0,) * len(shape))


def local(projected, conv_weight, initial_memory, log_forget, log_momentum, learn_rate, cotangent):
    rows = projected[0]
    upstream = cotangent[0]
    tokens, channels = rows.shape
    heads = initial_memory.shape[0]
    width = 2 * DK
    blocks = heads * DK // width
    count = lax.axis_size("seq")
    mine = lax.axis_index("seq")
    core = mine % 2
    chip = mine // 2
    place = jnp.stack([core, chip // 8]).astype(jnp.int32)
    pairs = [(i, i ^ 1) for i in range(count)]
    groups = [[2 * c + k for c in range(count // 2)] for k in range(2)]

    rim = lax.ppermute(rows[tokens - 3 :], "seq", [(i, i + 1) for i in range(count - 1)])
    shape = jax.ShapeDtypeStruct
    coupling, columns, coefs = pl.pallas_call(
        tables_kernel,
        out_shape=(
            shape((heads, tokens, tokens), F32),
            shape((heads // 2, tokens, 8), F32),
            shape((3 * heads, DK), F32),
        ),
        compiler_params=PARAMS,
        name="tables",
    )(log_forget[0], log_momentum[0], learn_rate[0])
    halo = jnp.pad(rim.astype(F32), ((5, 0), (0, 0)))
    other_coefs = lax.ppermute(coefs, "seq", pairs)

    def elements(base):
        def block_of(part):
            return pl.BlockSpec((tokens, width), lambda i, b: (0, part * blocks + b[0] + i))

        return pl.pallas_call(
            element_kernel,
            out_shape=shape((heads // 2, 4 * DK, DK), BF),
            grid_spec=pltpu.PrefetchScalarGridSpec(
                num_scalar_prefetch=1,
                grid=(blocks // 2,),
                in_specs=[
                    block_of(0),
                    block_of(1),
                    block_of(2),
                    block_of(0),
                    whole(8, channels),
                    whole(4, channels),
                    pl.BlockSpec((1, tokens, 8), lambda i, b: (b[0] + i, 0, 0)),
                ],
                out_specs=pl.BlockSpec((2, 4 * DK, DK), lambda i, b: (i, 0, 0)),
                scratch_shapes=[pltpu.VMEM((tokens + 8, 6 * DK), F32)],
            ),
            compiler_params=PARAMS,
            name="elements",
        )(base.astype(jnp.int32).reshape(1), rows, rows, rows, upstream, halo, conv_weight, columns)

    sent = elements((1 - core) * (blocks // 2))
    other = lax.ppermute(sent, "seq", pairs)
    own = elements(core * (blocks // 2))

    by_two = pl.BlockSpec((2, 4 * DK, DK), lambda i, b: (i, 0, 0))
    pieces = pl.BlockSpec((4, PIECE, DK), lambda i, b: (i, 0, 0))
    payload = pl.pallas_call(
        compose_kernel,
        out_shape=shape((CHIPS, PIECE, DK), BF),
        grid_spec=pltpu.PrefetchScalarGridSpec(
            num_scalar_prefetch=1,
            grid=(HALF // 2,),
            in_specs=[by_two, by_two, whole(3 * heads, DK), whole(3 * heads, DK)],
            out_specs=pieces,
        ),
        compiler_params=SHARED,
        name="compose",
    )(place, own, other, coefs, other_coefs)
    payload, coupling = lax.optimization_barrier((payload, coupling))
    got = lax.all_to_all(payload, "seq", 0, 0, axis_index_groups=groups)

    def block_at(part):
        return pl.BlockSpec((tokens, width), lambda i: (0, part * blocks + i))

    inner, inside = pl.pallas_call(
        inner_kernel,
        out_shape=(
            shape((blocks, 13, tokens, width), BF),
            shape((blocks, 2, tokens, width), BF),
        ),
        grid=(blocks,),
        in_specs=[
            block_at(0),
            block_at(1),
            block_at(2),
            block_at(0),
            whole(8, channels),
            whole(4, channels),
            pl.BlockSpec((2, tokens, tokens), lambda i: (i, 0, 0)),
        ],
        out_specs=(
            pl.BlockSpec((1, 13, tokens, width), lambda i: (i, 0, 0, 0)),
            pl.BlockSpec((1, 2, tokens, width), lambda i: (i, 0, 0, 0)),
        ),
        scratch_shapes=[pltpu.VMEM((tokens + 8, 6 * DK), F32)],
        compiler_params=PARAMS,
        name="inner",
    )(rows, rows, rows, upstream, halo, conv_weight, coupling)

    start = lax.dynamic_slice_in_dim(
        initial_memory.reshape(heads * DK, DK), core * (HALF * DK) + chip * 64, 64, 0
    )
    got, inner = lax.optimization_barrier((got, inner))
    back = pl.pallas_call(
        scan_kernel,
        out_shape=shape((CHIPS, PIECE, DK), BF),
        compiler_params=SHARED,
        name="scan",
    )(got, start)
    states = lax.all_to_all(back, "seq", 0, 0, axis_index_groups=groups)

    kept, passed, start_grad = pl.pallas_call(
        spread_kernel,
        out_shape=(
            shape((HALF, 4 * DK, DK), BF),
            shape((HALF, 4 * DK, DK), BF),
            shape((HALF, 8, DK), F32),
        ),
        grid_spec=pltpu.PrefetchScalarGridSpec(
            num_scalar_prefetch=1,
            grid=(HALF // 2,),
            in_specs=[pieces, by_two, by_two, whole(3 * heads, DK), whole(3 * heads, DK)],
            out_specs=(by_two, by_two, pl.BlockSpec((2, 8, DK), lambda i, b: (i, 0, 0))),
        ),
        compiler_params=SHARED,
        name="spread",
    )(place, states, own, other, coefs, other_coefs)
    received = lax.ppermute(passed, "seq", pairs)
    other_start = lax.ppermute(start_grad, "seq", pairs)

    half_blocks = blocks // 2

    def sense(base, state, before):
        return pl.pallas_call(
            sense_kernel,
            out_shape=(
                shape((half_blocks, 3, tokens, width), F32),
                shape((2, 16, channels // 2), BF),
                shape((12 * HALF, DK), F32),
            ),
            grid_spec=pltpu.PrefetchScalarGridSpec(
                num_scalar_prefetch=1,
                grid=(half_blocks,),
                in_specs=[
                    pl.BlockSpec((1, 13, tokens, width), lambda i, b: (b[0] + i, 0, 0, 0)),
                    whole(8, channels),
                    whole(4, channels),
                    pl.BlockSpec((1, tokens, 8), lambda i, b: (b[0] + i, 0, 0)),
                    by_two,
                    pl.BlockSpec((2, 16, 3 * width), lambda i, b: (0, 0, i)),
                ],
                out_specs=(
                    pl.BlockSpec((1, 3, tokens, width), lambda i, b: (i, 0, 0, 0)),
                    pl.BlockSpec((2, 16, 3 * width), lambda i, b: (0, 0, i)),
                    whole(12 * HALF, DK),
                ),
                scratch_shapes=[
                    pltpu.VMEM((tokens + 16, 6 * DK), F32),
                    pltpu.VMEM((tokens + 8, 6 * DK), F32),
                ],
            ),
            compiler_params=PARAMS,
            name="sense",
        )(base.astype(jnp.int32).reshape(1), inner, halo, conv_weight, columns, state, before)

    rim = jnp.zeros((2, 16, channels // 2), BF)
    conv_own, rim, tap_own = sense(core * half_blocks, kept, rim)
    conv_other, rim, tap_other = sense((1 - core) * half_blocks, received, rim)

    tap_far = lax.ppermute(tap_other, "seq", pairs)

    def ordered(one, two):
        return jnp.where(core == 0, one, two), jnp.where(core == 0, two, one)

    back_one = [(i + 1, i) for i in range(count - 1)]
    rim = lax.ppermute(rim, "seq", back_one)

    def own_at(i, b):
        return jnp.clip(i - b[0] * half_blocks, 0, half_blocks - 1)

    def other_at(i, b):
        return jnp.clip(i - (1 - b[0]) * half_blocks, 0, half_blocks - 1)

    def readouts(inside):
        return pl.pallas_call(
            readout_kernel,
            out_shape=shape((tokens, heads * DK), BF),
            grid_spec=pltpu.PrefetchScalarGridSpec(
                num_scalar_prefetch=1,
                grid=(blocks,),
                in_specs=[
                    pl.BlockSpec((1, 2, tokens, width), lambda i, b: (i, 0, 0, 0)),
                    pl.BlockSpec((1, tokens, 8), lambda i, b: (i, 0, 0)),
                    pl.BlockSpec((2, 2 * DK, DK), lambda i, b: (own_at(i, b), 0, 0)),
                    pl.BlockSpec((2, 2 * DK, DK), lambda i, b: (other_at(i, b), 0, 0)),
                ],
                out_specs=pl.BlockSpec((tokens, width), lambda i, b: (0, i)),
            ),
            compiler_params=PARAMS,
            name="readout",
        )(place, inside, columns, kept, received)

    def unrolled(rim):
        return pl.pallas_call(
            unroll_kernel,
            out_shape=shape((tokens, channels), BF),
            grid_spec=pltpu.PrefetchScalarGridSpec(
                num_scalar_prefetch=1,
                grid=(blocks,),
                in_specs=[
                    pl.BlockSpec((1, 3, tokens, width), lambda i, b: (own_at(i, b), 0, 0, 0)),
                    pl.BlockSpec((1, 3, tokens, width), lambda i, b: (other_at(i, b), 0, 0, 0)),
                    whole(4, channels),
                    pl.BlockSpec((1, 16, 3 * width), lambda i, b: (1, 0, own_at(i, b))),
                    pl.BlockSpec((1, 16, 3 * width), lambda i, b: (0, 0, other_at(i, b))),
                ],
                out_specs=whole(tokens, channels),
                scratch_shapes=[pltpu.VMEM((tokens + 8, 6 * DK), F32)],
            ),
            compiler_params=PARAMS,
            name="unroll",
        )(place, conv_own, conv_other, conv_weight, rim, rim)

    start_own = lax.dynamic_slice_in_dim(start_grad, 4 * core, 4, 1)
    start_other = lax.dynamic_slice_in_dim(other_start, 4 * core, 4, 1)
    start_all = jnp.concatenate(ordered(start_own, start_other), axis=0)
    start_all = start_all.reshape(4 * heads, DK)

    def gathered_sum(value, axis, size, axis_groups, ready, beside):
        value = value.astype(BF)
        value, ready = lax.optimization_barrier((value, ready))
        spread = jnp.broadcast_to(value[None], (size, *value.shape))
        pieces = lax.all_to_all(spread, axis, 0, 0, axis_index_groups=axis_groups)
        pieces, made = lax.optimization_barrier((pieces, beside(ready)))
        return jnp.sum(pieces.astype(F32), axis=0), made

    total, output = gathered_sum(tap_own + tap_far, "seq", CHIPS, groups, inside, readouts)
    total = jnp.concatenate([total, start_all], axis=0)
    total, grad = gathered_sum(total, "dp", lax.axis_size("dp"), None, rim, unrolled)
    tap_far = lax.ppermute(total[: 12 * HALF], "seq", pairs)
    start_all = total[12 * HALF :].reshape(heads, 4, DK)

    taps = pl.pallas_call(
        assemble_kernel,
        out_shape=shape((4, channels), F32),
        grid_spec=pltpu.PrefetchScalarGridSpec(
            num_scalar_prefetch=1,
            grid=(1,),
            in_specs=[whole(12 * HALF + 4 * heads, DK), whole(12 * HALF, DK)],
            out_specs=whole(4, channels),
        ),
        compiler_params=SHARED,
        name="assemble",
    )(place, total, tap_far)

    return (output[None], grad[None], taps, start_all)


def solution(mesh):
    in_specs = (
        P("dp", "seq", None),
        P(),
        P(),
        P("dp", None, "seq"),
        P("dp", None, "seq"),
        P("dp", None, "seq"),
        P("dp", "seq", None),
    )
    out_specs = (P("dp", "seq", None), P("dp", "seq", None), P(), P(None, "seq", None))
    return jax.shard_map(local, mesh=mesh, in_specs=in_specs, out_specs=out_specs, check_vma=False)
```

time: 1320 us -> 134 us (0.10)
  waiting for transfers between devices: 755 us -> 14.1 us
  other arithmetic: 273 us -> 0.94 us
  local copies, waits for them, and re-layouts: 155 us -> 7.13 us
  Pallas kernels: 0 us -> 59 us
  matrix products: 46.2 us -> 0 us
  blocking collectives: 64.9 us -> 20.7 us
  starting transfers between devices: 7.13 us -> 30 us
  between operations: 15.4 us -> 0.86 us
    psum x3 -> x0, waiting for transfers between devices: 388 us -> none  [the longest x1 229 us: local(): conv_grad = lax.psum(weight_grad, ('dp', 'seq'))]
    all_gather x4 -> x0, waiting for transfers between devices: 367 us -> none  [carried_in(): pieces = jax.tree.map(lambda part: lax.all_gather(part, axis), value)]
    select_n x94 -> x0, other arithmetic: 243 us -> none  [the longest x93 242 us: step(): jnp.where(position < mine, new, old)]
    unnamed x1 -> x0, blocking collectives: 64.9 us -> none
    mul x93 -> x0, local copies, waits for them, and re-layouts: 64.6 us -> none  [the longest x31 21.8 us: compose_forward(): expand_heads(carry_second) * state_one]
    pallas_call x0 -> x12, Pallas kernels: none -> 59 us  [the longest x2 11.6 us: sense(): pl.pallas_call(sense_kernel, out_shape=(shape((half_blocks, 3, tokens, wi...]
    rev x5 -> x0, local copies, waits for them, and re-layouts: 49.6 us -> none  [carried_in(): pieces = jax.tree.map(lambda part: part[::-1], pieces)]
    dot_general x20 -> x0, matrix products: 46.2 us -> none  [the longest x3 7.81 us: local_part(): jnp.einsum('shd,she->hde', weighted * jnp.transpose(coupling[:, -1, :])[:...]
  transfers between devices with their start and end apart: 9 -> 11, of which waited for: 7 -> 5; matrix products, arithmetic and copies ran while one was open for 7% -> 1% of each run, Pallas kernels for 0% -> 32%
where the time goes in v1:
time: 134 us; the launch traced here: 133 us
  Pallas kernels  59 us (44%)
  starting transfers between devices  30 us (22%)
  blocking collectives  20.7 us (15%)
  waiting for transfers between devices  14.1 us (11%)
  local copies, waits for them, and re-layouts  7.13 us (5%)
    all_to_all x1, blocking collectives, local(): states = lax.all_to_all(back, 'seq', 0, 0, axis_index_groups=groups)  20.7 us
    all_to_all x2, starting transfers between devices, gathered_sum(): pieces = lax.all_to_all(spread, axis, 0, 0, axis_index_groups=axis_groups)  11.7 us
    pallas_call x2, Pallas kernels, sense(): pl.pallas_call(sense_kernel, out_shape=(shape((half_blocks, 3, tokens, wi...  11.6 us
    pallas_call x1, Pallas kernels, local(): pl.pallas_call(inner_kernel, out_shape=(shape((blocks, 13, tokens, width)...  11.2 us
    pallas_call x2, Pallas kernels, elements(): pl.pallas_call(element_kernel, out_shape=shape((heads // 2, 4 * DK, DK),...  10.9 us
    pallas_call x1, Pallas kernels, unrolled(): pl.pallas_call(unroll_kernel, out_shape=shape((tokens, channels), BF), gr...  7.54 us
    all_to_all x1, waiting for transfers between devices, local(): got = lax.all_to_all(payload, 'seq', 0, 0, axis_index_groups=groups)  7 us
    pallas_call x1, Pallas kernels, readouts(): pl.pallas_call(readout_kernel, out_shape=shape((tokens, heads * DK), BF),...  6.95 us
  transfers between devices with their start and end apart: 11, of which 5 were waited for; matrix products, arithmetic and copies ran while one was open for 1% of the time, Pallas kernels for 32%

profile of v1, /device:TPU:1, one launch (start us, length us, event | category | flops | bytes accessed | tf_op | source)
XLA Modules:
  0.0 132.7 jit_solution(18427838355288322900)
XLA Ops:
  0.6 0.0 copy-start
  0.6 1.0 slice_bitcast_fusion
  1.7 4.5 %collective-permute-start = (bf16[3,6144]{1,0:T(4,128)(2,1)S(1)}, bf16[3,6144]{1,0:T(4,128)(2,1)S(1)}, u32[]{:S(2)}, u32[]{:S(2)}) collective-permute-start(bf16[3,6144]{1,0:T(4,128)(2,1)S(1)} %slice_bitcast_fusion), channel_id=1, source_target_pairs={{0,1},{1,2},{2,3},{3,4},{4,5},{5,6},{6,7},{7,8},{8,9},{9,10},{10,1... | collective-permute-start | bytes 110600 | tf_op jit(solution)/shard_map/ppermute | solution.py:444
  6.2 5.5 %tables.1 = (f32[16,128,128]{2,1,0:T(8,128)}, f32[8,128,8]{2,1,0:T(8,128)}, f32[48,128]{1,0:T(8,128)}) custom-call(f32[16,128]{1,0:T(8,128)} %bitcast.33, f32[16,128]{1,0:T(8,128)} %bitcast.34, f32[16,128]{1,0:T(8,128)} %bitcast.35), custom_call_target="tpu_custom_call" | custom-call | tf_op jit(solution)/shard_map/tables/pallas_call | solution.py:446
  11.7 0.0 collective-permute-done
  11.7 0.7 pad_convert_fusion.halo_ref
  12.4 5.5 %elements.3 = bf16[8,512,128]{2,1,0:T(8,128)(2,1)} custom-call(s32[1]{0:T(128)} %bitcast.9.base_ref, bf16[128,6144]{1,0:T(8,128)(2,1)} %bitcast.17, bf16[128,6144]{1,0:T(8,128)(2,1)} %bitcast.18, bf16[128,6144]{1,0:T(8,128)(2,1)} %bitcast.19, bf16[128,2048]{1,0:T(8,128)(2,1)} %bitcast.26, f32[8,6144]{1,0:T(8,128)} %pad_convert_fusion.halo_ref, ...), custom_call_target="tpu_custom_call" | custom-call | tf_op jit(solution)/shard_map/elements/pallas_call | solution.py:463
  17.9 0.0 collective-permute-start.1
  17.9 0.5 collective-permute-start.2
  18.4 0.1 pad_add_fusion.place_ref
  18.5 5.5 %elements.2.own_ref = bf16[8,512,128]{2,1,0:T(8,128)(2,1)} custom-call(s32[1]{0:T(128)} %bitcast.base_ref, bf16[128,6144]{1,0:T(8,128)(2,1)} %bitcast.20, bf16[128,6144]{1,0:T(8,128)(2,1)} %bitcast.21, bf16[128,6144]{1,0:T(8,128)(2,1)} %bitcast.22, bf16[128,2048]{1,0:T(8,128)(2,1)} %bitcast.27, f32[8,6144]{1,0:T(8,128)} %pad_convert_fusion.halo_ref, ...), custom_call_target="tpu_custom_call" | custom-call | tf_op jit(solution)/shard_map/elements/pallas_call | solution.py:463
  23.9 0.0 collective-permute-done.2.other_coef_ref
  23.9 0.0 collective-permute-done.1.other_ref
  24.0 1.2 copy-done.1
  25.2 2.4 %compose.1 = bf16[16,272,128]{2,1,0:T(8,128)(2,1)} custom-call(s32[2]{0:T(128)S(1)} %pad_add_fusion.place_ref, bf16[8,512,128]{2,1,0:T(8,128)(2,1)S(1)} %copy-done.1, bf16[8,512,128]{2,1,0:T(8,128)(2,1)S(1)} %collective-permute-done.1.other_ref, f32[48,128]{1,0:T(8,128)S(1)} %copy-done.4, f32[48,128]{1,0:T(8,128)S(1)} %collective-permute-done.2.other_coef_ref), custom_call_target="tpu_custom_call" | custom-call | tf_op jit(solution)/shard_map/compose/pallas_call | solution.py:491
  27.6 6.5 %all-to-all-start = ((bf16[16,272,128]{2,1,0:T(8,128)(2,1)}), bf16[16,272,128]{2,1,0:T(8,128)(2,1)S(1)}, u32[]{:S(2)}, u32[]{:S(2)}) async-start(bf16[16,272,128]{2,1,0:T(8,128)(2,1)} %compose.1), calls=%async_computation | async-start | bytes 2228224 | tf_op jit(solution)/shard_map/all_to_all | solution.py:504
  34.1 11.2 %inner.1 = (bf16[8,13,128,256]{3,2,1,0:T(8,128)(2,1)}, bf16[8,2,128,256]{3,2,1,0:T(8,128)(2,1)}) custom-call(bf16[128,6144]{1,0:T(8,128)(2,1)} %bitcast.23, bf16[128,6144]{1,0:T(8,128)(2,1)} %bitcast.24, bf16[128,6144]{1,0:T(8,128)(2,1)} %bitcast.25, bf16[128,2048]{1,0:T(8,128)(2,1)} %bitcast.28, f32[8,6144]{1,0:T(8,128)} %pad_convert_fusion.halo_ref, ...), custom_call_target="tpu_custom_call" | custom-call | tf_op jit(solution)/shard_map/inner/pallas_call | solution.py:509
  45.3 7.0 %all-to-all-done.got_ref = bf16[16,272,128]{2,1,0:T(8,128)(2,1)S(1)} async-done(((bf16[16,272,128]{2,1,0:T(8,128)(2,1)}), bf16[16,272,128]{2,1,0:T(8,128)(2,1)S(1)}, u32[]{:S(2)}, u32[]{:S(2)}) %all-to-all-start) | async-done | bytes 1114144 | tf_op jit(solution)/shard_map/all_to_all | solution.py:504
  52.3 0.3 scan.1
  52.7 20.7 %all_to_all.20.got_ref = bf16[16,272,128]{2,1,0:T(8,128)(2,1)S(1)} all-to-all(bf16[16,272,128]{2,1,0:T(8,128)(2,1)S(1)} %scan.1), channel_id=1, replica_groups={{0,2,4,6,8,10,12,14,16,18,20,22,24,26,28,30},{1,3,5,7,9,11,13,15,17,19,..., dimensions={0} | all-to-all | bytes 2228224 | tf_op jit(solution)/shard_map/all_to_all | solution.py:544
  73.4 1.3 spread.1
  74.7 0.0 copy-start.3
  74.7 1.0 copy-done.3
  75.7 1.9 %collective-permute-start.3 = (bf16[8,512,128]{2,1,0:T(8,128)(2,1)S(1)}, bf16[8,512,128]{2,1,0:T(8,128)(2,1)S(1)}, u32[]{:S(2)}, u32[]{:S(2)}) collective-permute-start(bf16[8,512,128]{2,1,0:T(8,128)(2,1)S(1)} %get-tuple-element.40), channel_id=1, source_target_pairs={{0,1},{1,0},{2,3},{3,2},{4,5},{5,4},{6,7},{7,6},{8,9},{9,8},{10,11... | collective-permute-start | bytes 3145736 | tf_op jit(solution)/shard_map/ppermute | solution.py:562
  77.6 0.7 broadcast_in_dim.10.before_ref
  78.3 5.8 %sense.2 = (f32[4,3,128,256]{3,2,1,0:T(8,128)}, bf16[2,16,3072]{2,1,0:T(8,128)(2,1)}, f32[96,128]{1,0:T(8,128)}) custom-call(s32[1]{0:T(128)} %bitcast.base_ref, bf16[8,13,128,256]{3,2,1,0:T(8,128)(2,1)} %get-tuple-element.36.in_ref, f32[8,6144]{1,0:T(8,128)} %pad_convert_fusion.halo_ref, f32[4,6144]{1,0:T(4,128)} %weight_ref.11, ...), custom_call_target="tpu_custom_call" | custom-call | tf_op jit(solution)/shard_map/sense/pallas_call | solution.py:568
  84.1 0.0 collective-permute-done.3.state_ref.other_ref
  84.1 1.0 copy-done.7
  85.1 5.8 %sense.3 = (f32[4,3,128,256]{3,2,1,0:T(8,128)}, bf16[2,16,3072]{2,1,0:T(8,128)(2,1)}, f32[96,128]{1,0:T(8,128)}) custom-call(s32[1]{0:T(128)} %bitcast.9.base_ref, bf16[8,13,128,256]{3,2,1,0:T(8,128)(2,1)} %get-tuple-element.36.in_ref, f32[8,6144]{1,0:T(8,128)} %pad_convert_fusion.halo_ref, f32[4,6144]{1,0:T(4,128)} %weight_ref.11, ...), custom_call_target="tpu_custom_call" | custom-call | tf_op jit(solution)/shard_map/sense/pallas_call | solution.py:568
  90.9 0.1 collective-permute-start.4
  91.0 1.4 %collective-permute-done.4 = f32[96,128]{1,0:T(8,128)S(1)} collective-permute-done((f32[96,128]{1,0:T(8,128)}, f32[96,128]{1,0:T(8,128)S(1)}, u32[]{:S(2)}, u32[]{:S(2)}) %collective-permute-start.4) | collective-permute-done | bytes 49184 | tf_op jit(solution)/shard_map/ppermute | solution.py:604
  92.4 0.8 broadcast_in_dim.22
  93.2 3.6 %all-to-all-start.2 = ((bf16[16,96,128]{2,1,0:T(8,128)(2,1)}), bf16[16,96,128]{2,1,0:T(8,128)(2,1)S(1)}, u32[]{:S(2)}, u32[]{:S(2)}) async-start(bf16[16,96,128]{2,1,0:T(8,128)(2,1)} %broadcast_in_dim.22), calls=%async_computation.2 | async-start | bytes 786432 | tf_op jit(solution)/shard_map/all_to_all | solution.py:667
  96.8 0.2 collective-permute-start.5
  97.1 1.0 collective-permute-done.5
  98.1 2.1 %collective-permute-start.6 = (bf16[2,16,3072]{2,1,0:T(8,128)(2,1)}, bf16[2,16,3072]{2,1,0:T(8,128)(2,1)S(1)}, u32[]{:S(2)}, u32[]{:S(2)}) collective-permute-start(bf16[2,16,3072]{2,1,0:T(8,128)(2,1)} %get-tuple-element.49), channel_id=1, source_target_pairs={{1,0},{2,1},{3,2},{4,3},{5,4},{6,5},{7,6},{8,7},{9,8},{10,9},{11,1... | collective-permute-start | bytes 589832 | tf_op jit(solution)/shard_map/ppermute | solution.py:610
  100.2 7.0 %readout.1 = bf16[128,2048]{1,0:T(8,128)(2,1)} custom-call(s32[2]{0:T(128)} %copy-done.5, bf16[8,2,128,256]{3,2,1,0:T(8,128)(2,1)} %get-tuple-element.45.read_ref, f32[8,128,8]{2,1,0:T(8,128)} %get-tuple-element.30.column_ref, bf16[8,512,128]{2,1,0:T(8,128)(2,1)} %copy-done.3, bf16[8,512,128]{2,1,0:T(8,128)(2,1)} %copy-done.7), custom_call_target="tpu_custom_call" | custom-call | tf_op jit(solution)/shard_map/readout/pallas_call | solution.py:619
  107.2 0.0 all-to-all-done.2
  107.2 0.1 reduce
  107.2 0.0 collective-permute-done.6.rim_own_ref.rim_other_ref
  107.3 0.8 broadcast_in_dim.24
  108.1 8.2 %all-to-all-start.3 = ((bf16[8,160,128]{2,1,0:T(8,128)(2,1)}), bf16[8,160,128]{2,1,0:T(8,128)(2,1)S(1)}, u32[]{:S(2)}, u32[]{:S(2)}) async-start(bf16[8,160,128]{2,1,0:T(8,128)(2,1)} %broadcast_in_dim.24), calls=%async_computation.3 | async-start | bytes 655360 | tf_op jit(solution)/shard_map/all_to_all | solution.py:667
  116.3 7.5 %unroll.1 = bf16[128,6144]{1,0:T(8,128)(2,1)} custom-call(s32[2]{0:T(128)} %copy-done.5, f32[4,3,128,256]{3,2,1,0:T(8,128)} %get-tuple-element.51.conv_own_ref, f32[4,3,128,256]{3,2,1,0:T(8,128)} %get-tuple-element.52.conv_other_ref, f32[4,6144]{1,0:T(4,128)} %weight_ref.11, bf16[2,16,3072]{2,1,0:T(8,128)(2,1)} %copy-done.8, bf16[2,16,3072]{2,1,0:T(8,128)(2,1)} %copy-done.8), custom_call_target="tpu_custom_call" | custom-call | tf_op jit(solution)/shard_map/unroll/pallas_call | solution.py:638
  123.8 4.3 %all-to-all-done.3 = bf16[8,160,128]{2,1,0:T(8,128)(2,1)S(1)} async-done(((bf16[8,160,128]{2,1,0:T(8,128)(2,1)}), bf16[8,160,128]{2,1,0:T(8,128)(2,1)S(1)}, u32[]{:S(2)}, u32[]{:S(2)}) %all-to-all-start.3) | async-done | bytes 327712 | tf_op jit(solution)/shard_map/all_to_all | solution.py:667
  128.2 2.4 %collective-permute-start.7 = (f32[96,128]{1,0:T(8,128)S(1)}, f32[96,128]{1,0:T(8,128)S(1)}, u32[]{:S(2)}, u32[]{:S(2)}) collective-permute-start(f32[96,128]{1,0:T(8,128)S(1)} %slice.16), channel_id=1, source_target_pairs={{0,1},{1,0},{2,3},{3,2},{4,5},{5,4},{6,7},{7,6},{8,9},{9,8},{10,11... | collective-permute-start | bytes 147464 | tf_op jit(solution)/shard_map/ppermute | solution.py:674
  130.6 0.6 slice.17
  131.3 0.3 collective-permute-done.7.other_ref
  131.5 1.2 assemble.1
  (23 shorter events, 0.1 us)
Async XLA Ops:
  0.6 33.5 %copy-start = (f32[16,128,128]{2,1,0:T(8,128)S(1)}, f32[16,128,128]{2,1,0:T(8,128)}, u32[]{:S(2)}) copy-start(f32[16,128,128]{2,1,0:T(8,128)} %param.9) | copy-start | bytes 3145732
  1.7 10.0 %collective-permute-start = (bf16[3,6144]{1,0:T(4,128)(2,1)S(1)}, bf16[3,6144]{1,0:T(4,128)(2,1)S(1)}, u32[]{:S(2)}, u32[]{:S(2)}) collective-permute-start(bf16[3,6144]{1,0:T(4,128)(2,1)S(1)} %slice_bitcast_fusion), channel_id=1, source_target_pairs={{0,1},{1,2},{2,3},{3,4},{4,5},{5,6},{6,7},{7,8},{8,9},{9,10},{10,1... | collective-permute-start | bytes 110600 | tf_op jit(solution)/shard_map/ppermute | solution.py:444
  12.4 5.5 %copy-start.4 = (f32[48,128]{1,0:T(8,128)S(1)}, f32[48,128]{1,0:T(8,128)}, u32[]{:S(2)}) copy-start(f32[48,128]{1,0:T(8,128)} %get-tuple-element.31.own_coef_ref) | copy-start | bytes 73732
  17.9 6.1 %collective-permute-start.1 = (bf16[8,512,128]{2,1,0:T(8,128)(2,1)}, bf16[8,512,128]{2,1,0:T(8,128)(2,1)S(1)}, u32[]{:S(2)}, u32[]{:S(2)}) collective-permute-start(bf16[8,512,128]{2,1,0:T(8,128)(2,1)} %elements.3), channel_id=1, source_target_pairs={{0,1},{1,0},{2,3},{3,2},{4,5},{5,4},{6,7},{7,6},{8,9},{9,8},{10,11... | collective-permute-start | bytes 3145736 | tf_op jit(solution)/shard_map/ppermute | solution.py:486
  17.9 6.1 %collective-permute-start.2 = (f32[48,128]{1,0:T(8,128)S(1)}, f32[48,128]{1,0:T(8,128)S(1)}, u32[]{:S(2)}, u32[]{:S(2)}) collective-permute-start(f32[48,128]{1,0:T(8,128)S(1)} %copy-done.4), channel_id=1, source_target_pairs={{0,1},{1,0},{2,3},{3,2},{4,5},{5,4},{6,7},{7,6},{8,9},{9,8},{10,11... | collective-permute-start | bytes 73736 | tf_op jit(solution)/shard_map/ppermute | solution.py:457
  18.5 54.9 %copy-start.5 = (s32[2]{0:T(128)}, s32[2]{0:T(128)S(1)}, u32[]{:S(2)}) copy-start(s32[2]{0:T(128)S(1)} %pad_add_fusion.place_ref) | copy-start | bytes 28
  24.0 1.2 copy-start.1
  27.6 24.7 %all-to-all-start = ((bf16[16,272,128]{2,1,0:T(8,128)(2,1)}), bf16[16,272,128]{2,1,0:T(8,128)(2,1)S(1)}, u32[]{:S(2)}, u32[]{:S(2)}) async-start(bf16[16,272,128]{2,1,0:T(8,128)(2,1)} %compose.1), calls=%async_computation | async-start | bytes 2228224 | tf_op jit(solution)/shard_map/all_to_all | solution.py:504
  52.7 20.7 %copy-start.2 = (bf16[8,512,128]{2,1,0:T(8,128)(2,1)S(1)}, bf16[8,512,128]{2,1,0:T(8,128)(2,1)}, u32[]{:S(2)}) copy-start(bf16[8,512,128]{2,1,0:T(8,128)(2,1)} %elements.2.own_ref) | copy-start | bytes 3145732
  74.7 1.0 copy-start.3
  75.7 8.4 %collective-permute-start.3 = (bf16[8,512,128]{2,1,0:T(8,128)(2,1)S(1)}, bf16[8,512,128]{2,1,0:T(8,128)(2,1)S(1)}, u32[]{:S(2)}, u32[]{:S(2)}) collective-permute-start(bf16[8,512,128]{2,1,0:T(8,128)(2,1)S(1)} %get-tuple-element.40), channel_id=1, source_target_pairs={{0,1},{1,0},{2,3},{3,2},{4,5},{5,4},{6,7},{7,6},{8,9},{9,8},{10,11... | collective-permute-start | bytes 3145736 | tf_op jit(solution)/shard_map/ppermute | solution.py:562
  84.1 1.0 copy-start.7
  85.1 7.4 %copy-start.9 = (f32[96,128]{1,0:T(8,128)S(1)}, f32[96,128]{1,0:T(8,128)}, u32[]{:S(2)}) copy-start(f32[96,128]{1,0:T(8,128)} %get-tuple-element.39) | copy-start | bytes 147460
  90.9 1.5 %collective-permute-start.4 = (f32[96,128]{1,0:T(8,128)}, f32[96,128]{1,0:T(8,128)S(1)}, u32[]{:S(2)}, u32[]{:S(2)}) collective-permute-start(f32[96,128]{1,0:T(8,128)} %get-tuple-element.42), channel_id=1, source_target_pairs={{0,1},{1,0},{2,3},{3,2},{4,5},{5,4},{6,7},{7,6},{8,9},{9,8},{10,11... | collective-permute-start | bytes 147464 | tf_op jit(solution)/shard_map/ppermute | solution.py:604
  93.2 13.9 %all-to-all-start.2 = ((bf16[16,96,128]{2,1,0:T(8,128)(2,1)}), bf16[16,96,128]{2,1,0:T(8,128)(2,1)S(1)}, u32[]{:S(2)}, u32[]{:S(2)}) async-start(bf16[16,96,128]{2,1,0:T(8,128)(2,1)} %broadcast_in_dim.22), calls=%async_computation.2 | async-start | bytes 786432 | tf_op jit(solution)/shard_map/all_to_all | solution.py:667
  96.8 1.3 collective-permute-start.5
  98.1 9.1 %collective-permute-start.6 = (bf16[2,16,3072]{2,1,0:T(8,128)(2,1)}, bf16[2,16,3072]{2,1,0:T(8,128)(2,1)S(1)}, u32[]{:S(2)}, u32[]{:S(2)}) collective-permute-start(bf16[2,16,3072]{2,1,0:T(8,128)(2,1)} %get-tuple-element.49), channel_id=1, source_target_pairs={{1,0},{2,1},{3,2},{4,3},{5,4},{6,5},{7,6},{8,7},{9,8},{10,9},{11,1... | collective-permute-start | bytes 589832 | tf_op jit(solution)/shard_map/ppermute | solution.py:610
  107.2 9.0 %copy-start.8 = (bf16[2,16,3072]{2,1,0:T(8,128)(2,1)}, bf16[2,16,3072]{2,1,0:T(8,128)(2,1)S(1)}, u32[]{:S(2)}) copy-start(bf16[2,16,3072]{2,1,0:T(8,128)(2,1)S(1)} %collective-permute-done.6.rim_own_ref.rim_other_ref) | copy-start | bytes 589828
  108.1 20.1 %all-to-all-start.3 = ((bf16[8,160,128]{2,1,0:T(8,128)(2,1)}), bf16[8,160,128]{2,1,0:T(8,128)(2,1)S(1)}, u32[]{:S(2)}, u32[]{:S(2)}) async-start(bf16[8,160,128]{2,1,0:T(8,128)(2,1)} %broadcast_in_dim.24), calls=%async_computation.3 | async-start | bytes 655360 | tf_op jit(solution)/shard_map/all_to_all | solution.py:667
  116.3 15.3 %copy-start.6 = (s32[2]{0:T(128)S(1)}, s32[2]{0:T(128)}, u32[]{:S(2)}) copy-start(s32[2]{0:T(128)} %copy-done.5) | copy-start | bytes 28
  128.2 3.3 %collective-permute-start.7 = (f32[96,128]{1,0:T(8,128)S(1)}, f32[96,128]{1,0:T(8,128)S(1)}, u32[]{:S(2)}, u32[]{:S(2)}) collective-permute-start(f32[96,128]{1,0:T(8,128)S(1)} %slice.16), channel_id=1, source_target_pairs={{0,1},{1,0},{2,3},{3,2},{4,5},{5,4},{6,7},{7,6},{8,9},{9,8},{10,11... | collective-permute-start | bytes 147464 | tf_op jit(solution)/shard_map/ppermute | solution.py:674

commit v2 on v1

--- a/solution.py
+++ b/solution.py
@@ -8,9 +8,10 @@
 from jax.sharding import PartitionSpec as P
 
 DK = 128
+SIDES = 8
 BF = jnp.bfloat16
 F32 = jnp.float32
-PARAMS = pltpu.CompilerParams(vmem_limit_bytes=60 * 1024 * 1024)
+PARAMS = pltpu.CompilerParams(vmem_limit_bytes=32 * 1024 * 1024)
 SHARED = pltpu.CompilerParams(vmem_limit_bytes=32 * 1024 * 1024)
 CHIPS = 16
 HALF = 8
@@ -26,8 +27,8 @@
     return jnp.sum(jnp.where(eye, row, 0.0), axis=1, keepdims=True)
 
 
-def tables_kernel(forget_ref, momentum_ref, rate_ref, coupling_ref, column_ref, coef_ref):
-    heads, tokens = forget_ref.shape
+def tables_kernel(gate_ref, coupling_ref, column_ref, coef_ref):
+    heads, tokens = gate_ref.shape[0] // 3, gate_ref.shape[1]
     rows = lax.broadcasted_iota(jnp.int32, (tokens, tokens), 0)
     lanes = lax.broadcasted_iota(jnp.int32, (tokens, tokens), 1)
     eye = rows == lanes
@@ -39,14 +40,14 @@
         precision=lax.Precision.HIGHEST,
         preferred_element_type=F32,
     )
-    cum_forget = exact(forget_ref[...], upper)
-    cum_moment = exact(momentum_ref[...], upper)
-    narrow = lax.broadcasted_iota(jnp.int32, (tokens, 8), 1)
+    cum_forget = exact(gate_ref[0:heads], upper)
+    cum_moment = exact(gate_ref[heads : 2 * heads], upper)
+    narrow = lax.broadcasted_iota(jnp.int32, (tokens, 4 * SIDES), 1)
     last = tokens - 1
     for h in range(heads):
         forget_row = cum_forget[h : h + 1, :]
         moment_row = cum_moment[h : h + 1, :]
-        rate_row = rate_ref[h : h + 1, :]
+        rate_row = gate_ref[2 * heads + h : 2 * heads + h + 1, :]
         forget_col = to_column(forget_row, eye)
         moment_col = to_column(moment_row, eye)
         rate_col = to_column(rate_row, eye)
@@ -55,7 +56,7 @@
         coupling = dot(forget_map.astype(BF), moment_map.astype(BF), (1, 0))
         carry = coupling[:, 0:1] * jnp.exp(moment_row[:, 0:1])
         rated = coupling * rate_row
-        coupling_ref[h] = rated
+        coupling_ref[h] = rated.astype(BF)
         memory_col = to_column(rated[last : last + 1, :], eye)
         tail_col = rate_col * jnp.exp(jnp.minimum(moment_row[:, last:] - moment_col, 0.0))
         quad = jnp.where(
@@ -63,10 +64,9 @@
             memory_col,
             jnp.where(narrow % 4 == 1, tail_col, jnp.where(narrow % 4 == 2, jnp.exp(forget_col), carry)),
         )
-        if h % 2 == 0:
-            first_quad = quad
-        else:
-            column_ref[h // 2] = jnp.where(narrow < 4, first_quad, quad)
+        packed = quad if h % SIDES == 0 else jnp.where(narrow // 4 == h % SIDES, quad, packed)
+        if h % SIDES == SIDES - 1:
+            column_ref[h // SIDES] = packed
         spread = functools.partial(jnp.broadcast_to, shape=(1, tokens))
         coef_ref[h : h + 1, :] = spread(jnp.exp(forget_row[:, last:]))
         coef_ref[heads + h : heads + h + 1, :] = spread(carry[last : last + 1, :])
@@ -75,7 +75,7 @@
 
 def extend(ext_ref, slot, halo, own):
     cols = slice(slot * DK, (slot + 1) * DK)
-    ext_ref[0:8, cols] = halo
+    ext_ref[5:8, cols] = halo.astype(F32)
     ext_ref[8 : 8 + own.shape[0], cols] = own.astype(F32)
 
 
@@ -87,12 +87,16 @@
     return total
 
 
+def first_block(mine, place_ref, blocks):
+    return (place_ref[0] if mine else 1 - place_ref[0]) * (blocks // 2)
+
+
 def element_kernel(
-    base_ref, q_ref, k_ref, v_ref, u_ref, halo_ref, weight_ref, column_ref, element_ref, ext_ref
+    mine, place_ref, q_ref, k_ref, v_ref, u_ref, halo_ref, weight_ref, column_ref, element_ref, ext_ref
 ):
     tokens, width = q_ref.shape
     section = halo_ref.shape[1] // 3
-    block = base_ref[0] + pl.program_id(0)
+    block = first_block(mine, place_ref, section // width) + pl.program_id(0)
     for side in range(width // DK):
         cols = slice(side * DK, (side + 1) * DK)
         made = []
@@ -172,7 +176,7 @@
             out_ref[2 * j + half, 256:PIECE] = tail
 
 
-def scan_kernel(got_ref, start_ref, out_ref):
+def scan_kernel(place_ref, got_ref, start_ref, out_ref):
     count = got_ref.shape[0]
 
     def coefs(c):
@@ -206,7 +210,7 @@
 
 
 def spread_kernel(
-    place_ref, got_ref, own_ref, other_ref, own_coef_ref, other_coef_ref, keep_ref, send_ref, start_ref
+    place_ref, got_ref, own_ref, other_ref, own_coef_ref, other_coef_ref, keep_ref, send_ref
 ):
     core = place_ref[0]
     side = place_ref[1]
@@ -251,8 +255,9 @@
             at = slice(which * DK, (which + 1) * DK)
             keep_ref[j, at] = jnp.where(first_core, one[which], two[which]).astype(BF)
             send_ref[j, at] = jnp.where(first_core, two[which], one[which]).astype(BF)
-        rows = got_ref[2 * j + side, 256:PIECE].astype(F32)
-        start_ref[j] = rows[0:8] + rows[8:16]
+        start = got_ref[2 * j + side, 256:PIECE]
+        keep_ref[j, 4 * DK :] = start
+        send_ref[j, 4 * DK :] = start
 
 
 def inner_kernel(
@@ -287,7 +292,7 @@
         query, key, value = made
         upstream = u_ref[:, cols]
         out_ref[0, 3, :, cols] = upstream
-        coupling = coupling_ref[side]
+        coupling = coupling_ref[side].astype(F32)
         scores = (dot(query, key, (1, 1)) * coupling).astype(BF)
         sense = (dot(upstream, value, (1, 1)) * coupling).astype(BF)
         grads = (
@@ -314,20 +319,25 @@
 
 
 def sense_kernel(
-    base_ref, in_ref, halo_ref, weight_ref, column_ref, state_ref, before_ref,
-    conv_ref, rim_ref, tap_ref, pad_ref, ext_ref,
+    mine, place_ref, in_ref, halo_ref, weight_ref, column_ref, state_ref, *refs
 ):
+    conv_ref, rim_ref, tap_ref, pad_ref, ext_ref = refs[-5:]
+    step = pl.program_id(0)
     tokens = in_ref.shape[2]
     width = in_ref.shape[3]
     section = halo_ref.shape[1] // 3
-    block = base_ref[0] + pl.program_id(0)
+    block = first_block(mine, place_ref, section // width) + step
+    if len(refs) > 5:
+        rim_ref[0] = refs[0][1]
+    else:
+        rim_ref[0] = jnp.zeros(rim_ref.shape[1:], BF)
 
     @pl.when(pl.program_id(0) == 0)
     def _():
         pad_ref[0:8] = jnp.zeros((8, pad_ref.shape[1]), F32)
         pad_ref[8 + tokens :] = jnp.zeros((8, pad_ref.shape[1]), F32)
-
-    rim_ref[0] = before_ref[1]
+        ext_ref[0:8] = jnp.zeros((8, ext_ref.shape[1]), F32)
+
     for side in range(width // DK):
         cols = slice(side * DK, (side + 1) * DK)
         query, key, value, upstream = (in_ref[0, i, :, cols] for i in range(4))
@@ -348,8 +358,8 @@
                 grad = grad - unit * jnp.sum(unit * grad, axis=1, keepdims=True)
             grad = grad * in_ref[0, 4 + part, :, cols].astype(F32)
             grad = grad + in_ref[0, 7 + part, :, cols].astype(F32)
-            conv_ref[0, part, :, cols] = grad
             slot = side * 3 + part
+            conv_ref[0, slot] = grad.astype(BF)
             there = slice(slot * DK, (slot + 1) * DK)
             pad_ref[8 : 8 + tokens, there] = grad
             at = pl.ds(pl.multiple_of(part * section + block * width + side * DK, DK), DK)
@@ -359,7 +369,7 @@
             rim = None
             for tap in range(4):
                 moved = pad_ref[3 - tap : 3 - tap + 8 + tokens, there]
-                slot_row = 12 * (2 * pl.program_id(0) + side) + 4 * part + tap
+                slot_row = 12 * (SIDES * pl.program_id(0) + side) + 4 * part + tap
                 tap_ref[pl.ds(slot_row, 1), :] = jnp.sum(moved * rows, axis=0, keepdims=True)
                 lead = moved[0:8] * weights[tap : tap + 1]
                 rim = lead if rim is None else rim + lead
@@ -368,7 +378,10 @@
             ).astype(BF)
 
 
-def readout_kernel(place_ref, read_ref, column_ref, own_ref, other_ref, output_ref):
+def readout_kernel(
+    place_ref, read_ref, column_ref, own_ref, other_ref, own_start_ref, other_start_ref,
+    output_ref, start_ref,
+):
     width = read_ref.shape[3]
     owned = (pl.program_id(0) // (pl.num_programs(0) // 2)) == place_ref[0]
     for side in range(width // DK):
@@ -378,12 +391,16 @@
         from_memory, from_moment = along_rows(read_ref[0, 0, :, cols], states)
         readout = read_ref[0, 1, :, cols].astype(F32) + column[:, 2:3] * from_memory + column[:, 3:4] * from_moment
         output_ref[:, cols] = readout.astype(BF)
+        rows = jnp.where(owned, own_start_ref[side], other_start_ref[side]).astype(F32)
+        rows = rows[0:8] + rows[8:16]
+        start_ref[4 * side : 4 * side + 4] = jnp.where(place_ref[0] == 0, rows[0:4], rows[4:8])
 
 
 def unroll_kernel(
     place_ref, conv_own_ref, conv_other_ref, weight_ref, rim_own_ref, rim_other_ref, grad_ref, pad_ref
 ):
-    tokens, width = conv_own_ref.shape[2:]
+    tokens = conv_own_ref.shape[2]
+    width = conv_own_ref.shape[1] // 3 * DK
     section = weight_ref.shape[1] // 3
     block = pl.program_id(0)
     owned = (block // (pl.num_programs(0) // 2)) == place_ref[0]
@@ -398,7 +415,7 @@
             at = pl.ds(pl.multiple_of(part * section + block * width + side * DK, DK), DK)
             slot = side * 3 + part
             there = slice(slot * DK, (slot + 1) * DK)
-            grad = jnp.where(owned, conv_own_ref[0, part, :, cols], conv_other_ref[0, part, :, cols])
+            grad = jnp.where(owned, conv_own_ref[0, slot], conv_other_ref[0, slot]).astype(F32)
             weights = weight_ref[:, at]
             pad_ref[0:tokens, there] = grad
             total = grad * weights[3:4]
@@ -410,8 +427,33 @@
             grad_ref[:, at] = total.astype(BF)
 
 
-def assemble_kernel(place_ref, own_ref, other_ref, out_ref):
+def pack_kernel(own_ref, far_ref, out_ref):
+    value = (own_ref[...] + far_ref[...]).astype(BF)
+    for i in range(out_ref.shape[0]):
+        out_ref[i] = value
+
+
+def fold_kernel(pieces_ref, start_ref, out_ref):
+    total = pieces_ref[0].astype(F32)
+    for i in range(1, pieces_ref.shape[0]):
+        total = total + pieces_ref[i].astype(F32)
+    value = jnp.concatenate([total, start_ref[...]], axis=0).astype(BF)
+    for i in range(out_ref.shape[0]):
+        out_ref[i] = value
+
+
+def sum_kernel(pieces_ref, out_ref):
+    total = pieces_ref[0].astype(F32)
+    for i in range(1, pieces_ref.shape[0]):
+        total = total + pieces_ref[i].astype(F32)
+    out_ref[...] = total
+
+
+def assemble_kernel(place_ref, own_ref, other_ref, out_ref, start_ref):
     section = out_ref.shape[1] // 3
+    for h in range(section // DK):
+        first = 12 * HALF + 4 * h
+        start_ref[h] = own_ref[first : first + 4]
     for h in range(section // DK):
         for part in range(3):
             first = 12 * (h % HALF) + 4 * part
@@ -431,13 +473,15 @@
     upstream = cotangent[0]
     tokens, channels = rows.shape
     heads = initial_memory.shape[0]
-    width = 2 * DK
+    width = SIDES * DK
     blocks = heads * DK // width
     count = lax.axis_size("seq")
     mine = lax.axis_index("seq")
     core = mine % 2
     chip = mine // 2
-    place = jnp.stack([core, chip // 8]).astype(jnp.int32)
+    place = jnp.stack([core, chip // 8, core * (HALF * DK // 64) + chip]).astype(jnp.int32)
+    gates = jnp.concatenate([log_forget[0], log_momentum[0], learn_rate[0]], axis=0)
+    gates, place = lax.optimization_barrier((gates, place))
     pairs = [(i, i ^ 1) for i in range(count)]
     groups = [[2 * c + k for c in range(count // 2)] for k in range(2)]
 
@@ -446,22 +490,25 @@
     coupling, columns, coefs = pl.pallas_call(
         tables_kernel,
         out_shape=(
-            shape((heads, tokens, tokens), F32),
-            shape((heads // 2, tokens, 8), F32),
+            shape((heads, tokens, tokens), BF),
+            shape((heads // SIDES, tokens, 4 * SIDES), F32),
             shape((3 * heads, DK), F32),
         ),
         compiler_params=PARAMS,
         name="tables",
-    )(log_forget[0], log_momentum[0], learn_rate[0])
-    halo = jnp.pad(rim.astype(F32), ((5, 0), (0, 0)))
+        cost_estimate=pl.CostEstimate(flops=4000000000, transcendentals=0, bytes_accessed=14400000),
+    )(gates)
     other_coefs = lax.ppermute(coefs, "seq", pairs)
 
-    def elements(base):
+    def elements(mine):
+        def first(b):
+            return first_block(mine, b, blocks)
+
         def block_of(part):
-            return pl.BlockSpec((tokens, width), lambda i, b: (0, part * blocks + b[0] + i))
+            return pl.BlockSpec((tokens, width), lambda i, b: (0, part * blocks + first(b) + i))
 
         return pl.pallas_call(
-            element_kernel,
+            functools.partial(element_kernel, mine),
             out_shape=shape((heads // 2, 4 * DK, DK), BF),
             grid_spec=pltpu.PrefetchScalarGridSpec(
                 num_scalar_prefetch=1,
@@ -471,20 +518,21 @@
                     block_of(1),
                     block_of(2),
                     block_of(0),
-                    whole(8, channels),
+                    whole(3, channels),
                     whole(4, channels),
-                    pl.BlockSpec((1, tokens, 8), lambda i, b: (b[0] + i, 0, 0)),
+                    pl.BlockSpec((1, tokens, 4 * SIDES), lambda i, b: (first(b) + i, 0, 0)),
                 ],
-                out_specs=pl.BlockSpec((2, 4 * DK, DK), lambda i, b: (i, 0, 0)),
-                scratch_shapes=[pltpu.VMEM((tokens + 8, 6 * DK), F32)],
+                out_specs=pl.BlockSpec((SIDES, 4 * DK, DK), lambda i, b: (i, 0, 0)),
+                scratch_shapes=[pltpu.VMEM((tokens + 8, 3 * SIDES * DK), F32)],
             ),
             compiler_params=PARAMS,
             name="elements",
-        )(base.astype(jnp.int32).reshape(1), rows, rows, rows, upstream, halo, conv_weight, columns)
-
-    sent = elements((1 - core) * (blocks // 2))
+            cost_estimate=pl.CostEstimate(flops=3400000000, transcendentals=0, bytes_accessed=12240000),
+        )(place, rows, rows, rows, upstream, rim, conv_weight, columns)
+
+    sent = elements(False)
     other = lax.ppermute(sent, "seq", pairs)
-    own = elements(core * (blocks // 2))
+    own = elements(True)
 
     by_two = pl.BlockSpec((2, 4 * DK, DK), lambda i, b: (i, 0, 0))
     pieces = pl.BlockSpec((4, PIECE, DK), lambda i, b: (i, 0, 0))
@@ -499,6 +547,7 @@
         ),
         compiler_params=SHARED,
         name="compose",
+        cost_estimate=pl.CostEstimate(flops=1200000000, transcendentals=0, bytes_accessed=4320000),
     )(place, own, other, coefs, other_coefs)
     payload, coupling = lax.optimization_barrier((payload, coupling))
     got = lax.all_to_all(payload, "seq", 0, 0, axis_index_groups=groups)
@@ -518,57 +567,64 @@
             block_at(1),
             block_at(2),
             block_at(0),
-            whole(8, channels),
+            whole(3, channels),
             whole(4, channels),
-            pl.BlockSpec((2, tokens, tokens), lambda i: (i, 0, 0)),
+            pl.BlockSpec((SIDES, tokens, tokens), lambda i: (i, 0, 0)),
         ],
         out_specs=(
             pl.BlockSpec((1, 13, tokens, width), lambda i: (i, 0, 0, 0)),
             pl.BlockSpec((1, 2, tokens, width), lambda i: (i, 0, 0, 0)),
         ),
-        scratch_shapes=[pltpu.VMEM((tokens + 8, 6 * DK), F32)],
+        scratch_shapes=[pltpu.VMEM((tokens + 8, 3 * SIDES * DK), F32)],
         compiler_params=PARAMS,
         name="inner",
-    )(rows, rows, rows, upstream, halo, conv_weight, coupling)
-
-    start = lax.dynamic_slice_in_dim(
-        initial_memory.reshape(heads * DK, DK), core * (HALF * DK) + chip * 64, 64, 0
-    )
-    got, inner = lax.optimization_barrier((got, inner))
+        cost_estimate=pl.CostEstimate(flops=8000000000, transcendentals=0, bytes_accessed=28800000),
+    )(rows, rows, rows, upstream, rim, conv_weight, coupling)
+
+    got, inner, inside = lax.optimization_barrier((got, inner, inside))
     back = pl.pallas_call(
         scan_kernel,
         out_shape=shape((CHIPS, PIECE, DK), BF),
+        grid_spec=pltpu.PrefetchScalarGridSpec(
+            num_scalar_prefetch=1,
+            grid=(1,),
+            in_specs=[whole(CHIPS, PIECE, DK), pl.BlockSpec((64, DK), lambda i, b: (b[2], 0))],
+            out_specs=whole(CHIPS, PIECE, DK),
+        ),
         compiler_params=SHARED,
         name="scan",
-    )(got, start)
+        cost_estimate=pl.CostEstimate(flops=400000000, transcendentals=0, bytes_accessed=1440000),
+    )(place, got, initial_memory.reshape(heads * DK, DK))
     states = lax.all_to_all(back, "seq", 0, 0, axis_index_groups=groups)
 
-    kept, passed, start_grad = pl.pallas_call(
+    kept, passed = pl.pallas_call(
         spread_kernel,
         out_shape=(
-            shape((HALF, 4 * DK, DK), BF),
-            shape((HALF, 4 * DK, DK), BF),
-            shape((HALF, 8, DK), F32),
+            shape((HALF, 4 * DK + EXTRA, DK), BF),
+            shape((HALF, 4 * DK + EXTRA, DK), BF),
         ),
         grid_spec=pltpu.PrefetchScalarGridSpec(
             num_scalar_prefetch=1,
             grid=(HALF // 2,),
             in_specs=[pieces, by_two, by_two, whole(3 * heads, DK), whole(3 * heads, DK)],
-            out_specs=(by_two, by_two, pl.BlockSpec((2, 8, DK), lambda i, b: (i, 0, 0))),
+            out_specs=(pl.BlockSpec((2, 4 * DK + EXTRA, DK), lambda i, b: (i, 0, 0)),) * 2,
         ),
         compiler_params=SHARED,
         name="spread",
+        cost_estimate=pl.CostEstimate(flops=1300000000, transcendentals=0, bytes_accessed=4680000),
     )(place, states, own, other, coefs, other_coefs)
     received = lax.ppermute(passed, "seq", pairs)
-    other_start = lax.ppermute(start_grad, "seq", pairs)
 
     half_blocks = blocks // 2
 
-    def sense(base, state, before):
+    def sense(mine, state, *before):
+        def first(b):
+            return first_block(mine, b, blocks)
+
         return pl.pallas_call(
-            sense_kernel,
+            functools.partial(sense_kernel, mine),
             out_shape=(
-                shape((half_blocks, 3, tokens, width), F32),
+                shape((half_blocks, 3 * SIDES, tokens, DK), BF),
                 shape((2, 16, channels // 2), BF),
                 shape((12 * HALF, DK), F32),
             ),
@@ -576,30 +632,30 @@
                 num_scalar_prefetch=1,
                 grid=(half_blocks,),
                 in_specs=[
-                    pl.BlockSpec((1, 13, tokens, width), lambda i, b: (b[0] + i, 0, 0, 0)),
-                    whole(8, channels),
+                    pl.BlockSpec((1, 13, tokens, width), lambda i, b: (first(b) + i, 0, 0, 0)),
+                    whole(3, channels),
                     whole(4, channels),
-                    pl.BlockSpec((1, tokens, 8), lambda i, b: (b[0] + i, 0, 0)),
-                    by_two,
-                    pl.BlockSpec((2, 16, 3 * width), lambda i, b: (0, 0, i)),
+                    pl.BlockSpec((1, tokens, 4 * SIDES), lambda i, b: (first(b) + i, 0, 0)),
+                    pl.BlockSpec((SIDES, 4 * DK, DK), lambda i, b: (i, 0, 0)),
+                    *[pl.BlockSpec((2, 16, 3 * width), lambda i, b: (0, 0, i)) for _ in before],
                 ],
                 out_specs=(
-                    pl.BlockSpec((1, 3, tokens, width), lambda i, b: (i, 0, 0, 0)),
+                    pl.BlockSpec((1, 3 * SIDES, tokens, DK), lambda i, b: (i, 0, 0, 0)),
                     pl.BlockSpec((2, 16, 3 * width), lambda i, b: (0, 0, i)),
                     whole(12 * HALF, DK),
                 ),
                 scratch_shapes=[
-                    pltpu.VMEM((tokens + 16, 6 * DK), F32),
-                    pltpu.VMEM((tokens + 8, 6 * DK), F32),
+                    pltpu.VMEM((tokens + 16, 3 * SIDES * DK), F32),
+                    pltpu.VMEM((tokens + 8, 3 * SIDES * DK), F32),
                 ],
             ),
             compiler_params=PARAMS,
             name="sense",
-        )(base.astype(jnp.int32).reshape(1), inner, halo, conv_weight, columns, state, before)
-
-    rim = jnp.zeros((2, 16, channels // 2), BF)
-    conv_own, rim, tap_own = sense(core * half_blocks, kept, rim)
-    conv_other, rim, tap_other = sense((1 - core) * half_blocks, received, rim)
+            cost_estimate=pl.CostEstimate(flops=3000000000, transcendentals=0, bytes_accessed=10800000),
+        )(place, inner, rim, conv_weight, columns, state, *before)
+
+    conv_own, edge, tap_own = sense(True, kept)
+    conv_other, edge, tap_other = sense(False, received, edge)
 
     tap_far = lax.ppermute(tap_other, "seq", pairs)
 
@@ -607,7 +663,7 @@
         return jnp.where(core == 0, one, two), jnp.where(core == 0, two, one)
 
     back_one = [(i + 1, i) for i in range(count - 1)]
-    rim = lax.ppermute(rim, "seq", back_one)
+    edge = lax.ppermute(edge, "seq", back_one)
 
     def own_at(i, b):
         return jnp.clip(i - b[0] * half_blocks, 0, half_blocks - 1)
@@ -618,21 +674,27 @@
     def readouts(inside):
         return pl.pallas_call(
             readout_kernel,
-            out_shape=shape((tokens, heads * DK), BF),
+            out_shape=(shape((tokens, heads * DK), BF), shape((4 * heads, DK), F32)),
             grid_spec=pltpu.PrefetchScalarGridSpec(
                 num_scalar_prefetch=1,
                 grid=(blocks,),
                 in_specs=[
                     pl.BlockSpec((1, 2, tokens, width), lambda i, b: (i, 0, 0, 0)),
-                    pl.BlockSpec((1, tokens, 8), lambda i, b: (i, 0, 0)),
-                    pl.BlockSpec((2, 2 * DK, DK), lambda i, b: (own_at(i, b), 0, 0)),
-                    pl.BlockSpec((2, 2 * DK, DK), lambda i, b: (other_at(i, b), 0, 0)),
+                    pl.BlockSpec((1, tokens, 4 * SIDES), lambda i, b: (i, 0, 0)),
+                    pl.BlockSpec((SIDES, 2 * DK, DK), lambda i, b: (own_at(i, b), 0, 0)),
+                    pl.BlockSpec((SIDES, 2 * DK, DK), lambda i, b: (other_at(i, b), 0, 0)),
+                    pl.BlockSpec((SIDES, EXTRA, DK), lambda i, b: (own_at(i, b), 4 * DK // EXTRA, 0)),
+                    pl.BlockSpec((SIDES, EXTRA, DK), lambda i, b: (other_at(i, b), 4 * DK // EXTRA, 0)),
                 ],
-                out_specs=pl.BlockSpec((tokens, width), lambda i, b: (0, i)),
+                out_specs=(
+                    pl.BlockSpec((tokens, width), lambda i, b: (0, i)),
+                    pl.BlockSpec((4 * SIDES, DK), lambda i, b: (i, 0)),
+                ),
             ),
             compiler_params=PARAMS,
             name="readout",
-        )(place, inside, columns, kept, received)
+            cost_estimate=pl.CostEstimate(flops=3000000000, transcendentals=0, bytes_accessed=10800000),
+        )(place, inside, columns, kept, received, kept, received)
 
     def unrolled(rim):
         return pl.pallas_call(
@@ -642,51 +704,67 @@
                 num_scalar_prefetch=1,
                 grid=(blocks,),
                 in_specs=[
-                    pl.BlockSpec((1, 3, tokens, width), lambda i, b: (own_at(i, b), 0, 0, 0)),
-                    pl.BlockSpec((1, 3, tokens, width), lambda i, b: (other_at(i, b), 0, 0, 0)),
+                    pl.BlockSpec((1, 3 * SIDES, tokens, DK), lambda i, b: (own_at(i, b), 0, 0, 0)),
+                    pl.BlockSpec((1, 3 * SIDES, tokens, DK), lambda i, b: (other_at(i, b), 0, 0, 0)),
                     whole(4, channels),
                     pl.BlockSpec((1, 16, 3 * width), lambda i, b: (1, 0, own_at(i, b))),
                     pl.BlockSpec((1, 16, 3 * width), lambda i, b: (0, 0, other_at(i, b))),
                 ],
                 out_specs=whole(tokens, channels),
-                scratch_shapes=[pltpu.VMEM((tokens + 8, 6 * DK), F32)],
+                scratch_shapes=[pltpu.VMEM((tokens + 8, 3 * SIDES * DK), F32)],
             ),
             compiler_params=PARAMS,
             name="unroll",
+            cost_estimate=pl.CostEstimate(flops=4000000000, transcendentals=0, bytes_accessed=14400000),
         )(place, conv_own, conv_other, conv_weight, rim, rim)
 
-    start_own = lax.dynamic_slice_in_dim(start_grad, 4 * core, 4, 1)
-    start_other = lax.dynamic_slice_in_dim(other_start, 4 * core, 4, 1)
-    start_all = jnp.concatenate(ordered(start_own, start_other), axis=0)
-    start_all = start_all.reshape(4 * heads, DK)
-
-    def gathered_sum(value, axis, size, axis_groups, ready, beside):
-        value = value.astype(BF)
-        value, ready = lax.optimization_barrier((value, ready))
-        spread = jnp.broadcast_to(value[None], (size, *value.shape))
-        pieces = lax.all_to_all(spread, axis, 0, 0, axis_index_groups=axis_groups)
-        pieces, made = lax.optimization_barrier((pieces, beside(ready)))
-        return jnp.sum(pieces.astype(F32), axis=0), made
-
-    total, output = gathered_sum(tap_own + tap_far, "seq", CHIPS, groups, inside, readouts)
-    total = jnp.concatenate([total, start_all], axis=0)
-    total, grad = gathered_sum(total, "dp", lax.axis_size("dp"), None, rim, unrolled)
-    tap_far = lax.ppermute(total[: 12 * HALF], "seq", pairs)
-    start_all = total[12 * HALF :].reshape(heads, 4, DK)
-
-    taps = pl.pallas_call(
+    dp = lax.axis_size("dp")
+    tap_rows = 12 * HALF
+    sum_rows = tap_rows + 4 * heads
+    spread_taps = pl.pallas_call(
+        pack_kernel,
+        out_shape=shape((CHIPS, tap_rows, DK), BF),
+        compiler_params=SHARED,
+        name="pack",
+        cost_estimate=pl.CostEstimate(flops=800000000, transcendentals=0, bytes_accessed=2880000),
+    )(tap_own, tap_far)
+
+    spread_taps, inside = lax.optimization_barrier((spread_taps, inside))
+    pieces = lax.all_to_all(spread_taps, "seq", 0, 0, axis_index_groups=groups)
+    output, start_all = readouts(inside)
+    pieces, output = lax.optimization_barrier((pieces, output))
+    spread_sums = pl.pallas_call(
+        fold_kernel,
+        out_shape=shape((dp, sum_rows, DK), BF),
+        compiler_params=SHARED,
+        name="fold",
+        cost_estimate=pl.CostEstimate(flops=800000000, transcendentals=0, bytes_accessed=2880000),
+    )(pieces, start_all)
+    spread_sums, edge = lax.optimization_barrier((spread_sums, edge))
+    pieces = lax.all_to_all(spread_sums, "dp", 0, 0)
+    grad = unrolled(edge)
+    pieces, grad = lax.optimization_barrier((pieces, grad))
+    total = pl.pallas_call(
+        sum_kernel,
+        out_shape=shape((sum_rows, DK), F32),
+        compiler_params=SHARED,
+        name="total",
+        cost_estimate=pl.CostEstimate(flops=800000000, transcendentals=0, bytes_accessed=2880000),
+    )(pieces)
+    total_far = lax.ppermute(total, "seq", pairs)
+    taps, start_all = pl.pallas_call(
         assemble_kernel,
-        out_shape=shape((4, channels), F32),
+        out_shape=(shape((4, channels), F32), shape((heads, 4, DK), F32)),
         grid_spec=pltpu.PrefetchScalarGridSpec(
             num_scalar_prefetch=1,
             grid=(1,),
-            in_specs=[whole(12 * HALF + 4 * heads, DK), whole(12 * HALF, DK)],
-            out_specs=whole(4, channels),
+            in_specs=[whole(sum_rows, DK)] * 2,
+            out_specs=(whole(4, channels), whole(heads, 4, DK)),
         ),
         compiler_params=SHARED,
         name="assemble",
-    )(place, total, tap_far)
-
+        cost_estimate=pl.CostEstimate(flops=1000000000, transcendentals=0, bytes_accessed=3600000),
+    )(place, total, total_far)
     return (output[None], grad[None], taps, start_all)
 
 

time: 134 us -> 121 us (0.903)
  Pallas kernels: 59 us -> 38.3 us
  local copies, waits for them, and re-layouts: 7.13 us -> 12.3 us
  waiting for transfers between devices: 14.1 us -> 16.2 us
    pallas_call x9 -> x12, Pallas kernels: 37.8 us -> 24.8 us  [the longest x2 7.17 us: elements(): pl.pallas_call(functools.partial(element_kernel, mine), out_shape=shape((...]
    unnamed x20 -> x36, local copies, waits for them, and re-layouts: 3.18 us -> 11.4 us
    all_to_all x2, waiting for transfers between devices: 4.35 us -> 10.5 us  [the longest x1 7.49 us: local(): pieces = lax.all_to_all(spread_sums, 'dp', 0, 0)]
    pallas_call x1, Pallas kernels: 7.54 us -> 3.66 us  [unrolled(): pl.pallas_call(unroll_kernel, out_shape=shape((tokens, channels), BF), gr...]
    pallas_call x1, Pallas kernels: 11.2 us -> 7.35 us  [local(): pl.pallas_call(inner_kernel, out_shape=(shape((blocks, 13, tokens, width)...]
    all_to_all x1, waiting for transfers between devices: 7 us -> 3.56 us  [local(): got = lax.all_to_all(payload, 'seq', 0, 0, axis_index_groups=groups)]
    broadcast_in_dim x3 -> x0, local copies, waits for them, and re-layouts: 2.32 us -> none  [the longest x2 1.61 us: gathered_sum(): spread = jnp.broadcast_to(value[None], (size, *value.shape))]
    ppermute x3 -> x2, starting transfers between devices: 4.75 us -> 5.24 us  [the longest x1 3.17 us: local(): total_far = lax.ppermute(total, 'seq', pairs)]
  transfers between devices with their start and end apart: 11 -> 10, of which waited for: 5 -> 5; matrix products, arithmetic and copies ran while one was open for 1% -> 1% of each run, Pallas kernels for 32% -> 21%
where the time goes in v2:
time: 121 us; the launch traced here: 120 us
  Pallas kernels  38.3 us (32%)
  starting transfers between devices  30.7 us (25%)
  blocking collectives  20.9 us (17%)
  waiting for transfers between devices  16.2 us (13%)
  local copies, waits for them, and re-layouts  12.3 us (10%)
    all_to_all x1, blocking collectives, local(): states = lax.all_to_all(back, 'seq', 0, 0, axis_index_groups=groups)  20.9 us
    unnamed x36, local copies, waits for them, and re-layouts  11.4 us
    all_to_all x1, starting transfers between devices, local(): pieces = lax.all_to_all(spread_sums, 'dp', 0, 0)  8.18 us
    all_to_all x1, waiting for transfers between devices, local(): pieces = lax.all_to_all(spread_sums, 'dp', 0, 0)  7.49 us
    pallas_call x1, Pallas kernels, local(): pl.pallas_call(inner_kernel, out_shape=(shape((blocks, 13, tokens, width)...  7.35 us
    pallas_call x2, Pallas kernels, elements(): pl.pallas_call(functools.partial(element_kernel, mine), out_shape=shape((...  7.17 us
    pallas_call x2, Pallas kernels, sense(): pl.pallas_call(functools.partial(sense_kernel, mine), out_shape=(shape((h...  6.5 us
    all_to_all x1, starting transfers between devices, local(): got = lax.all_to_all(payload, 'seq', 0, 0, axis_index_groups=groups)  6.49 us
  transfers between devices with their start and end apart: 10, of which 5 were waited for; matrix products, arithmetic and copies ran while one was open for 1% of the time, Pallas kernels for 21%

profile of v2, /device:TPU:1, one launch (start us, length us, event | category | flops | bytes accessed | tf_op | source)
XLA Modules:
  0.0 120.1 jit_solution(13154905379051329575)
XLA Ops:
  0.6 0.9 slice_bitcast_fusion
  1.6 4.5 %collective-permute-start = (bf16[3,6144]{1,0:T(4,128)(2,1)S(1)}, bf16[3,6144]{1,0:T(4,128)(2,1)S(1)}, u32[]{:S(2)}, u32[]{:S(2)}) collective-permute-start(bf16[3,6144]{1,0:T(4,128)(2,1)S(1)} %slice_bitcast_fusion), channel_id=1, source_target_pairs={{0,1},{1,2},{2,3},{3,4},{4,5},{5,6},{6,7},{7,8},{8,9},{9,10},{10,1... | collective-permute-start | bytes 110600 | tf_op jit(solution)/shard_map/ppermute | solution.py:488
  6.1 0.1 pad_add_fusion.place_ref
  6.2 0.7 pad_maximum_fusion.gate_ref
  6.9 4.0 %tables.1 = (bf16[16,128,128]{2,1,0:T(8,128)(2,1)S(1)}, f32[2,128,32]{2,1,0:T(8,128)S(1)}, f32[48,128]{1,0:T(8,128)S(1)}) custom-call(f32[48,128]{1,0:T(8,128)S(1)} %pad_maximum_fusion.gate_ref), custom_call_target="tpu_custom_call" | custom-call | flops 4000000000 | bytes 14400000 | tf_op jit(solution)/shard_map/tables/pallas_call | solution.py:490
  10.9 0.0 copy-start.16
  10.9 0.8 copy-done.16
  11.7 3.6 %elements.3 = bf16[8,512,128]{2,1,0:T(8,128)(2,1)S(1)} custom-call(s32[3]{0:T(128)S(1)} %pad_add_fusion.place_ref, bf16[128,6144]{1,0:T(8,128)(2,1)S(1)} %bitcast.14, bf16[128,6144]{1,0:T(8,128)(2,1)S(1)} %bitcast.15, bf16[128,6144]{1,0:T(8,128)(2,1)S(1)} %bitcast.16, bf16[128,2048]{1,0:T(8,128)(2,1)S(1)} %bitcast.23, ...), custom_call_target="tpu_custom_call" | custom-call | flops 3400000000 | bytes 12240000 | tf_op jit(solution)/shard_map/elements/pallas_call | solution.py:510
  15.3 0.1 collective-permute-start.1
  15.4 0.5 collective-permute-start.2
  15.9 3.6 %elements.2.own_ref = bf16[8,512,128]{2,1,0:T(8,128)(2,1)S(1)} custom-call(s32[3]{0:T(128)S(1)} %pad_add_fusion.place_ref, bf16[128,6144]{1,0:T(8,128)(2,1)S(1)} %bitcast.17, bf16[128,6144]{1,0:T(8,128)(2,1)S(1)} %bitcast.18, bf16[128,6144]{1,0:T(8,128)(2,1)S(1)} %bitcast.19, bf16[128,2048]{1,0:T(8,128)(2,1)S(1)} %bitcast.24, ...), custom_call_target="tpu_custom_call" | custom-call | flops 3400000000 | bytes 12240000 | tf_op jit(solution)/shard_map/elements/pallas_call | solution.py:510
  19.5 0.0 collective-permute-done.2.other_coef_ref
  19.6 2.4 %compose.1 = bf16[16,272,128]{2,1,0:T(8,128)(2,1)} custom-call(s32[3]{0:T(128)S(1)} %pad_add_fusion.place_ref, bf16[8,512,128]{2,1,0:T(8,128)(2,1)S(1)} %elements.2.own_ref, bf16[8,512,128]{2,1,0:T(8,128)(2,1)S(1)} %collective-permute-done.1.other_ref, f32[48,128]{1,0:T(8,128)S(1)} %get-tuple-element.39.own_coef_ref, ...), custom_call_target="tpu_custom_call" | custom-call | flops 1200000000 | bytes 4320000 | tf_op jit(solution)/shard_map/compose/pallas_call | solution.py:539
  22.0 6.5 %all-to-all-start = ((bf16[16,272,128]{2,1,0:T(8,128)(2,1)}), bf16[16,272,128]{2,1,0:T(8,128)(2,1)S(1)}, u32[]{:S(2)}, u32[]{:S(2)}) async-start(bf16[16,272,128]{2,1,0:T(8,128)(2,1)} %compose.1), calls=%async_computation | async-start | bytes 2228224 | tf_op jit(solution)/shard_map/all_to_all | solution.py:553
  28.5 0.0 copy-start.2
  28.5 1.4 %copy-done.2 = bf16[1,128,6144]{2,1,0:T(8,128)(2,1)S(1)} copy-done((bf16[1,128,6144]{2,1,0:T(8,128)(2,1)S(1)}, bf16[1,128,6144]{2,1,0:T(8,128)(2,1)}, u32[]{:S(2)}) %copy-start.2) | copy-done | bytes 1572888
  29.9 1.0 copy-done.4
  31.0 1.0 copy-done.17
  32.0 7.4 %inner.1 = (bf16[2,13,128,1024]{3,2,1,0:T(8,128)(2,1)S(1)}, bf16[2,2,128,1024]{3,2,1,0:T(8,128)(2,1)S(1)}) custom-call(bf16[128,6144]{1,0:T(8,128)(2,1)S(1)} %bitcast.20, bf16[128,6144]{1,0:T(8,128)(2,1)S(1)} %bitcast.21, bf16[128,6144]{1,0:T(8,128)(2,1)S(1)} %bitcast.22, bf16[128,2048]{1,0:T(8,128)(2,1)S(1)} %bitcast.25, ...), custom_call_target="tpu_custom_call" | custom-call | flops 8000000000 | bytes 28800000 | tf_op jit(solution)/shard_map/inner/pallas_call | solution.py:558
  39.4 2.8 %copy-done.6 = bf16[2,13,128,1024]{3,2,1,0:T(8,128)(2,1)} copy-done((bf16[2,13,128,1024]{3,2,1,0:T(8,128)(2,1)}, bf16[2,13,128,1024]{3,2,1,0:T(8,128)(2,1)S(1)}, u32[]{:S(2)}) %copy-start.6) | copy-done | bytes 6815768
  42.1 1.0 copy-done.14
  43.1 3.6 %all-to-all-done.got_ref = bf16[16,272,128]{2,1,0:T(8,128)(2,1)S(1)} async-done(((bf16[16,272,128]{2,1,0:T(8,128)(2,1)}), bf16[16,272,128]{2,1,0:T(8,128)(2,1)S(1)}, u32[]{:S(2)}, u32[]{:S(2)}) %all-to-all-start) | async-done | bytes 1114144 | tf_op jit(solution)/shard_map/all_to_all | solution.py:553
  46.7 0.9 scan.1
  47.6 20.9 %all_to_all.20.got_ref = bf16[16,272,128]{2,1,0:T(8,128)(2,1)S(1)} all-to-all(bf16[16,272,128]{2,1,0:T(8,128)(2,1)S(1)} %scan.1), channel_id=1, replica_groups={{0,2,4,6,8,10,12,14,16,18,20,22,24,26,28,30},{1,3,5,7,9,11,13,15,17,19,..., dimensions={0} | all-to-all | bytes 2228224 | tf_op jit(solution)/shard_map/all_to_all | solution.py:598
  68.5 1.3 %spread.1 = (bf16[8,528,128]{2,1,0:T(8,128)(2,1)S(1)}, bf16[8,528,128]{2,1,0:T(8,128)(2,1)S(1)}) custom-call(s32[3]{0:T(128)S(1)} %pad_add_fusion.place_ref, bf16[16,272,128]{2,1,0:T(8,128)(2,1)S(1)} %all_to_all.20.got_ref, bf16[8,512,128]{2,1,0:T(8,128)(2,1)S(1)} %copy-done.9, bf16[8,512,128]{2,1,0:T(8,128)(2,1)S(1)} %collective-permute-done.1.other_ref, ...), custom_call_target="tpu_custom_call" | custom-call | flops 1300000000 | bytes 4680000 | tf_op jit(solution)/shard_map/spread/pallas_call | solution.py:600
  69.8 0.0 copy-start.10
  69.8 2.0 %collective-permute-start.3 = (bf16[8,528,128]{2,1,0:T(8,128)(2,1)S(1)}, bf16[8,528,128]{2,1,0:T(8,128)(2,1)S(1)}, u32[]{:S(2)}, u32[]{:S(2)}) collective-permute-start(bf16[8,528,128]{2,1,0:T(8,128)(2,1)S(1)} %get-tuple-element.49), channel_id=1, source_target_pairs={{0,1},{1,0},{2,3},{3,2},{4,5},{5,4},{6,7},{7,6},{8,9},{9,8},{10,11... | collective-permute-start | bytes 3244040 | tf_op jit(solution)/shard_map/ppermute | solution.py:616
  71.8 3.3 %sense.2 = (bf16[1,24,128,128]{3,2,1,0:T(8,128)(2,1)S(1)}, bf16[2,16,3072]{2,1,0:T(8,128)(2,1)S(1)}, f32[96,128]{1,0:T(8,128)S(1)}) custom-call(s32[3]{0:T(128)S(1)} %pad_add_fusion.place_ref, bf16[2,13,128,1024]{3,2,1,0:T(8,128)(2,1)S(1)} %copy-done.7, bf16[3,6144]{1,0:T(4,128)(2,1)S(1)} %collective-permute-done.halo_ref, f32[4,6144]{1,0:T(4,128)S(1)} %copy-done.5, ...), custom_call_target="tpu_custom_call" | custom-call | flops 3000000000 | bytes 10800000 | tf_op jit(solution)/shard_map/sense/pallas_call | solution.py:624
  75.1 0.9 copy-done.12
  76.0 0.0 collective-permute-done.3.state_ref.other_ref.other_start_ref
  76.0 3.2 %sense.3 = (bf16[1,24,128,128]{3,2,1,0:T(8,128)(2,1)S(1)}, bf16[2,16,3072]{2,1,0:T(8,128)(2,1)S(1)}, f32[96,128]{1,0:T(8,128)S(1)}) custom-call(s32[3]{0:T(128)S(1)} %pad_add_fusion.place_ref, bf16[2,13,128,1024]{3,2,1,0:T(8,128)(2,1)S(1)} %copy-done.7, bf16[3,6144]{1,0:T(4,128)(2,1)S(1)} %collective-permute-done.halo_ref, f32[4,6144]{1,0:T(4,128)S(1)} %copy-done.5, ...), custom_call_target="tpu_custom_call" | custom-call | flops 3000000000 | bytes 10800000 | tf_op jit(solution)/shard_map/sense/pallas_call | solution.py:624
  79.2 0.1 collective-permute-start.4
  79.3 1.2 %collective-permute-done.4.far_ref = f32[96,128]{1,0:T(8,128)S(1)} collective-permute-done((f32[96,128]{1,0:T(8,128)S(1)}, f32[96,128]{1,0:T(8,128)S(1)}, u32[]{:S(2)}, u32[]{:S(2)}) %collective-permute-start.4) | collective-permute-done | bytes 49184 | tf_op jit(solution)/shard_map/ppermute | solution.py:660
  80.5 0.8 pack.1
  81.3 3.6 %all-to-all-start.2 = ((bf16[16,96,128]{2,1,0:T(8,128)(2,1)}), bf16[16,96,128]{2,1,0:T(8,128)(2,1)S(1)}, u32[]{:S(2)}, u32[]{:S(2)}) async-start(bf16[16,96,128]{2,1,0:T(8,128)(2,1)} %pack.1), calls=%async_computation.2 | async-start | bytes 786432 | tf_op jit(solution)/shard_map/all_to_all | solution.py:733
  84.9 2.1 %collective-permute-start.5 = (bf16[2,16,3072]{2,1,0:T(8,128)(2,1)S(1)}, bf16[2,16,3072]{2,1,0:T(8,128)(2,1)S(1)}, u32[]{:S(2)}, u32[]{:S(2)}) collective-permute-start(bf16[2,16,3072]{2,1,0:T(8,128)(2,1)S(1)} %get-tuple-element.59), channel_id=1, source_target_pairs={{1,0},{2,1},{3,2},{4,3},{5,4},{6,5},{7,6},{8,7},{9,8},{10,9},{11,1... | collective-permute-start | bytes 589832 | tf_op jit(solution)/shard_map/ppermute | solution.py:666
  87.0 0.0 copy-start.11
  87.0 1.2 %copy-done.11 = bf16[8,528,128]{2,1,0:T(8,128)(2,1)S(1)} copy-done((bf16[8,528,128]{2,1,0:T(8,128)(2,1)S(1)}, bf16[8,528,128]{2,1,0:T(8,128)(2,1)}, u32[]{:S(2)}) %copy-start.11) | copy-done | bytes 1081368
  88.2 1.2 %copy-done.15 = bf16[2,2,128,1024]{3,2,1,0:T(8,128)(2,1)S(1)} copy-done((bf16[2,2,128,1024]{3,2,1,0:T(8,128)(2,1)S(1)}, bf16[2,2,128,1024]{3,2,1,0:T(8,128)(2,1)}, u32[]{:S(2)}) %copy-start.15) | copy-done | bytes 1048600
  89.4 2.2 %readout.1 = (bf16[128,2048]{1,0:T(8,128)(2,1)}, f32[64,128]{1,0:T(8,128)S(1)}) custom-call(s32[3]{0:T(128)S(1)} %pad_add_fusion.place_ref, bf16[2,2,128,1024]{3,2,1,0:T(8,128)(2,1)S(1)} %copy-done.15, f32[2,128,32]{2,1,0:T(8,128)S(1)} %get-tuple-element.38.column_ref, bf16[8,528,128]{2,1,0:T(8,128)(2,1)S(1)} %copy-done.11, ...), custom_call_target="tpu_custom_call" | custom-call | flops 3000000000 | bytes 10800000 | tf_op jit(solution)/shard_map/readout/pallas_call | solution.py:675
  91.6 3.1 %all-to-all-done.2.pieces_ref = bf16[16,96,128]{2,1,0:T(8,128)(2,1)S(1)} async-done(((bf16[16,96,128]{2,1,0:T(8,128)(2,1)}), bf16[16,96,128]{2,1,0:T(8,128)(2,1)S(1)}, u32[]{:S(2)}, u32[]{:S(2)}) %all-to-all-start.2) | async-done | bytes 393248 | tf_op jit(solution)/shard_map/all_to_all | solution.py:733
  94.7 0.8 fold.1
  95.5 8.2 %all-to-all-start.3 = ((bf16[8,160,128]{2,1,0:T(8,128)(2,1)}), bf16[8,160,128]{2,1,0:T(8,128)(2,1)S(1)}, u32[]{:S(2)}, u32[]{:S(2)}) async-start(bf16[8,160,128]{2,1,0:T(8,128)(2,1)} %fold.1), calls=%async_computation.3 | async-start | bytes 655360 | tf_op jit(solution)/shard_map/all_to_all | solution.py:744
  103.6 3.7 %unroll.1 = bf16[128,6144]{1,0:T(8,128)(2,1)} custom-call(s32[3]{0:T(128)S(1)} %pad_add_fusion.place_ref, bf16[1,24,128,128]{3,2,1,0:T(8,128)(2,1)S(1)} %copy-done.13, bf16[1,24,128,128]{3,2,1,0:T(8,128)(2,1)S(1)} %get-tuple-element.62.conv_other_ref, f32[4,6144]{1,0:T(4,128)S(1)} %copy-done.5, ...), custom_call_target="tpu_custom_call" | custom-call | flops 4000000000 | bytes 14400000 | tf_op jit(solution)/shard_map/unroll/pallas_call | solution.py:700
  107.3 7.5 %all-to-all-done.3.pieces_ref = bf16[8,160,128]{2,1,0:T(8,128)(2,1)S(1)} async-done(((bf16[8,160,128]{2,1,0:T(8,128)(2,1)}), bf16[8,160,128]{2,1,0:T(8,128)(2,1)S(1)}, u32[]{:S(2)}, u32[]{:S(2)}) %all-to-all-start.3) | async-done | bytes 327712 | tf_op jit(solution)/shard_map/all_to_all | solution.py:744
  114.8 3.2 %collective-permute-start.6 = (f32[160,128]{1,0:T(8,128)S(1)}, f32[160,128]{1,0:T(8,128)S(1)}, u32[]{:S(2)}, u32[]{:S(2)}) collective-permute-start(f32[160,128]{1,0:T(8,128)S(1)} %total.1.own_ref), channel_id=1, source_target_pairs={{0,1},{1,0},{2,3},{3,2},{4,5},{5,4},{6,7},{7,6},{8,9},{9,8},{10,11... | collective-permute-start | bytes 245768 | tf_op jit(solution)/shard_map/ppermute | solution.py:754
  118.0 0.9 collective-permute-done.6.other_ref
  118.9 1.2 %assemble.1 = (f32[4,6144]{1,0:T(4,128)}, f32[16,4,128]{2,1,0:T(4,128)}) custom-call(s32[3]{0:T(128)S(1)} %pad_add_fusion.place_ref, f32[160,128]{1,0:T(8,128)S(1)} %total.1.own_ref, f32[160,128]{1,0:T(8,128)S(1)} %collective-permute-done.6.other_ref), custom_call_target="tpu_custom_call" | custom-call | flops 1000000000 | bytes 3600000 | tf_op jit(solution)/shard_map/assemble/pallas_call | solution.py:755
  (27 shorter events, 0.1 us)
Async XLA Ops:
  1.6 10.2 %collective-permute-start = (bf16[3,6144]{1,0:T(4,128)(2,1)S(1)}, bf16[3,6144]{1,0:T(4,128)(2,1)S(1)}, u32[]{:S(2)}, u32[]{:S(2)}) collective-permute-start(bf16[3,6144]{1,0:T(4,128)(2,1)S(1)} %slice_bitcast_fusion), channel_id=1, source_target_pairs={{0,1},{1,2},{2,3},{3,4},{4,5},{5,6},{6,7},{7,8},{8,9},{9,10},{10,1... | collective-permute-start | bytes 110600 | tf_op jit(solution)/shard_map/ppermute | solution.py:488
  6.9 4.8 %copy-start.1 = (bf16[1,128,6144]{2,1,0:T(8,128)(2,1)S(1)}, bf16[1,128,6144]{2,1,0:T(8,128)(2,1)}, u32[]{:S(2)}) copy-start(bf16[1,128,6144]{2,1,0:T(8,128)(2,1)} %param.7) | copy-start | bytes 4718596
  6.9 4.8 %copy-start.3 = (bf16[1,128,2048]{2,1,0:T(8,128)(2,1)S(1)}, bf16[1,128,2048]{2,1,0:T(8,128)(2,1)}, u32[]{:S(2)}) copy-start(bf16[1,128,2048]{2,1,0:T(8,128)(2,1)} %param.13) | copy-start | bytes 1572868
  6.9 4.8 %copy-start.5 = (f32[4,6144]{1,0:T(4,128)S(1)}, f32[4,6144]{1,0:T(4,128)}, u32[]{:S(2)}) copy-start(f32[4,6144]{1,0:T(4,128)} %weight_ref.11) | copy-start | bytes 294916
  10.9 0.8 copy-start.16
  15.3 4.2 %collective-permute-start.1 = (bf16[8,512,128]{2,1,0:T(8,128)(2,1)S(1)}, bf16[8,512,128]{2,1,0:T(8,128)(2,1)S(1)}, u32[]{:S(2)}, u32[]{:S(2)}) collective-permute-start(bf16[8,512,128]{2,1,0:T(8,128)(2,1)S(1)} %elements.3), channel_id=1, source_target_pairs={{0,1},{1,0},{2,3},{3,2},{4,5},{5,4},{6,7},{7,6},{8,9},{9,8},{10,11... | collective-permute-start | bytes 3145736 | tf_op jit(solution)/shard_map/ppermute | solution.py:534
  15.4 4.1 %collective-permute-start.2 = (f32[48,128]{1,0:T(8,128)S(1)}, f32[48,128]{1,0:T(8,128)S(1)}, u32[]{:S(2)}, u32[]{:S(2)}) collective-permute-start(f32[48,128]{1,0:T(8,128)S(1)} %get-tuple-element.39.own_coef_ref), channel_id=1, source_target_pairs={{0,1},{1,0},{2,3},{3,2},{4,5},{5,4},{6,7},{7,6},{8,9},{9,8},{10,11... | collective-permute-start | bytes 73736 | tf_op jit(solution)/shard_map/ppermute | solution.py:501
  19.5 2.5 %copy-start.8 = (bf16[8,512,128]{2,1,0:T(8,128)(2,1)}, bf16[8,512,128]{2,1,0:T(8,128)(2,1)S(1)}, u32[]{:S(2)}) copy-start(bf16[8,512,128]{2,1,0:T(8,128)(2,1)S(1)} %elements.2.own_ref) | copy-start | bytes 3145732
  22.0 24.7 %all-to-all-start = ((bf16[16,272,128]{2,1,0:T(8,128)(2,1)}), bf16[16,272,128]{2,1,0:T(8,128)(2,1)S(1)}, u32[]{:S(2)}, u32[]{:S(2)}) async-start(bf16[16,272,128]{2,1,0:T(8,128)(2,1)} %compose.1), calls=%async_computation | async-start | bytes 2228224 | tf_op jit(solution)/shard_map/all_to_all | solution.py:553
  28.5 1.4 %copy-start.2 = (bf16[1,128,6144]{2,1,0:T(8,128)(2,1)S(1)}, bf16[1,128,6144]{2,1,0:T(8,128)(2,1)}, u32[]{:S(2)}) copy-start(bf16[1,128,6144]{2,1,0:T(8,128)(2,1)} %param.7) | copy-start | bytes 4718596
  29.9 1.0 copy-start.4
  30.9 1.0 copy-start.17
  32.0 14.7 %copy-start = (f32[16,128,128]{2,1,0:T(8,128)S(1)}, f32[16,128,128]{2,1,0:T(8,128)}, u32[]{:S(2)}) copy-start(f32[16,128,128]{2,1,0:T(8,128)} %param.9) | copy-start | bytes 3145732
  39.4 2.8 %copy-start.6 = (bf16[2,13,128,1024]{3,2,1,0:T(8,128)(2,1)}, bf16[2,13,128,1024]{3,2,1,0:T(8,128)(2,1)S(1)}, u32[]{:S(2)}) copy-start(bf16[2,13,128,1024]{3,2,1,0:T(8,128)(2,1)S(1)} %get-tuple-element.45.in_ref) | copy-start | bytes 20447236
  42.1 1.0 copy-start.14
  46.7 21.7 %copy-start.9 = (bf16[8,512,128]{2,1,0:T(8,128)(2,1)S(1)}, bf16[8,512,128]{2,1,0:T(8,128)(2,1)}, u32[]{:S(2)}) copy-start(bf16[8,512,128]{2,1,0:T(8,128)(2,1)} %copy-done.8) | copy-start | bytes 3145732
  47.6 24.2 %copy-start.7 = (bf16[2,13,128,1024]{3,2,1,0:T(8,128)(2,1)S(1)}, bf16[2,13,128,1024]{3,2,1,0:T(8,128)(2,1)}, u32[]{:S(2)}) copy-start(bf16[2,13,128,1024]{3,2,1,0:T(8,128)(2,1)} %copy-done.6) | copy-start | bytes 20447236
  69.8 5.3 %copy-start.10 = (bf16[8,528,128]{2,1,0:T(8,128)(2,1)}, bf16[8,528,128]{2,1,0:T(8,128)(2,1)S(1)}, u32[]{:S(2)}) copy-start(bf16[8,528,128]{2,1,0:T(8,128)(2,1)S(1)} %get-tuple-element.47.state_ref.own_ref.own_start_ref) | copy-start | bytes 3244036
  69.8 6.2 %collective-permute-start.3 = (bf16[8,528,128]{2,1,0:T(8,128)(2,1)S(1)}, bf16[8,528,128]{2,1,0:T(8,128)(2,1)S(1)}, u32[]{:S(2)}, u32[]{:S(2)}) collective-permute-start(bf16[8,528,128]{2,1,0:T(8,128)(2,1)S(1)} %get-tuple-element.49), channel_id=1, source_target_pairs={{0,1},{1,0},{2,3},{3,2},{4,5},{5,4},{6,7},{7,6},{8,9},{9,8},{10,11... | collective-permute-start | bytes 3244040 | tf_op jit(solution)/shard_map/ppermute | solution.py:616
  75.1 0.9 copy-start.12
  79.2 1.3 %collective-permute-start.4 = (f32[96,128]{1,0:T(8,128)S(1)}, f32[96,128]{1,0:T(8,128)S(1)}, u32[]{:S(2)}, u32[]{:S(2)}) collective-permute-start(f32[96,128]{1,0:T(8,128)S(1)} %get-tuple-element.51), channel_id=1, source_target_pairs={{0,1},{1,0},{2,3},{3,2},{4,5},{5,4},{6,7},{7,6},{8,9},{9,8},{10,11... | collective-permute-start | bytes 147464 | tf_op jit(solution)/shard_map/ppermute | solution.py:660
  81.3 13.3 %all-to-all-start.2 = ((bf16[16,96,128]{2,1,0:T(8,128)(2,1)}), bf16[16,96,128]{2,1,0:T(8,128)(2,1)S(1)}, u32[]{:S(2)}, u32[]{:S(2)}) async-start(bf16[16,96,128]{2,1,0:T(8,128)(2,1)} %pack.1), calls=%async_computation.2 | async-start | bytes 786432 | tf_op jit(solution)/shard_map/all_to_all | solution.py:733
  84.9 10.6 %collective-permute-start.5 = (bf16[2,16,3072]{2,1,0:T(8,128)(2,1)S(1)}, bf16[2,16,3072]{2,1,0:T(8,128)(2,1)S(1)}, u32[]{:S(2)}, u32[]{:S(2)}) collective-permute-start(bf16[2,16,3072]{2,1,0:T(8,128)(2,1)S(1)} %get-tuple-element.59), channel_id=1, source_target_pairs={{1,0},{2,1},{3,2},{4,3},{5,4},{6,5},{7,6},{8,7},{9,8},{10,9},{11,1... | collective-permute-start | bytes 589832 | tf_op jit(solution)/shard_map/ppermute | solution.py:666
  87.0 1.2 %copy-start.11 = (bf16[8,528,128]{2,1,0:T(8,128)(2,1)S(1)}, bf16[8,528,128]{2,1,0:T(8,128)(2,1)}, u32[]{:S(2)}) copy-start(bf16[8,528,128]{2,1,0:T(8,128)(2,1)} %copy-done.10) | copy-start | bytes 3244036
  88.2 1.2 %copy-start.15 = (bf16[2,2,128,1024]{3,2,1,0:T(8,128)(2,1)S(1)}, bf16[2,2,128,1024]{3,2,1,0:T(8,128)(2,1)}, u32[]{:S(2)}) copy-start(bf16[2,2,128,1024]{3,2,1,0:T(8,128)(2,1)} %copy-done.14) | copy-start | bytes 3145732
  94.7 9.0 %copy-start.13 = (bf16[1,24,128,128]{3,2,1,0:T(8,128)(2,1)S(1)}, bf16[1,24,128,128]{3,2,1,0:T(8,128)(2,1)}, u32[]{:S(2)}) copy-start(bf16[1,24,128,128]{3,2,1,0:T(8,128)(2,1)} %copy-done.12) | copy-start | bytes 2359300
  95.5 19.3 %all-to-all-start.3 = ((bf16[8,160,128]{2,1,0:T(8,128)(2,1)}), bf16[8,160,128]{2,1,0:T(8,128)(2,1)S(1)}, u32[]{:S(2)}, u32[]{:S(2)}) async-start(bf16[8,160,128]{2,1,0:T(8,128)(2,1)} %fold.1), calls=%async_computation.3 | async-start | bytes 655360 | tf_op jit(solution)/shard_map/all_to_all | solution.py:744
  114.8 4.1 %collective-permute-start.6 = (f32[160,128]{1,0:T(8,128)S(1)}, f32[160,128]{1,0:T(8,128)S(1)}, u32[]{:S(2)}, u32[]{:S(2)}) collective-permute-start(f32[160,128]{1,0:T(8,128)S(1)} %total.1.own_ref), channel_id=1, source_target_pairs={{0,1},{1,0},{2,3},{3,2},{4,5},{5,4},{6,7},{7,6},{8,9},{9,8},{10,11... | collective-permute-start | bytes 245768 | tf_op jit(solution)/shard_map/ppermute | solution.py:754

commit v3 on v2

--- a/solution.py
+++ b/solution.py
@@ -27,55 +27,73 @@
     return jnp.sum(jnp.where(eye, row, 0.0), axis=1, keepdims=True)
 
 
-def tables_kernel(gate_ref, coupling_ref, column_ref, coef_ref):
+def shifted(value, by, fill):
+    tokens = value.shape[1]
+    lane = lax.broadcasted_iota(jnp.int32, value.shape, 1)
+    moved = pltpu.roll(value, by % tokens, axis=1)
+    return jnp.where(lane >= by if by > 0 else lane < tokens + by, moved, fill)
+
+
+def recurrence(factor, added, step):
+    by = step
+    while abs(by) < factor.shape[1]:
+        added = added + factor * shifted(added, by, 0.0)
+        factor = factor * shifted(factor, by, 1.0)
+        by *= 2
+    return added
+
+
+def tables_kernel(gate_ref, column_ref, coef_ref, cum_ref):
+    heads, tokens = gate_ref.shape[0] // 3, gate_ref.shape[1]
+    rows = lax.broadcasted_iota(jnp.int32, (tokens, tokens), 0)
+    lanes = lax.broadcasted_iota(jnp.int32, (tokens, tokens), 1)
+    cum = lax.dot_general(
+        gate_ref[0 : 2 * heads],
+        (rows <= lanes).astype(F32),
+        (((1,), (0,)), ((), ())),
+        precision=lax.Precision.HIGHEST,
+        preferred_element_type=F32,
+    )
+    cum_ref[...] = cum
+    last = tokens - 1
+    cum_forget, cum_moment = cum[:heads], cum[heads:]
+    rate = gate_ref[2 * heads :]
+    forget = jnp.exp(cum_forget)
+    moment = jnp.exp(cum_moment)
+    carry = recurrence(jnp.exp(gate_ref[0:heads]), moment, 1)
+    lane = lax.broadcasted_iota(jnp.int32, (heads, tokens), 1)
+    later = jnp.where(lane < last, pltpu.roll(jnp.exp(gate_ref[heads : 2 * heads]), last, axis=1), 0.0)
+    memory = recurrence(later, jnp.exp(jnp.minimum(cum_forget[:, last:] - cum_forget, 0.0)), -1)
+    memory = memory * rate
+    tail = rate * jnp.exp(jnp.minimum(cum_moment[:, last:] - cum_moment, 0.0))
+    for group in range(heads // SIDES):
+        at = slice(group * SIDES, (group + 1) * SIDES)
+        column_ref[group] = jnp.transpose(
+            jnp.concatenate([memory[at], tail[at], forget[at], carry[at]], axis=0)
+        )
+    for which, value in enumerate((forget, carry, moment)):
+        coef_ref[which * heads : (which + 1) * heads] = jnp.broadcast_to(value[:, last:], (heads, tokens))
+
+
+def couple_kernel(gate_ref, cum_ref, coupling_ref):
     heads, tokens = gate_ref.shape[0] // 3, gate_ref.shape[1]
     rows = lax.broadcasted_iota(jnp.int32, (tokens, tokens), 0)
     lanes = lax.broadcasted_iota(jnp.int32, (tokens, tokens), 1)
     eye = rows == lanes
     causal = rows >= lanes
-    upper = (rows <= lanes).astype(F32)
-    exact = functools.partial(
-        lax.dot_general,
-        dimension_numbers=(((1,), (0,)), ((), ())),
-        precision=lax.Precision.HIGHEST,
-        preferred_element_type=F32,
-    )
-    cum_forget = exact(gate_ref[0:heads], upper)
-    cum_moment = exact(gate_ref[heads : 2 * heads], upper)
-    narrow = lax.broadcasted_iota(jnp.int32, (tokens, 4 * SIDES), 1)
-    last = tokens - 1
     for h in range(heads):
-        forget_row = cum_forget[h : h + 1, :]
-        moment_row = cum_moment[h : h + 1, :]
-        rate_row = gate_ref[2 * heads + h : 2 * heads + h + 1, :]
-        forget_col = to_column(forget_row, eye)
-        moment_col = to_column(moment_row, eye)
-        rate_col = to_column(rate_row, eye)
-        forget_map = jnp.where(causal, jnp.exp(jnp.minimum(forget_col - forget_row, 0.0)), 0.0)
-        moment_map = jnp.where(causal, jnp.exp(jnp.minimum(moment_col - moment_row, 0.0)), 0.0)
-        coupling = dot(forget_map.astype(BF), moment_map.astype(BF), (1, 0))
-        carry = coupling[:, 0:1] * jnp.exp(moment_row[:, 0:1])
-        rated = coupling * rate_row
+        maps = []
+        for at in (h, heads + h):
+            row = cum_ref[at : at + 1, :]
+            decay = jnp.exp(jnp.minimum(to_column(row, eye) - row, 0.0))
+            maps.append(jnp.where(causal, decay, 0.0).astype(BF))
+        rated = dot(maps[0], maps[1], (1, 0)) * gate_ref[2 * heads + h : 2 * heads + h + 1, :]
         coupling_ref[h] = rated.astype(BF)
-        memory_col = to_column(rated[last : last + 1, :], eye)
-        tail_col = rate_col * jnp.exp(jnp.minimum(moment_row[:, last:] - moment_col, 0.0))
-        quad = jnp.where(
-            narrow % 4 == 0,
-            memory_col,
-            jnp.where(narrow % 4 == 1, tail_col, jnp.where(narrow % 4 == 2, jnp.exp(forget_col), carry)),
-        )
-        packed = quad if h % SIDES == 0 else jnp.where(narrow // 4 == h % SIDES, quad, packed)
-        if h % SIDES == SIDES - 1:
-            column_ref[h // SIDES] = packed
-        spread = functools.partial(jnp.broadcast_to, shape=(1, tokens))
-        coef_ref[h : h + 1, :] = spread(jnp.exp(forget_row[:, last:]))
-        coef_ref[heads + h : heads + h + 1, :] = spread(carry[last : last + 1, :])
-        coef_ref[2 * heads + h : 2 * heads + h + 1, :] = spread(jnp.exp(moment_row[:, last:]))
 
 
 def extend(ext_ref, slot, halo, own):
     cols = slice(slot * DK, (slot + 1) * DK)
-    ext_ref[5:8, cols] = halo.astype(F32)
+    ext_ref[0:8, cols] = halo.astype(F32)
     ext_ref[8 : 8 + own.shape[0], cols] = own.astype(F32)
 
 
@@ -87,42 +105,38 @@
     return total
 
 
-def first_block(mine, place_ref, blocks):
-    return (place_ref[0] if mine else 1 - place_ref[0]) * (blocks // 2)
-
-
 def element_kernel(
-    mine, place_ref, q_ref, k_ref, v_ref, u_ref, halo_ref, weight_ref, column_ref, element_ref, ext_ref
+    mine, place_ref, rows_ref, u_ref, halo_ref, weight_ref, column_ref, element_ref, ext_ref
 ):
-    tokens, width = q_ref.shape
-    section = halo_ref.shape[1] // 3
-    block = first_block(mine, place_ref, section // width) + pl.program_id(0)
-    for side in range(width // DK):
-        cols = slice(side * DK, (side + 1) * DK)
+    tokens = rows_ref.shape[0]
+    section = rows_ref.shape[1] // 3
+    half = place_ref[0] if mine else 1 - place_ref[0]
+    for side in range(HALF):
         made = []
-        for part, ref in enumerate((q_ref, k_ref, v_ref)):
-            at = pl.ds(pl.multiple_of(part * section + block * width + side * DK, DK), DK)
+        for part in range(3):
+            at = pl.ds(pl.multiple_of(part * section + half * (HALF * DK) + side * DK, DK), DK)
             slot = side * 3 + part
-            extend(ext_ref, slot, halo_ref[:, at], ref[:, cols])
+            extend(ext_ref, slot, halo_ref[:, at], rows_ref[:, at])
             conv = convolve(ext_ref, slot, weight_ref[:, at], tokens)
             active = conv * (0.5 + 0.5 * jnp.tanh(0.5 * conv))
             if part < 2:
                 active = active * lax.rsqrt(
                     jnp.sum(active * active, axis=1, keepdims=True) + 1e-06
                 )
-            made.append(active.astype(BF))
+            made.append(active)
         query, key, value = made
-        column = column_ref[0, :, 4 * side : 4 * side + 4]
-        query = query.astype(F32)
-        key = key.astype(F32)
+        column = picker(column_ref, half, side)
+        query = query.astype(BF).astype(F32)
+        key = key.astype(BF).astype(F32)
         left = jnp.concatenate(
-            [(key * column[:, 0:1]).astype(BF), (key * column[:, 1:2]).astype(BF)], axis=1
+            [(key * column(0)).astype(BF), (key * column(1)).astype(BF)], axis=1
         )
-        element_ref[side, 0 : 2 * DK] = dot(left, value, (0, 0)).astype(BF)
+        element_ref[side, 0 : 2 * DK] = dot(left, value.astype(BF), (0, 0)).astype(BF)
         left = jnp.concatenate(
-            [(query * column[:, 2:3]).astype(BF), (query * column[:, 3:4]).astype(BF)], axis=1
+            [(query * column(2)).astype(BF), (query * column(3)).astype(BF)], axis=1
         )
-        element_ref[side, 2 * DK : 4 * DK] = dot(left, u_ref[:, cols], (0, 0)).astype(BF)
+        upstream = u_ref[:, pl.ds(pl.multiple_of(half * (HALF * DK) + side * DK, DK), DK)]
+        element_ref[side, 2 * DK : 4 * DK] = dot(left, upstream, (0, 0)).astype(BF)
 
 
 def compose_kernel(place_ref, own_ref, other_ref, own_coef_ref, other_coef_ref, out_ref):
@@ -187,7 +201,7 @@
         )
 
     scalars = [coefs(c) for c in range(count)]
-    memory = start_ref[...]
+    memory = start_ref[pl.ds(pl.multiple_of(place_ref[2] * 64, 64), 64), :]
     state = jnp.zeros_like(memory)
     for c in range(count):
         out_ref[c, 0:64] = memory.astype(BF)
@@ -309,6 +323,11 @@
         read_ref[0, 1, :, cols] = dot(scores, value, (1, 0)).astype(BF)
 
 
+def picker(column_ref, group, side):
+    values = column_ref[group]
+    return lambda which: values[:, which * SIDES + side : which * SIDES + side + 1]
+
+
 def along_rows(left, pair):
     return dot(left, pair[:DK], (1, 0)), dot(left, pair[DK:], (1, 0))
 
@@ -321,29 +340,28 @@
 def sense_kernel(
     mine, place_ref, in_ref, halo_ref, weight_ref, column_ref, state_ref, *refs
 ):
-    conv_ref, rim_ref, tap_ref, pad_ref, ext_ref = refs[-5:]
-    step = pl.program_id(0)
+    conv_ref, rim_ref, tap_ref, start_ref, pad_ref, ext_ref = refs[-6:]
     tokens = in_ref.shape[2]
     width = in_ref.shape[3]
     section = halo_ref.shape[1] // 3
-    block = first_block(mine, place_ref, section // width) + step
-    if len(refs) > 5:
+    block = place_ref[0] if mine else 1 - place_ref[0]
+    if len(refs) > 6:
         rim_ref[0] = refs[0][1]
     else:
         rim_ref[0] = jnp.zeros(rim_ref.shape[1:], BF)
 
-    @pl.when(pl.program_id(0) == 0)
-    def _():
-        pad_ref[0:8] = jnp.zeros((8, pad_ref.shape[1]), F32)
-        pad_ref[8 + tokens :] = jnp.zeros((8, pad_ref.shape[1]), F32)
-        ext_ref[0:8] = jnp.zeros((8, ext_ref.shape[1]), F32)
+    pad_ref[0:8] = jnp.zeros((8, pad_ref.shape[1]), F32)
+    pad_ref[8 + tokens :] = jnp.zeros((8, pad_ref.shape[1]), F32)
 
     for side in range(width // DK):
         cols = slice(side * DK, (side + 1) * DK)
-        query, key, value, upstream = (in_ref[0, i, :, cols] for i in range(4))
-        column = column_ref[0, :, 4 * side : 4 * side + 4]
-        memory_col, tail_col, forget_col, carry_col = (column[:, i : i + 1] for i in range(4))
-        forward, adjoint = state_ref[side, : 2 * DK], state_ref[side, 2 * DK :]
+        query, key, value, upstream = (in_ref[block, i, :, cols] for i in range(4))
+        column = picker(column_ref, block, side)
+        memory_col, tail_col, forget_col, carry_col = (column(i) for i in range(4))
+        start = state_ref[side, 4 * DK :].astype(F32)
+        start = start[0:8] + start[8:16]
+        start_ref[4 * side : 4 * side + 4] = jnp.where(place_ref[0] == 0, start[0:4], start[4:8])
+        forward, adjoint = state_ref[side, : 2 * DK], state_ref[side, 2 * DK : 4 * DK]
         grads = []
         a, b = along_lanes(upstream, forward)
         grads.append(forget_col * a + carry_col * b)
@@ -356,21 +374,21 @@
             if part < 2:
                 unit = (query, key)[part].astype(F32)
                 grad = grad - unit * jnp.sum(unit * grad, axis=1, keepdims=True)
-            grad = grad * in_ref[0, 4 + part, :, cols].astype(F32)
-            grad = grad + in_ref[0, 7 + part, :, cols].astype(F32)
+            grad = grad * in_ref[block, 4 + part, :, cols].astype(F32)
+            grad = grad + in_ref[block, 7 + part, :, cols].astype(F32)
             slot = side * 3 + part
             conv_ref[0, slot] = grad.astype(BF)
             there = slice(slot * DK, (slot + 1) * DK)
             pad_ref[8 : 8 + tokens, there] = grad
             at = pl.ds(pl.multiple_of(part * section + block * width + side * DK, DK), DK)
-            extend(ext_ref, slot, halo_ref[:, at], in_ref[0, 10 + part, :, cols])
+            extend(ext_ref, slot, halo_ref[:, at], in_ref[block, 10 + part, :, cols])
             rows = ext_ref[:, there]
             weights = weight_ref[:, at]
             rim = None
             for tap in range(4):
                 moved = pad_ref[3 - tap : 3 - tap + 8 + tokens, there]
-                slot_row = 12 * (SIDES * pl.program_id(0) + side) + 4 * part + tap
-                tap_ref[pl.ds(slot_row, 1), :] = jnp.sum(moved * rows, axis=0, keepdims=True)
+                slot_row = 12 * side + 4 * part + tap
+                tap_ref[slot_row : slot_row + 1, :] = jnp.sum(moved * rows, axis=0, keepdims=True)
                 lead = moved[0:8] * weights[tap : tap + 1]
                 rim = lead if rim is None else rim + lead
             rim_ref[1, :, part * width + side * DK : part * width + (side + 1) * DK] = jnp.concatenate(
@@ -379,21 +397,17 @@
 
 
 def readout_kernel(
-    place_ref, read_ref, column_ref, own_ref, other_ref, own_start_ref, other_start_ref,
-    output_ref, start_ref,
+    place_ref, read_ref, column_ref, own_ref, other_ref, output_ref
 ):
     width = read_ref.shape[3]
     owned = (pl.program_id(0) // (pl.num_programs(0) // 2)) == place_ref[0]
     for side in range(width // DK):
         cols = slice(side * DK, (side + 1) * DK)
-        column = column_ref[0, :, 4 * side : 4 * side + 4]
+        column = picker(column_ref, 0, side)
         states = jnp.where(owned, own_ref[side], other_ref[side])
         from_memory, from_moment = along_rows(read_ref[0, 0, :, cols], states)
-        readout = read_ref[0, 1, :, cols].astype(F32) + column[:, 2:3] * from_memory + column[:, 3:4] * from_moment
+        readout = read_ref[0, 1, :, cols].astype(F32) + column(2) * from_memory + column(3) * from_moment
         output_ref[:, cols] = readout.astype(BF)
-        rows = jnp.where(owned, own_start_ref[side], other_start_ref[side]).astype(F32)
-        rows = rows[0:8] + rows[8:16]
-        start_ref[4 * side : 4 * side + 4] = jnp.where(place_ref[0] == 0, rows[0:4], rows[4:8])
 
 
 def unroll_kernel(
@@ -433,11 +447,15 @@
         out_ref[i] = value
 
 
-def fold_kernel(pieces_ref, start_ref, out_ref):
+def fold_kernel(place_ref, pieces_ref, own_ref, other_ref, out_ref):
     total = pieces_ref[0].astype(F32)
     for i in range(1, pieces_ref.shape[0]):
         total = total + pieces_ref[i].astype(F32)
-    value = jnp.concatenate([total, start_ref[...]], axis=0).astype(BF)
+    own, other = own_ref[...], other_ref[...]
+    first_core = place_ref[0] == 0
+    value = jnp.concatenate(
+        [total, jnp.where(first_core, own, other), jnp.where(first_core, other, own)], axis=0
+    ).astype(BF)
     for i in range(out_ref.shape[0]):
         out_ref[i] = value
 
@@ -462,6 +480,9 @@
             out_ref[:, at : at + DK] = jnp.where(
                 place_ref[0] == h // HALF, own_ref[rows], other_ref[rows]
             )
+
+
+RESIDENT = pl.BlockSpec(memory_space=pltpu.VMEM)
 
 
 def whole(*shape):
@@ -485,72 +506,64 @@
     pairs = [(i, i ^ 1) for i in range(count)]
     groups = [[2 * c + k for c in range(count // 2)] for k in range(2)]
 
-    rim = lax.ppermute(rows[tokens - 3 :], "seq", [(i, i + 1) for i in range(count - 1)])
+    rim = lax.ppermute(rows[tokens - 8 :], "seq", [(i, i + 1) for i in range(count - 1)])
     shape = jax.ShapeDtypeStruct
-    coupling, columns, coefs = pl.pallas_call(
+    columns, coefs, cums = pl.pallas_call(
         tables_kernel,
         out_shape=(
-            shape((heads, tokens, tokens), BF),
             shape((heads // SIDES, tokens, 4 * SIDES), F32),
             shape((3 * heads, DK), F32),
-        ),
-        compiler_params=PARAMS,
+            shape((2 * heads, tokens), F32),
+        ),
+        compiler_params=SHARED,
         name="tables",
-        cost_estimate=pl.CostEstimate(flops=4000000000, transcendentals=0, bytes_accessed=14400000),
+        cost_estimate=pl.CostEstimate(flops=2000000000, transcendentals=0, bytes_accessed=7200000),
     )(gates)
     other_coefs = lax.ppermute(coefs, "seq", pairs)
 
     def elements(mine):
-        def first(b):
-            return first_block(mine, b, blocks)
-
-        def block_of(part):
-            return pl.BlockSpec((tokens, width), lambda i, b: (0, part * blocks + first(b) + i))
-
         return pl.pallas_call(
             functools.partial(element_kernel, mine),
-            out_shape=shape((heads // 2, 4 * DK, DK), BF),
+            out_shape=shape((HALF, 4 * DK, DK), BF),
             grid_spec=pltpu.PrefetchScalarGridSpec(
                 num_scalar_prefetch=1,
-                grid=(blocks // 2,),
-                in_specs=[
-                    block_of(0),
-                    block_of(1),
-                    block_of(2),
-                    block_of(0),
-                    whole(3, channels),
-                    whole(4, channels),
-                    pl.BlockSpec((1, tokens, 4 * SIDES), lambda i, b: (first(b) + i, 0, 0)),
-                ],
-                out_specs=pl.BlockSpec((SIDES, 4 * DK, DK), lambda i, b: (i, 0, 0)),
-                scratch_shapes=[pltpu.VMEM((tokens + 8, 3 * SIDES * DK), F32)],
+                grid=(1,),
+                in_specs=[RESIDENT] * 5,
+                out_specs=RESIDENT,
+                scratch_shapes=[pltpu.VMEM((tokens + 8, 3 * HALF * DK), F32)],
             ),
-            compiler_params=PARAMS,
+            compiler_params=SHARED,
             name="elements",
             cost_estimate=pl.CostEstimate(flops=3400000000, transcendentals=0, bytes_accessed=12240000),
-        )(place, rows, rows, rows, upstream, rim, conv_weight, columns)
+        )(place, rows, upstream, rim, conv_weight, columns)
 
     sent = elements(False)
     other = lax.ppermute(sent, "seq", pairs)
     own = elements(True)
 
-    by_two = pl.BlockSpec((2, 4 * DK, DK), lambda i, b: (i, 0, 0))
-    pieces = pl.BlockSpec((4, PIECE, DK), lambda i, b: (i, 0, 0))
     payload = pl.pallas_call(
         compose_kernel,
         out_shape=shape((CHIPS, PIECE, DK), BF),
         grid_spec=pltpu.PrefetchScalarGridSpec(
             num_scalar_prefetch=1,
-            grid=(HALF // 2,),
-            in_specs=[by_two, by_two, whole(3 * heads, DK), whole(3 * heads, DK)],
-            out_specs=pieces,
+            grid=(1,),
+            in_specs=[RESIDENT] * 4,
+            out_specs=RESIDENT,
         ),
         compiler_params=SHARED,
         name="compose",
         cost_estimate=pl.CostEstimate(flops=1200000000, transcendentals=0, bytes_accessed=4320000),
     )(place, own, other, coefs, other_coefs)
-    payload, coupling = lax.optimization_barrier((payload, coupling))
+    payload, cums = lax.optimization_barrier((payload, cums))
     got = lax.all_to_all(payload, "seq", 0, 0, axis_index_groups=groups)
+
+    coupling = pl.pallas_call(
+        couple_kernel,
+        out_shape=shape((heads, tokens, tokens), BF),
+        compiler_params=SHARED,
+        name="couple",
+        cost_estimate=pl.CostEstimate(flops=3500000000, transcendentals=0, bytes_accessed=12600000),
+    )(gates, cums)
 
     def block_at(part):
         return pl.BlockSpec((tokens, width), lambda i: (0, part * blocks + i))
@@ -567,7 +580,7 @@
             block_at(1),
             block_at(2),
             block_at(0),
-            whole(3, channels),
+            whole(8, channels),
             whole(4, channels),
             pl.BlockSpec((SIDES, tokens, tokens), lambda i: (i, 0, 0)),
         ],
@@ -588,8 +601,8 @@
         grid_spec=pltpu.PrefetchScalarGridSpec(
             num_scalar_prefetch=1,
             grid=(1,),
-            in_specs=[whole(CHIPS, PIECE, DK), pl.BlockSpec((64, DK), lambda i, b: (b[2], 0))],
-            out_specs=whole(CHIPS, PIECE, DK),
+            in_specs=[RESIDENT] * 2,
+            out_specs=RESIDENT,
         ),
         compiler_params=SHARED,
         name="scan",
@@ -605,9 +618,9 @@
         ),
         grid_spec=pltpu.PrefetchScalarGridSpec(
             num_scalar_prefetch=1,
-            grid=(HALF // 2,),
-            in_specs=[pieces, by_two, by_two, whole(3 * heads, DK), whole(3 * heads, DK)],
-            out_specs=(pl.BlockSpec((2, 4 * DK + EXTRA, DK), lambda i, b: (i, 0, 0)),) * 2,
+            grid=(1,),
+            in_specs=[RESIDENT] * 5,
+            out_specs=(RESIDENT,) * 2,
         ),
         compiler_params=SHARED,
         name="spread",
@@ -618,32 +631,19 @@
     half_blocks = blocks // 2
 
     def sense(mine, state, *before):
-        def first(b):
-            return first_block(mine, b, blocks)
-
         return pl.pallas_call(
             functools.partial(sense_kernel, mine),
             out_shape=(
                 shape((half_blocks, 3 * SIDES, tokens, DK), BF),
                 shape((2, 16, channels // 2), BF),
                 shape((12 * HALF, DK), F32),
+                shape((4 * HALF, DK), F32),
             ),
             grid_spec=pltpu.PrefetchScalarGridSpec(
                 num_scalar_prefetch=1,
-                grid=(half_blocks,),
-                in_specs=[
-                    pl.BlockSpec((1, 13, tokens, width), lambda i, b: (first(b) + i, 0, 0, 0)),
-                    whole(3, channels),
-                    whole(4, channels),
-                    pl.BlockSpec((1, tokens, 4 * SIDES), lambda i, b: (first(b) + i, 0, 0)),
-                    pl.BlockSpec((SIDES, 4 * DK, DK), lambda i, b: (i, 0, 0)),
-                    *[pl.BlockSpec((2, 16, 3 * width), lambda i, b: (0, 0, i)) for _ in before],
-                ],
-                out_specs=(
-                    pl.BlockSpec((1, 3 * SIDES, tokens, DK), lambda i, b: (i, 0, 0, 0)),
-                    pl.BlockSpec((2, 16, 3 * width), lambda i, b: (0, 0, i)),
-                    whole(12 * HALF, DK),
-                ),
+                grid=(1,),
+                in_specs=[RESIDENT] * (5 + len(before)),
+                out_specs=(RESIDENT,) * 4,
                 scratch_shapes=[
                     pltpu.VMEM((tokens + 16, 3 * SIDES * DK), F32),
                     pltpu.VMEM((tokens + 8, 3 * SIDES * DK), F32),
@@ -654,8 +654,8 @@
             cost_estimate=pl.CostEstimate(flops=3000000000, transcendentals=0, bytes_accessed=10800000),
         )(place, inner, rim, conv_weight, columns, state, *before)
 
-    conv_own, edge, tap_own = sense(True, kept)
-    conv_other, edge, tap_other = sense(False, received, edge)
+    conv_own, edge, tap_own, start_own = sense(True, kept)
+    conv_other, edge, tap_other, start_other = sense(False, received, edge)
 
     tap_far = lax.ppermute(tap_other, "seq", pairs)
 
@@ -674,7 +674,7 @@
     def readouts(inside):
         return pl.pallas_call(
             readout_kernel,
-            out_shape=(shape((tokens, heads * DK), BF), shape((4 * heads, DK), F32)),
+            out_shape=shape((tokens, heads * DK), BF),
             grid_spec=pltpu.PrefetchScalarGridSpec(
                 num_scalar_prefetch=1,
                 grid=(blocks,),
@@ -683,18 +683,13 @@
                     pl.BlockSpec((1, tokens, 4 * SIDES), lambda i, b: (i, 0, 0)),
                     pl.BlockSpec((SIDES, 2 * DK, DK), lambda i, b: (own_at(i, b), 0, 0)),
                     pl.BlockSpec((SIDES, 2 * DK, DK), lambda i, b: (other_at(i, b), 0, 0)),
-                    pl.BlockSpec((SIDES, EXTRA, DK), lambda i, b: (own_at(i, b), 4 * DK // EXTRA, 0)),
-                    pl.BlockSpec((SIDES, EXTRA, DK), lambda i, b: (other_at(i, b), 4 * DK // EXTRA, 0)),
                 ],
-                out_specs=(
-                    pl.BlockSpec((tokens, width), lambda i, b: (0, i)),
-                    pl.BlockSpec((4 * SIDES, DK), lambda i, b: (i, 0)),
-                ),
+                out_specs=pl.BlockSpec((tokens, width), lambda i, b: (0, i)),
             ),
             compiler_params=PARAMS,
             name="readout",
             cost_estimate=pl.CostEstimate(flops=3000000000, transcendentals=0, bytes_accessed=10800000),
-        )(place, inside, columns, kept, received, kept, received)
+        )(place, inside, columns, kept, received)
 
     def unrolled(rim):
         return pl.pallas_call(
@@ -729,21 +724,26 @@
         cost_estimate=pl.CostEstimate(flops=800000000, transcendentals=0, bytes_accessed=2880000),
     )(tap_own, tap_far)
 
-    spread_taps, inside = lax.optimization_barrier((spread_taps, inside))
     pieces = lax.all_to_all(spread_taps, "seq", 0, 0, axis_index_groups=groups)
-    output, start_all = readouts(inside)
-    pieces, output = lax.optimization_barrier((pieces, output))
+    pieces, edge = lax.optimization_barrier((pieces, edge))
     spread_sums = pl.pallas_call(
         fold_kernel,
         out_shape=shape((dp, sum_rows, DK), BF),
+        grid_spec=pltpu.PrefetchScalarGridSpec(
+            num_scalar_prefetch=1,
+            grid=(1,),
+            in_specs=[RESIDENT] * 3,
+            out_specs=RESIDENT,
+        ),
         compiler_params=SHARED,
         name="fold",
         cost_estimate=pl.CostEstimate(flops=800000000, transcendentals=0, bytes_accessed=2880000),
-    )(pieces, start_all)
-    spread_sums, edge = lax.optimization_barrier((spread_sums, edge))
+    )(place, pieces, start_own, start_other)
+    spread_sums, edge, inside = lax.optimization_barrier((spread_sums, edge, inside))
     pieces = lax.all_to_all(spread_sums, "dp", 0, 0)
+    output = readouts(inside)
     grad = unrolled(edge)
-    pieces, grad = lax.optimization_barrier((pieces, grad))
+    pieces, output, grad = lax.optimization_barrier((pieces, output, grad))
     total = pl.pallas_call(
         sum_kernel,
         out_shape=shape((sum_rows, DK), F32),

time: 121 us -> 117 us (0.967)
  local copies, waits for them, and re-layouts: 12.3 us -> 9.38 us
  Pallas kernels: 38.3 us -> 35.7 us
    ppermute x1, waiting for transfers between devices: 0.01 us -> 6.98 us  [local(): edge = lax.ppermute(edge, 'seq', back_one)]
    all_to_all x1, waiting for transfers between devices: 7.49 us -> 2.89 us  [local(): pieces = lax.all_to_all(spread_sums, 'dp', 0, 0)]
    unnamed x36, local copies, waits for them, and re-layouts: 11.4 us -> 8.48 us
    all_to_all x1, waiting for transfers between devices: 3.06 us -> 0.73 us  [local(): pieces = lax.all_to_all(spread_taps, 'seq', 0, 0, axis_index_groups=groups)]
    pallas_call x3 -> x4, Pallas kernels: 6.96 us -> 5.14 us  [the longest x1 2.14 us: readouts(): pl.pallas_call(readout_kernel, out_shape=shape((tokens, heads * DK), BF),...]
  transfers between devices with their start and end apart: 10 -> 10, of which waited for: 5 -> 6; matrix products, arithmetic and copies ran while one was open for 1% -> 1% of each run, Pallas kernels for 21% -> 18%
where the time goes in v3:
time: 117 us
  Pallas kernels  35.7 us (31%)
  starting transfers between devices  31.1 us (27%)
  blocking collectives  21.7 us (19%)
  waiting for transfers between devices  17.1 us (15%)
  local copies, waits for them, and re-layouts  9.38 us (8%)
    all_to_all x1, blocking collectives, local(): states = lax.all_to_all(back, 'seq', 0, 0, axis_index_groups=groups)  21.7 us
    unnamed x36, local copies, waits for them, and re-layouts  8.48 us
    all_to_all x1, starting transfers between devices, local(): pieces = lax.all_to_all(spread_sums, 'dp', 0, 0)  8.19 us
    pallas_call x1, Pallas kernels, local(): pl.pallas_call(inner_kernel, out_shape=(shape((blocks, 13, tokens, width)...  7.34 us
    pallas_call x2, Pallas kernels, elements(): pl.pallas_call(functools.partial(element_kernel, mine), out_shape=shape((...  7.07 us
    ppermute x1, waiting for transfers between devices, local(): edge = lax.ppermute(edge, 'seq', back_one)  6.98 us
    all_to_all x1, starting transfers between devices, local(): got = lax.all_to_all(payload, 'seq', 0, 0, axis_index_groups=groups)  6.91 us
    pallas_call x2, Pallas kernels, sense(): pl.pallas_call(functools.partial(sense_kernel, mine), out_shape=(shape((h...  6.25 us
  transfers between devices with their start and end apart: 10, of which 6 were waited for; matrix products, arithmetic and copies ran while one was open for 1% of the time, Pallas kernels for 18%

profile of v3, /device:TPU:1, one launch (start us, length us, event | category | flops | bytes accessed | tf_op | source)
XLA Modules:
  0.0 116.7 jit_solution(7767202289477307551)
XLA Ops:
  0.6 0.9 slice_bitcast_fusion
  1.5 4.5 %collective-permute-start = (bf16[8,6144]{1,0:T(8,128)(2,1)S(1)}, bf16[8,6144]{1,0:T(8,128)(2,1)S(1)}, u32[]{:S(2)}, u32[]{:S(2)}) collective-permute-start(bf16[8,6144]{1,0:T(8,128)(2,1)S(1)} %slice_bitcast_fusion), channel_id=1, source_target_pairs={{0,1},{1,2},{2,3},{3,4},{4,5},{5,6},{6,7},{7,8},{8,9},{9,10},{10,1... | collective-permute-start | bytes 294920 | tf_op jit(solution)/shard_map/ppermute | solution.py:509
  6.1 0.1 pad_add_fusion.place_ref
  6.2 0.7 pad_maximum_fusion.gate_ref
  6.9 0.9 tables.1
  7.8 0.5 copy-done.1
  8.3 0.1 copy-done.3
  8.4 0.0 copy-done.5
  8.4 3.5 %elements.3 = bf16[8,512,128]{2,1,0:T(8,128)(2,1)S(1)} custom-call(s32[3]{0:T(128)S(1)} %pad_add_fusion.place_ref, bf16[128,6144]{1,0:T(8,128)(2,1)S(1)} %bitcast.14, bf16[128,2048]{1,0:T(8,128)(2,1)S(1)} %bitcast.19, bf16[8,6144]{1,0:T(8,128)(2,1)S(1)} %collective-permute-done.halo_ref, f32[4,6144]{1,0:T(4,128)S(1)} %copy-done.5, ...), custom_call_target="tpu_custom_call" | custom-call | flops 3400000000 | bytes 12240000 | tf_op jit(solution)/shard_map/elements/pallas_call | solution.py:525
  12.0 0.1 collective-permute-start.1
  12.1 0.5 collective-permute-start.2
  12.6 3.5 %elements.2.own_ref = bf16[8,512,128]{2,1,0:T(8,128)(2,1)S(1)} custom-call(s32[3]{0:T(128)S(1)} %pad_add_fusion.place_ref, bf16[128,6144]{1,0:T(8,128)(2,1)S(1)} %bitcast.15, bf16[128,2048]{1,0:T(8,128)(2,1)S(1)} %bitcast.20, bf16[8,6144]{1,0:T(8,128)(2,1)S(1)} %collective-permute-done.halo_ref, f32[4,6144]{1,0:T(4,128)S(1)} %copy-done.5, ...), custom_call_target="tpu_custom_call" | custom-call | flops 3400000000 | bytes 12240000 | tf_op jit(solution)/shard_map/elements/pallas_call | solution.py:525
  16.1 2.1 %compose.1 = bf16[16,272,128]{2,1,0:T(8,128)(2,1)} custom-call(s32[3]{0:T(128)S(1)} %pad_add_fusion.place_ref, bf16[8,512,128]{2,1,0:T(8,128)(2,1)S(1)} %elements.2.own_ref, bf16[8,512,128]{2,1,0:T(8,128)(2,1)S(1)} %collective-permute-done.1.other_ref, f32[48,128]{1,0:T(8,128)S(1)} %get-tuple-element.39.own_coef_ref, ...), custom_call_target="tpu_custom_call" | custom-call | flops 1200000000 | bytes 4320000 | tf_op jit(solution)/shard_map/compose/pallas_call | solution.py:544
  18.2 6.9 %all-to-all-start = ((bf16[16,272,128]{2,1,0:T(8,128)(2,1)}), bf16[16,272,128]{2,1,0:T(8,128)(2,1)S(1)}, u32[]{:S(2)}, u32[]{:S(2)}) async-start(bf16[16,272,128]{2,1,0:T(8,128)(2,1)} %compose.1), calls=%async_computation | async-start | bytes 2228224 | tf_op jit(solution)/shard_map/all_to_all | solution.py:558
  25.2 0.0 copy-start.2
  25.2 0.0 copy-start.4
  25.2 0.8 couple.1.coupling_ref
  26.0 0.6 copy-done.2
  26.6 0.1 copy-done.4
  26.7 7.3 %inner.1 = (bf16[2,13,128,1024]{3,2,1,0:T(8,128)(2,1)S(1)}, bf16[2,2,128,1024]{3,2,1,0:T(8,128)(2,1)S(1)}) custom-call(bf16[128,6144]{1,0:T(8,128)(2,1)S(1)} %bitcast.16, bf16[128,6144]{1,0:T(8,128)(2,1)S(1)} %bitcast.17, bf16[128,6144]{1,0:T(8,128)(2,1)S(1)} %bitcast.18, bf16[128,2048]{1,0:T(8,128)(2,1)S(1)} %bitcast.21, ...), custom_call_target="tpu_custom_call" | custom-call | flops 8000000000 | bytes 28800000 | tf_op jit(solution)/shard_map/inner/pallas_call | solution.py:571
  34.0 2.8 %copy-done.6 = bf16[2,13,128,1024]{3,2,1,0:T(8,128)(2,1)} copy-done((bf16[2,13,128,1024]{3,2,1,0:T(8,128)(2,1)}, bf16[2,13,128,1024]{3,2,1,0:T(8,128)(2,1)S(1)}, u32[]{:S(2)}) %copy-start.6) | copy-done | bytes 6815768
  36.8 1.0 copy-done.14
  37.8 4.3 %all-to-all-done.got_ref = bf16[16,272,128]{2,1,0:T(8,128)(2,1)S(1)} async-done(((bf16[16,272,128]{2,1,0:T(8,128)(2,1)}), bf16[16,272,128]{2,1,0:T(8,128)(2,1)S(1)}, u32[]{:S(2)}, u32[]{:S(2)}) %all-to-all-start) | async-done | bytes 1114144 | tf_op jit(solution)/shard_map/all_to_all | solution.py:558
  42.2 0.9 scan.1
  43.0 21.7 %all_to_all.20.got_ref = bf16[16,272,128]{2,1,0:T(8,128)(2,1)S(1)} all-to-all(bf16[16,272,128]{2,1,0:T(8,128)(2,1)S(1)} %scan.1), channel_id=1, replica_groups={{0,2,4,6,8,10,12,14,16,18,20,22,24,26,28,30},{1,3,5,7,9,11,13,15,17,19,..., dimensions={0} | all-to-all | bytes 2228224 | tf_op jit(solution)/shard_map/all_to_all | solution.py:611
  64.8 1.2 %spread.1 = (bf16[8,528,128]{2,1,0:T(8,128)(2,1)S(1)}, bf16[8,528,128]{2,1,0:T(8,128)(2,1)S(1)}) custom-call(s32[3]{0:T(128)S(1)} %pad_add_fusion.place_ref, bf16[16,272,128]{2,1,0:T(8,128)(2,1)S(1)} %all_to_all.20.got_ref, bf16[8,512,128]{2,1,0:T(8,128)(2,1)S(1)} %copy-done.9, bf16[8,512,128]{2,1,0:T(8,128)(2,1)S(1)} %collective-permute-done.1.other_ref, ...), custom_call_target="tpu_custom_call" | custom-call | flops 1300000000 | bytes 4680000 | tf_op jit(solution)/shard_map/spread/pallas_call | solution.py:613
  66.0 0.0 copy-start.10
  66.0 2.0 %collective-permute-start.3 = (bf16[8,528,128]{2,1,0:T(8,128)(2,1)S(1)}, bf16[8,528,128]{2,1,0:T(8,128)(2,1)S(1)}, u32[]{:S(2)}, u32[]{:S(2)}) collective-permute-start(bf16[8,528,128]{2,1,0:T(8,128)(2,1)S(1)} %get-tuple-element.49), channel_id=1, source_target_pairs={{0,1},{1,0},{2,3},{3,2},{4,5},{5,4},{6,7},{7,6},{8,9},{9,8},{10,11... | collective-permute-start | bytes 3244040 | tf_op jit(solution)/shard_map/ppermute | solution.py:629
  68.0 3.1 %sense.2 = (bf16[1,24,128,128]{3,2,1,0:T(8,128)(2,1)S(1)}, bf16[2,16,3072]{2,1,0:T(8,128)(2,1)S(1)}, f32[96,128]{1,0:T(8,128)S(1)}, f32[32,128]{1,0:T(8,128)S(1)}) custom-call(s32[3]{0:T(128)S(1)} %pad_add_fusion.place_ref, bf16[2,13,128,1024]{3,2,1,0:T(8,128)(2,1)S(1)} %copy-done.7, bf16[8,6144]{1,0:T(8,128)(2,1)S(1)} %collective-permute-done.halo_ref, ...), custom_call_target="tpu_custom_call" | custom-call | flops 3000000000 | bytes 10800000 | tf_op jit(solution)/shard_map/sense/pallas_call | solution.py:634
  71.2 0.9 copy-done.12
  72.1 3.1 %sense.3 = (bf16[1,24,128,128]{3,2,1,0:T(8,128)(2,1)S(1)}, bf16[2,16,3072]{2,1,0:T(8,128)(2,1)S(1)}, f32[96,128]{1,0:T(8,128)S(1)}, f32[32,128]{1,0:T(8,128)S(1)}) custom-call(s32[3]{0:T(128)S(1)} %pad_add_fusion.place_ref, bf16[2,13,128,1024]{3,2,1,0:T(8,128)(2,1)S(1)} %copy-done.7, bf16[8,6144]{1,0:T(8,128)(2,1)S(1)} %collective-permute-done.halo_ref, ...), custom_call_target="tpu_custom_call" | custom-call | flops 3000000000 | bytes 10800000 | tf_op jit(solution)/shard_map/sense/pallas_call | solution.py:634
  75.2 0.1 collective-permute-start.4
  75.3 1.2 %collective-permute-done.4.far_ref = f32[96,128]{1,0:T(8,128)S(1)} collective-permute-done((f32[96,128]{1,0:T(8,128)S(1)}, f32[96,128]{1,0:T(8,128)S(1)}, u32[]{:S(2)}, u32[]{:S(2)}) %collective-permute-start.4) | collective-permute-done | bytes 49184 | tf_op jit(solution)/shard_map/ppermute | solution.py:660
  76.5 0.8 pack.1
  77.3 3.6 %all-to-all-start.2 = ((bf16[16,96,128]{2,1,0:T(8,128)(2,1)}), bf16[16,96,128]{2,1,0:T(8,128)(2,1)S(1)}, u32[]{:S(2)}, u32[]{:S(2)}) async-start(bf16[16,96,128]{2,1,0:T(8,128)(2,1)} %pack.1), calls=%async_computation.2 | async-start | bytes 786432 | tf_op jit(solution)/shard_map/all_to_all | solution.py:727
  80.9 2.1 %collective-permute-start.5 = (bf16[2,16,3072]{2,1,0:T(8,128)(2,1)S(1)}, bf16[2,16,3072]{2,1,0:T(8,128)(2,1)S(1)}, u32[]{:S(2)}, u32[]{:S(2)}) collective-permute-start(bf16[2,16,3072]{2,1,0:T(8,128)(2,1)S(1)} %get-tuple-element.52), channel_id=1, source_target_pairs={{1,0},{2,1},{3,2},{4,3},{5,4},{6,5},{7,6},{8,7},{9,8},{10,9},{11,1... | collective-permute-start | bytes 589832 | tf_op jit(solution)/shard_map/ppermute | solution.py:666
  82.9 7.0 %collective-permute-done.5.rim_own_ref.rim_other_ref = bf16[2,16,3072]{2,1,0:T(8,128)(2,1)S(1)} collective-permute-done((bf16[2,16,3072]{2,1,0:T(8,128)(2,1)S(1)}, bf16[2,16,3072]{2,1,0:T(8,128)(2,1)S(1)}, u32[]{:S(2)}, u32[]{:S(2)}) %collective-permute-start.5) | collective-permute-done | bytes 196640 | tf_op jit(solution)/shard_map/ppermute | solution.py:666
  89.9 0.7 all-to-all-done.2.pieces_ref
  90.7 1.3 %fold.1 = bf16[8,160,128]{2,1,0:T(8,128)(2,1)} custom-call(s32[3]{0:T(128)S(1)} %pad_add_fusion.place_ref, bf16[16,96,128]{2,1,0:T(8,128)(2,1)S(1)} %all-to-all-done.2.pieces_ref, f32[32,128]{1,0:T(8,128)S(1)} %get-tuple-element.54.own_ref, f32[32,128]{1,0:T(8,128)S(1)} %get-tuple-element.55.other_ref), custom_call_target="tpu_custom_call" | custom-call | flops 800000000 | bytes 2880000 | tf_op jit(solution)/shard_map/fold/pallas_call | solution.py:729
  92.0 8.2 %all-to-all-start.3 = ((bf16[8,160,128]{2,1,0:T(8,128)(2,1)}), bf16[8,160,128]{2,1,0:T(8,128)(2,1)S(1)}, u32[]{:S(2)}, u32[]{:S(2)}) async-start(bf16[8,160,128]{2,1,0:T(8,128)(2,1)} %fold.1), calls=%async_computation.3 | async-start | bytes 655360 | tf_op jit(solution)/shard_map/all_to_all | solution.py:743
  100.2 1.2 %copy-done.11 = bf16[8,528,128]{2,1,0:T(8,128)(2,1)S(1)} copy-done((bf16[8,528,128]{2,1,0:T(8,128)(2,1)S(1)}, bf16[8,528,128]{2,1,0:T(8,128)(2,1)}, u32[]{:S(2)}) %copy-start.11) | copy-done | bytes 1081368
  101.4 1.2 %copy-done.15 = bf16[2,2,128,1024]{3,2,1,0:T(8,128)(2,1)S(1)} copy-done((bf16[2,2,128,1024]{3,2,1,0:T(8,128)(2,1)S(1)}, bf16[2,2,128,1024]{3,2,1,0:T(8,128)(2,1)}, u32[]{:S(2)}) %copy-start.15) | copy-done | bytes 1048600
  102.7 2.1 %readout.1 = bf16[128,2048]{1,0:T(8,128)(2,1)} custom-call(s32[3]{0:T(128)S(1)} %pad_add_fusion.place_ref, bf16[2,2,128,1024]{3,2,1,0:T(8,128)(2,1)S(1)} %copy-done.15, f32[2,128,32]{2,1,0:T(8,128)S(1)} %copy-done.17, bf16[8,528,128]{2,1,0:T(8,128)(2,1)S(1)} %copy-done.11, bf16[8,528,128]{2,1,0:T(8,128)(2,1)S(1)} %collective-permute-done.3.state_ref.other_ref), custom_call_target="tpu_custom_call" | custom-call | flops 3000000000 | bytes 10800000 | tf_op jit(solution)/shard_map/readout/pallas_call | solution.py:675
  104.8 3.7 %unroll.1 = bf16[128,6144]{1,0:T(8,128)(2,1)} custom-call(s32[3]{0:T(128)S(1)} %pad_add_fusion.place_ref, bf16[1,24,128,128]{3,2,1,0:T(8,128)(2,1)S(1)} %copy-done.13, bf16[1,24,128,128]{3,2,1,0:T(8,128)(2,1)S(1)} %get-tuple-element.61.conv_other_ref, f32[4,6144]{1,0:T(4,128)S(1)} %copy-done.5, ...), custom_call_target="tpu_custom_call" | custom-call | flops 4000000000 | bytes 14400000 | tf_op jit(solution)/shard_map/unroll/pallas_call | solution.py:695
  108.5 2.9 %all-to-all-done.3.pieces_ref = bf16[8,160,128]{2,1,0:T(8,128)(2,1)S(1)} async-done(((bf16[8,160,128]{2,1,0:T(8,128)(2,1)}), bf16[8,160,128]{2,1,0:T(8,128)(2,1)S(1)}, u32[]{:S(2)}, u32[]{:S(2)}) %all-to-all-start.3) | async-done | bytes 327712 | tf_op jit(solution)/shard_map/all_to_all | solution.py:743
  111.4 3.2 %collective-permute-start.6 = (f32[160,128]{1,0:T(8,128)S(1)}, f32[160,128]{1,0:T(8,128)S(1)}, u32[]{:S(2)}, u32[]{:S(2)}) collective-permute-start(f32[160,128]{1,0:T(8,128)S(1)} %total.1.own_ref), channel_id=1, source_target_pairs={{0,1},{1,0},{2,3},{3,2},{4,5},{5,4},{6,7},{7,6},{8,9},{9,8},{10,11... | collective-permute-start | bytes 245768 | tf_op jit(solution)/shard_map/ppermute | solution.py:754
  114.6 0.9 collective-permute-done.6.other_ref
  115.5 1.2 %assemble.1 = (f32[4,6144]{1,0:T(4,128)}, f32[16,4,128]{2,1,0:T(4,128)}) custom-call(s32[3]{0:T(128)S(1)} %pad_add_fusion.place_ref, f32[160,128]{1,0:T(8,128)S(1)} %total.1.own_ref, f32[160,128]{1,0:T(8,128)S(1)} %collective-permute-done.6.other_ref), custom_call_target="tpu_custom_call" | custom-call | flops 1000000000 | bytes 3600000 | tf_op jit(solution)/shard_map/assemble/pallas_call | solution.py:755
  (28 shorter events, 0.1 us)
Async XLA Ops:
  1.5 6.2 %collective-permute-start = (bf16[8,6144]{1,0:T(8,128)(2,1)S(1)}, bf16[8,6144]{1,0:T(8,128)(2,1)S(1)}, u32[]{:S(2)}, u32[]{:S(2)}) collective-permute-start(bf16[8,6144]{1,0:T(8,128)(2,1)S(1)} %slice_bitcast_fusion), channel_id=1, source_target_pairs={{0,1},{1,2},{2,3},{3,4},{4,5},{5,6},{6,7},{7,8},{8,9},{9,10},{10,1... | collective-permute-start | bytes 294920 | tf_op jit(solution)/shard_map/ppermute | solution.py:509
  6.9 1.4 %copy-start.1 = (bf16[1,128,6144]{2,1,0:T(8,128)(2,1)S(1)}, bf16[1,128,6144]{2,1,0:T(8,128)(2,1)}, u32[]{:S(2)}) copy-start(bf16[1,128,6144]{2,1,0:T(8,128)(2,1)} %param.7) | copy-start | bytes 4718596
  6.9 1.5 %copy-start.3 = (bf16[1,128,2048]{2,1,0:T(8,128)(2,1)S(1)}, bf16[1,128,2048]{2,1,0:T(8,128)(2,1)}, u32[]{:S(2)}) copy-start(bf16[1,128,2048]{2,1,0:T(8,128)(2,1)} %param.13) | copy-start | bytes 1572868
  6.9 1.5 %copy-start.5 = (f32[4,6144]{1,0:T(4,128)S(1)}, f32[4,6144]{1,0:T(4,128)}, u32[]{:S(2)}) copy-start(f32[4,6144]{1,0:T(4,128)} %weight_ref.11) | copy-start | bytes 294916
  7.8 4.8 %copy-start.16 = (f32[2,128,32]{2,1,0:T(8,128)}, f32[2,128,32]{2,1,0:T(8,128)S(1)}, u32[]{:S(2)}) copy-start(f32[2,128,32]{2,1,0:T(8,128)S(1)} %get-tuple-element.38.column_ref) | copy-start | bytes 98308
  12.0 4.2 %collective-permute-start.1 = (bf16[8,512,128]{2,1,0:T(8,128)(2,1)S(1)}, bf16[8,512,128]{2,1,0:T(8,128)(2,1)S(1)}, u32[]{:S(2)}, u32[]{:S(2)}) collective-permute-start(bf16[8,512,128]{2,1,0:T(8,128)(2,1)S(1)} %elements.3), channel_id=1, source_target_pairs={{0,1},{1,0},{2,3},{3,2},{4,5},{5,4},{6,7},{7,6},{8,9},{9,8},{10,11... | collective-permute-start | bytes 3145736 | tf_op jit(solution)/shard_map/ppermute | solution.py:541
  12.1 4.0 %collective-permute-start.2 = (f32[48,128]{1,0:T(8,128)S(1)}, f32[48,128]{1,0:T(8,128)S(1)}, u32[]{:S(2)}, u32[]{:S(2)}) collective-permute-start(f32[48,128]{1,0:T(8,128)S(1)} %get-tuple-element.39.own_coef_ref), channel_id=1, source_target_pairs={{0,1},{1,0},{2,3},{3,2},{4,5},{5,4},{6,7},{7,6},{8,9},{9,8},{10,11... | collective-permute-start | bytes 73736 | tf_op jit(solution)/shard_map/ppermute | solution.py:522
  16.1 2.1 %copy-start.8 = (bf16[8,512,128]{2,1,0:T(8,128)(2,1)}, bf16[8,512,128]{2,1,0:T(8,128)(2,1)S(1)}, u32[]{:S(2)}) copy-start(bf16[8,512,128]{2,1,0:T(8,128)(2,1)S(1)} %elements.2.own_ref) | copy-start | bytes 3145732
  18.2 23.9 %all-to-all-start = ((bf16[16,272,128]{2,1,0:T(8,128)(2,1)}), bf16[16,272,128]{2,1,0:T(8,128)(2,1)S(1)}, u32[]{:S(2)}, u32[]{:S(2)}) async-start(bf16[16,272,128]{2,1,0:T(8,128)(2,1)} %compose.1), calls=%async_computation | async-start | bytes 2228224 | tf_op jit(solution)/shard_map/all_to_all | solution.py:558
  25.2 1.4 %copy-start.2 = (bf16[1,128,6144]{2,1,0:T(8,128)(2,1)S(1)}, bf16[1,128,6144]{2,1,0:T(8,128)(2,1)}, u32[]{:S(2)}) copy-start(bf16[1,128,6144]{2,1,0:T(8,128)(2,1)} %param.7) | copy-start | bytes 4718596
  25.2 1.5 %copy-start.4 = (bf16[1,128,2048]{2,1,0:T(8,128)(2,1)S(1)}, bf16[1,128,2048]{2,1,0:T(8,128)(2,1)}, u32[]{:S(2)}) copy-start(bf16[1,128,2048]{2,1,0:T(8,128)(2,1)} %param.13) | copy-start | bytes 1572868
  26.7 15.5 %copy-start = (f32[16,128,128]{2,1,0:T(8,128)S(1)}, f32[16,128,128]{2,1,0:T(8,128)}, u32[]{:S(2)}) copy-start(f32[16,128,128]{2,1,0:T(8,128)} %param.9) | copy-start | bytes 3145732
  34.0 2.8 %copy-start.6 = (bf16[2,13,128,1024]{3,2,1,0:T(8,128)(2,1)}, bf16[2,13,128,1024]{3,2,1,0:T(8,128)(2,1)S(1)}, u32[]{:S(2)}) copy-start(bf16[2,13,128,1024]{3,2,1,0:T(8,128)(2,1)S(1)} %get-tuple-element.45.in_ref) | copy-start | bytes 20447236
  36.8 1.0 copy-start.14
  42.1 22.6 %copy-start.9 = (bf16[8,512,128]{2,1,0:T(8,128)(2,1)S(1)}, bf16[8,512,128]{2,1,0:T(8,128)(2,1)}, u32[]{:S(2)}) copy-start(bf16[8,512,128]{2,1,0:T(8,128)(2,1)} %copy-done.8) | copy-start | bytes 3145732
  43.0 25.0 %copy-start.7 = (bf16[2,13,128,1024]{3,2,1,0:T(8,128)(2,1)S(1)}, bf16[2,13,128,1024]{3,2,1,0:T(8,128)(2,1)}, u32[]{:S(2)}) copy-start(bf16[2,13,128,1024]{3,2,1,0:T(8,128)(2,1)} %copy-done.6) | copy-start | bytes 20447236
  64.8 3.3 %copy-start.17 = (f32[2,128,32]{2,1,0:T(8,128)S(1)}, f32[2,128,32]{2,1,0:T(8,128)}, u32[]{:S(2)}) copy-start(f32[2,128,32]{2,1,0:T(8,128)} %copy-done.16) | copy-start | bytes 98308
  66.0 5.2 %copy-start.10 = (bf16[8,528,128]{2,1,0:T(8,128)(2,1)}, bf16[8,528,128]{2,1,0:T(8,128)(2,1)S(1)}, u32[]{:S(2)}) copy-start(bf16[8,528,128]{2,1,0:T(8,128)(2,1)S(1)} %get-tuple-element.47.state_ref.own_ref) | copy-start | bytes 3244036
  66.0 6.1 %collective-permute-start.3 = (bf16[8,528,128]{2,1,0:T(8,128)(2,1)S(1)}, bf16[8,528,128]{2,1,0:T(8,128)(2,1)S(1)}, u32[]{:S(2)}, u32[]{:S(2)}) collective-permute-start(bf16[8,528,128]{2,1,0:T(8,128)(2,1)S(1)} %get-tuple-element.49), channel_id=1, source_target_pairs={{0,1},{1,0},{2,3},{3,2},{4,5},{5,4},{6,7},{7,6},{8,9},{9,8},{10,11... | collective-permute-start | bytes 3244040 | tf_op jit(solution)/shard_map/ppermute | solution.py:629
  71.2 0.9 copy-start.12
  75.2 1.3 %collective-permute-start.4 = (f32[96,128]{1,0:T(8,128)S(1)}, f32[96,128]{1,0:T(8,128)S(1)}, u32[]{:S(2)}, u32[]{:S(2)}) collective-permute-start(f32[96,128]{1,0:T(8,128)S(1)} %get-tuple-element.51), channel_id=1, source_target_pairs={{0,1},{1,0},{2,3},{3,2},{4,5},{5,4},{6,7},{7,6},{8,9},{9,8},{10,11... | collective-permute-start | bytes 147464 | tf_op jit(solution)/shard_map/ppermute | solution.py:660
  77.3 13.3 %all-to-all-start.2 = ((bf16[16,96,128]{2,1,0:T(8,128)(2,1)}), bf16[16,96,128]{2,1,0:T(8,128)(2,1)S(1)}, u32[]{:S(2)}, u32[]{:S(2)}) async-start(bf16[16,96,128]{2,1,0:T(8,128)(2,1)} %pack.1), calls=%async_computation.2 | async-start | bytes 786432 | tf_op jit(solution)/shard_map/all_to_all | solution.py:727
  80.9 9.1 %collective-permute-start.5 = (bf16[2,16,3072]{2,1,0:T(8,128)(2,1)S(1)}, bf16[2,16,3072]{2,1,0:T(8,128)(2,1)S(1)}, u32[]{:S(2)}, u32[]{:S(2)}) collective-permute-start(bf16[2,16,3072]{2,1,0:T(8,128)(2,1)S(1)} %get-tuple-element.52), channel_id=1, source_target_pairs={{1,0},{2,1},{3,2},{4,3},{5,4},{6,5},{7,6},{8,7},{9,8},{10,9},{11,1... | collective-permute-start | bytes 589832 | tf_op jit(solution)/shard_map/ppermute | solution.py:666
  92.0 19.3 %all-to-all-start.3 = ((bf16[8,160,128]{2,1,0:T(8,128)(2,1)}), bf16[8,160,128]{2,1,0:T(8,128)(2,1)S(1)}, u32[]{:S(2)}, u32[]{:S(2)}) async-start(bf16[8,160,128]{2,1,0:T(8,128)(2,1)} %fold.1), calls=%async_computation.3 | async-start | bytes 655360 | tf_op jit(solution)/shard_map/all_to_all | solution.py:743
  100.2 1.2 %copy-start.11 = (bf16[8,528,128]{2,1,0:T(8,128)(2,1)S(1)}, bf16[8,528,128]{2,1,0:T(8,128)(2,1)}, u32[]{:S(2)}) copy-start(bf16[8,528,128]{2,1,0:T(8,128)(2,1)} %copy-done.10) | copy-start | bytes 3244036
  101.4 1.2 %copy-start.15 = (bf16[2,2,128,1024]{3,2,1,0:T(8,128)(2,1)S(1)}, bf16[2,2,128,1024]{3,2,1,0:T(8,128)(2,1)}, u32[]{:S(2)}) copy-start(bf16[2,2,128,1024]{3,2,1,0:T(8,128)(2,1)} %copy-done.14) | copy-start | bytes 3145732
  102.7 2.1 %copy-start.13 = (bf16[1,24,128,128]{3,2,1,0:T(8,128)(2,1)S(1)}, bf16[1,24,128,128]{3,2,1,0:T(8,128)(2,1)}, u32[]{:S(2)}) copy-start(bf16[1,24,128,128]{3,2,1,0:T(8,128)(2,1)} %copy-done.12) | copy-start | bytes 2359300
  111.4 4.1 %collective-permute-start.6 = (f32[160,128]{1,0:T(8,128)S(1)}, f32[160,128]{1,0:T(8,128)S(1)}, u32[]{:S(2)}, u32[]{:S(2)}) collective-permute-start(f32[160,128]{1,0:T(8,128)S(1)} %total.1.own_ref), channel_id=1, source_target_pairs={{0,1},{1,0},{2,3},{3,2},{4,5},{5,4},{6,7},{7,6},{8,9},{9,8},{10,11... | collective-permute-start | bytes 245768 | tf_op jit(solution)/shard_map/ppermute | solution.py:754

commit v4 on v3

--- a/solution.py
+++ b/solution.py
@@ -21,6 +21,12 @@
 
 def dot(a, b, contract):
     return lax.dot_general(a, b, ((contract[:1], contract[1:]), ((), ())), preferred_element_type=F32)
+
+
+def here():
+    mine = lax.axis_index("seq")
+    core, chip = lax.rem(mine, 2), lax.div(mine, 2)
+    return core, lax.div(chip, 8), core * (HALF * DK // 64) + chip
 
 
 def to_column(row, eye):
@@ -93,7 +99,7 @@
 
 def extend(ext_ref, slot, halo, own):
     cols = slice(slot * DK, (slot + 1) * DK)
-    ext_ref[0:8, cols] = halo.astype(F32)
+    ext_ref[0:8, cols] = halo.astype(F32)[8:16]
     ext_ref[8 : 8 + own.shape[0], cols] = own.astype(F32)
 
 
@@ -106,11 +112,11 @@
 
 
 def element_kernel(
-    mine, place_ref, rows_ref, u_ref, halo_ref, weight_ref, column_ref, element_ref, ext_ref
+    mine, rows_ref, u_ref, halo_ref, weight_ref, column_ref, element_ref, ext_ref
 ):
     tokens = rows_ref.shape[0]
     section = rows_ref.shape[1] // 3
-    half = place_ref[0] if mine else 1 - place_ref[0]
+    half = here()[0] if mine else 1 - here()[0]
     for side in range(HALF):
         made = []
         for part in range(3):
@@ -139,12 +145,12 @@
         element_ref[side, 2 * DK : 4 * DK] = dot(left, upstream, (0, 0)).astype(BF)
 
 
-def compose_kernel(place_ref, own_ref, other_ref, own_coef_ref, other_coef_ref, out_ref):
-    core = place_ref[0]
+def compose_kernel(own_ref, other_ref, own_coef_ref, other_coef_ref, out_ref):
+    core = here()[0]
     first_core = core == 0
     heads = own_coef_ref.shape[0] // 3
     for j in range(own_ref.shape[0]):
-        head = core * HALF + pl.program_id(0) * own_ref.shape[0] + j
+        head = core * HALF + j
 
         def coef(which):
             mine = own_coef_ref[pl.ds(which * heads + head, 1), :]
@@ -190,7 +196,7 @@
             out_ref[2 * j + half, 256:PIECE] = tail
 
 
-def scan_kernel(place_ref, got_ref, start_ref, out_ref):
+def scan_kernel(got_ref, start_ref, out_ref):
     count = got_ref.shape[0]
 
     def coefs(c):
@@ -201,7 +207,7 @@
         )
 
     scalars = [coefs(c) for c in range(count)]
-    memory = start_ref[pl.ds(pl.multiple_of(place_ref[2] * 64, 64), 64), :]
+    memory = start_ref[pl.ds(pl.multiple_of(here()[2] * 64, 64), 64), :]
     state = jnp.zeros_like(memory)
     for c in range(count):
         out_ref[c, 0:64] = memory.astype(BF)
@@ -224,14 +230,13 @@
 
 
 def spread_kernel(
-    place_ref, got_ref, own_ref, other_ref, own_coef_ref, other_coef_ref, keep_ref, send_ref
+    got_ref, own_ref, other_ref, own_coef_ref, other_coef_ref, keep_ref, send_ref
 ):
-    core = place_ref[0]
-    side = place_ref[1]
+    core, side, _ = here()
     first_core = core == 0
     heads = own_coef_ref.shape[0] // 3
     for j in range(own_ref.shape[0]):
-        head = core * HALF + pl.program_id(0) * own_ref.shape[0] + j
+        head = core * HALF + j
 
         def coef(which):
             mine = own_coef_ref[pl.ds(which * heads + head, 1), :]
@@ -338,13 +343,14 @@
 
 
 def sense_kernel(
-    mine, place_ref, in_ref, halo_ref, weight_ref, column_ref, state_ref, *refs
+    mine, in_ref, halo_ref, weight_ref, column_ref, state_ref, *refs
 ):
     conv_ref, rim_ref, tap_ref, start_ref, pad_ref, ext_ref = refs[-6:]
     tokens = in_ref.shape[2]
     width = in_ref.shape[3]
     section = halo_ref.shape[1] // 3
-    block = place_ref[0] if mine else 1 - place_ref[0]
+    core = here()[0]
+    block = core if mine else 1 - core
     if len(refs) > 6:
         rim_ref[0] = refs[0][1]
     else:
@@ -360,7 +366,7 @@
         memory_col, tail_col, forget_col, carry_col = (column(i) for i in range(4))
         start = state_ref[side, 4 * DK :].astype(F32)
         start = start[0:8] + start[8:16]
-        start_ref[4 * side : 4 * side + 4] = jnp.where(place_ref[0] == 0, start[0:4], start[4:8])
+        start_ref[4 * side : 4 * side + 4] = jnp.where(core == 0, start[0:4], start[4:8])
         forward, adjoint = state_ref[side, : 2 * DK], state_ref[side, 2 * DK : 4 * DK]
         grads = []
         a, b = along_lanes(upstream, forward)
@@ -447,12 +453,12 @@
         out_ref[i] = value
 
 
-def fold_kernel(place_ref, pieces_ref, own_ref, other_ref, out_ref):
+def fold_kernel(pieces_ref, own_ref, other_ref, out_ref):
     total = pieces_ref[0].astype(F32)
     for i in range(1, pieces_ref.shape[0]):
         total = total + pieces_ref[i].astype(F32)
     own, other = own_ref[...], other_ref[...]
-    first_core = place_ref[0] == 0
+    first_core = here()[0] == 0
     value = jnp.concatenate(
         [total, jnp.where(first_core, own, other), jnp.where(first_core, other, own)], axis=0
     ).astype(BF)
@@ -467,8 +473,9 @@
     out_ref[...] = total
 
 
-def assemble_kernel(place_ref, own_ref, other_ref, out_ref, start_ref):
+def assemble_kernel(own_ref, other_ref, out_ref, start_ref):
     section = out_ref.shape[1] // 3
+    core = here()[0]
     for h in range(section // DK):
         first = 12 * HALF + 4 * h
         start_ref[h] = own_ref[first : first + 4]
@@ -478,7 +485,7 @@
             rows = slice(first, first + 4)
             at = part * section + h * DK
             out_ref[:, at : at + DK] = jnp.where(
-                place_ref[0] == h // HALF, own_ref[rows], other_ref[rows]
+                core == h // HALF, own_ref[rows], other_ref[rows]
             )
 
 
@@ -498,15 +505,14 @@
     blocks = heads * DK // width
     count = lax.axis_size("seq")
     mine = lax.axis_index("seq")
-    core = mine % 2
-    chip = mine // 2
-    place = jnp.stack([core, chip // 8, core * (HALF * DK // 64) + chip]).astype(jnp.int32)
+    core = lax.rem(mine, 2)
+    place = core.astype(jnp.int32).reshape(1)
     gates = jnp.concatenate([log_forget[0], log_momentum[0], learn_rate[0]], axis=0)
     gates, place = lax.optimization_barrier((gates, place))
     pairs = [(i, i ^ 1) for i in range(count)]
     groups = [[2 * c + k for c in range(count // 2)] for k in range(2)]
 
-    rim = lax.ppermute(rows[tokens - 8 :], "seq", [(i, i + 1) for i in range(count - 1)])
+    rim = lax.ppermute(rows[tokens - 16 :], "seq", [(i, i + 1) for i in range(count - 1)])
     shape = jax.ShapeDtypeStruct
     columns, coefs, cums = pl.pallas_call(
         tables_kernel,
@@ -525,17 +531,13 @@
         return pl.pallas_call(
             functools.partial(element_kernel, mine),
             out_shape=shape((HALF, 4 * DK, DK), BF),
-            grid_spec=pltpu.PrefetchScalarGridSpec(
-                num_scalar_prefetch=1,
-                grid=(1,),
-                in_specs=[RESIDENT] * 5,
+            in_specs=[RESIDENT] * 5,
                 out_specs=RESIDENT,
                 scratch_shapes=[pltpu.VMEM((tokens + 8, 3 * HALF * DK), F32)],
-            ),
             compiler_params=SHARED,
             name="elements",
             cost_estimate=pl.CostEstimate(flops=3400000000, transcendentals=0, bytes_accessed=12240000),
-        )(place, rows, upstream, rim, conv_weight, columns)
+        )(rows, upstream, rim, conv_weight, columns)
 
     sent = elements(False)
     other = lax.ppermute(sent, "seq", pairs)
@@ -544,16 +546,12 @@
     payload = pl.pallas_call(
         compose_kernel,
         out_shape=shape((CHIPS, PIECE, DK), BF),
-        grid_spec=pltpu.PrefetchScalarGridSpec(
-            num_scalar_prefetch=1,
-            grid=(1,),
-            in_specs=[RESIDENT] * 4,
+        in_specs=[RESIDENT] * 4,
             out_specs=RESIDENT,
-        ),
         compiler_params=SHARED,
         name="compose",
         cost_estimate=pl.CostEstimate(flops=1200000000, transcendentals=0, bytes_accessed=4320000),
-    )(place, own, other, coefs, other_coefs)
+    )(own, other, coefs, other_coefs)
     payload, cums = lax.optimization_barrier((payload, cums))
     got = lax.all_to_all(payload, "seq", 0, 0, axis_index_groups=groups)
 
@@ -580,7 +578,7 @@
             block_at(1),
             block_at(2),
             block_at(0),
-            whole(8, channels),
+            whole(16, channels),
             whole(4, channels),
             pl.BlockSpec((SIDES, tokens, tokens), lambda i: (i, 0, 0)),
         ],
@@ -598,16 +596,12 @@
     back = pl.pallas_call(
         scan_kernel,
         out_shape=shape((CHIPS, PIECE, DK), BF),
-        grid_spec=pltpu.PrefetchScalarGridSpec(
-            num_scalar_prefetch=1,
-            grid=(1,),
-            in_specs=[RESIDENT] * 2,
+        in_specs=[RESIDENT] * 2,
             out_specs=RESIDENT,
-        ),
         compiler_params=SHARED,
         name="scan",
         cost_estimate=pl.CostEstimate(flops=400000000, transcendentals=0, bytes_accessed=1440000),
-    )(place, got, initial_memory.reshape(heads * DK, DK))
+    )(got, initial_memory.reshape(heads * DK, DK))
     states = lax.all_to_all(back, "seq", 0, 0, axis_index_groups=groups)
 
     kept, passed = pl.pallas_call(
@@ -616,16 +610,12 @@
             shape((HALF, 4 * DK + EXTRA, DK), BF),
             shape((HALF, 4 * DK + EXTRA, DK), BF),
         ),
-        grid_spec=pltpu.PrefetchScalarGridSpec(
-            num_scalar_prefetch=1,
-            grid=(1,),
-            in_specs=[RESIDENT] * 5,
+        in_specs=[RESIDENT] * 5,
             out_specs=(RESIDENT,) * 2,
-        ),
         compiler_params=SHARED,
         name="spread",
         cost_estimate=pl.CostEstimate(flops=1300000000, transcendentals=0, bytes_accessed=4680000),
-    )(place, states, own, other, coefs, other_coefs)
+    )(states, own, other, coefs, other_coefs)
     received = lax.ppermute(passed, "seq", pairs)
 
     half_blocks = blocks // 2
@@ -639,20 +629,16 @@
                 shape((12 * HALF, DK), F32),
                 shape((4 * HALF, DK), F32),
             ),
-            grid_spec=pltpu.PrefetchScalarGridSpec(
-                num_scalar_prefetch=1,
-                grid=(1,),
-                in_specs=[RESIDENT] * (5 + len(before)),
+            in_specs=[RESIDENT] * (5 + len(before)),
                 out_specs=(RESIDENT,) * 4,
                 scratch_shapes=[
                     pltpu.VMEM((tokens + 16, 3 * SIDES * DK), F32),
                     pltpu.VMEM((tokens + 8, 3 * SIDES * DK), F32),
                 ],
-            ),
             compiler_params=PARAMS,
             name="sense",
             cost_estimate=pl.CostEstimate(flops=3000000000, transcendentals=0, bytes_accessed=10800000),
-        )(place, inner, rim, conv_weight, columns, state, *before)
+        )(inner, rim, conv_weight, columns, state, *before)
 
     conv_own, edge, tap_own, start_own = sense(True, kept)
     conv_other, edge, tap_other, start_other = sense(False, received, edge)
@@ -725,23 +711,19 @@
     )(tap_own, tap_far)
 
     pieces = lax.all_to_all(spread_taps, "seq", 0, 0, axis_index_groups=groups)
-    pieces, edge = lax.optimization_barrier((pieces, edge))
     spread_sums = pl.pallas_call(
         fold_kernel,
         out_shape=shape((dp, sum_rows, DK), BF),
-        grid_spec=pltpu.PrefetchScalarGridSpec(
-            num_scalar_prefetch=1,
-            grid=(1,),
-            in_specs=[RESIDENT] * 3,
+        in_specs=[RESIDENT] * 3,
             out_specs=RESIDENT,
-        ),
         compiler_params=SHARED,
         name="fold",
         cost_estimate=pl.CostEstimate(flops=800000000, transcendentals=0, bytes_accessed=2880000),
-    )(place, pieces, start_own, start_other)
-    spread_sums, edge, inside = lax.optimization_barrier((spread_sums, edge, inside))
+    )(pieces, start_own, start_other)
+    spread_sums, inside = lax.optimization_barrier((spread_sums, inside))
     pieces = lax.all_to_all(spread_sums, "dp", 0, 0)
     output = readouts(inside)
+    edge, output = lax.optimization_barrier((edge, output))
     grad = unrolled(edge)
     pieces, output, grad = lax.optimization_barrier((pieces, output, grad))
     total = pl.pallas_call(
@@ -755,16 +737,12 @@
     taps, start_all = pl.pallas_call(
         assemble_kernel,
         out_shape=(shape((4, channels), F32), shape((heads, 4, DK), F32)),
-        grid_spec=pltpu.PrefetchScalarGridSpec(
-            num_scalar_prefetch=1,
-            grid=(1,),
-            in_specs=[whole(sum_rows, DK)] * 2,
-            out_specs=(whole(4, channels), whole(heads, 4, DK)),
-        ),
+        in_specs=[RESIDENT] * 2,
+            out_specs=(RESIDENT,) * 2,
         compiler_params=SHARED,
         name="assemble",
         cost_estimate=pl.CostEstimate(flops=1000000000, transcendentals=0, bytes_accessed=3600000),
-    )(place, total, total_far)
+    )(total, total_far)
     return (output[None], grad[None], taps, start_all)
 
 

time: 117 us -> 114 us (0.974)
  Pallas kernels: 35.7 us -> 29.6 us
  waiting for transfers between devices: 17.1 us -> 20.2 us
    all_to_all x1, waiting for transfers between devices: 0.73 us -> 7.71 us  [local(): pieces = lax.all_to_all(spread_taps, 'seq', 0, 0, axis_index_groups=groups)]
    ppermute x1, waiting for transfers between devices: 6.98 us -> 0.01 us  [local(): edge = lax.ppermute(edge, 'seq', back_one)]
    all_to_all x1, waiting for transfers between devices: 2.89 us -> 5.17 us  [local(): pieces = lax.all_to_all(spread_sums, 'dp', 0, 0)]
    pallas_call x3, Pallas kernels: 4.3 us -> 2.68 us  [the longest x1 1.59 us: local(): pl.pallas_call(compose_kernel, out_shape=shape((CHIPS, PIECE, DK), BF), i...]
    pallas_call x2, Pallas kernels: 6.25 us -> 4.93 us  [sense(): pl.pallas_call(functools.partial(sense_kernel, mine), out_shape=(shape((h...]
    unnamed x36 -> x42, local copies, waits for them, and re-layouts: 8.48 us -> 7.54 us
where the time goes in v4:
time: 114 us
  starting transfers between devices  31.9 us (28%)
  Pallas kernels  29.6 us (26%)
  blocking collectives  21.7 us (19%)
  waiting for transfers between devices  20.2 us (18%)
  local copies, waits for them, and re-layouts  8.49 us (7%)
    all_to_all x1, blocking collectives, local(): states = lax.all_to_all(back, 'seq', 0, 0, axis_index_groups=groups)  21.7 us
    all_to_all x1, starting transfers between devices, local(): pieces = lax.all_to_all(spread_sums, 'dp', 0, 0)  8.18 us
    all_to_all x1, starting transfers between devices, local(): got = lax.all_to_all(payload, 'seq', 0, 0, axis_index_groups=groups)  7.74 us
    all_to_all x1, waiting for transfers between devices, local(): pieces = lax.all_to_all(spread_taps, 'seq', 0, 0, axis_index_groups=groups)  7.71 us
    unnamed x42, local copies, waits for them, and re-layouts  7.54 us
    pallas_call x1, Pallas kernels, local(): pl.pallas_call(inner_kernel, out_shape=(shape((blocks, 13, tokens, width)...  7.36 us
    pallas_call x2, Pallas kernels, elements(): pl.pallas_call(functools.partial(element_kernel, mine), out_shape=shape((...  6.02 us
    all_to_all x1, waiting for transfers between devices, local(): pieces = lax.all_to_all(spread_sums, 'dp', 0, 0)  5.17 us
  transfers between devices with their start and end apart: 10, of which 6 were waited for; matrix products, arithmetic and copies ran while one was open for 1% of the time, Pallas kernels for 18%

profile of v4, /device:TPU:1, one launch (start us, length us, event | category | flops | bytes accessed | tf_op | source)
XLA Modules:
  0.0 113.6 jit_solution(15916237826747045132)
XLA Ops:
  0.6 0.9 slice_bitcast_fusion
  1.6 4.5 %collective-permute-start = (bf16[16,6144]{1,0:T(8,128)(2,1)S(1)}, bf16[16,6144]{1,0:T(8,128)(2,1)S(1)}, u32[]{:S(2)}, u32[]{:S(2)}) collective-permute-start(bf16[16,6144]{1,0:T(8,128)(2,1)S(1)} %slice_bitcast_fusion), channel_id=1, source_target_pairs={{0,1},{1,2},{2,3},{3,4},{4,5},{5,6},{6,7},{7,8},{8,9},{9,10},{10,1... | collective-permute-start | bytes 589832 | tf_op jit(solution)/shard_map/ppermute | solution.py:515
  6.1 0.7 pad_maximum_fusion.gate_ref
  6.8 0.9 tables.1
  7.7 1.0 collective-permute-done.halo_ref
  8.7 3.0 %elements.3 = bf16[8,512,128]{2,1,0:T(8,128)(2,1)S(1)} custom-call(bf16[128,6144]{1,0:T(8,128)(2,1)S(1)} %bitcast.12, bf16[128,2048]{1,0:T(8,128)(2,1)S(1)} %bitcast.17, bf16[16,6144]{1,0:T(8,128)(2,1)S(1)} %collective-permute-done.halo_ref, f32[4,6144]{1,0:T(4,128)S(1)} %copy-done.5, f32[2,128,32]{2,1,0:T(8,128)S(1)} %get-tuple-element.36.column_ref), custom_call_target="tpu_custom_call" | custom-call | flops 3400000000 | bytes 12240000 | tf_op jit(solution)/shard_map/elements/pallas_call | solution.py:531
  11.7 0.1 collective-permute-start.1
  11.8 0.5 collective-permute-start.2
  12.3 3.0 %elements.2.own_ref = bf16[8,512,128]{2,1,0:T(8,128)(2,1)S(1)} custom-call(bf16[128,6144]{1,0:T(8,128)(2,1)S(1)} %bitcast.13, bf16[128,2048]{1,0:T(8,128)(2,1)S(1)} %bitcast.18, bf16[16,6144]{1,0:T(8,128)(2,1)S(1)} %collective-permute-done.halo_ref, f32[4,6144]{1,0:T(4,128)S(1)} %copy-done.5, f32[2,128,32]{2,1,0:T(8,128)S(1)} %get-tuple-element.36.column_ref), custom_call_target="tpu_custom_call" | custom-call | flops 3400000000 | bytes 12240000 | tf_op jit(solution)/shard_map/elements/pallas_call | solution.py:531
  15.3 0.0 collective-permute-done.2.other_coef_ref
  15.4 0.0 collective-permute-done.1.other_ref
  15.4 1.6 %compose.1 = bf16[16,272,128]{2,1,0:T(8,128)(2,1)} custom-call(bf16[8,512,128]{2,1,0:T(8,128)(2,1)S(1)} %elements.2.own_ref, bf16[8,512,128]{2,1,0:T(8,128)(2,1)S(1)} %collective-permute-done.1.other_ref, f32[48,128]{1,0:T(8,128)S(1)} %get-tuple-element.37.own_coef_ref, f32[48,128]{1,0:T(8,128)S(1)} %collective-permute-done.2.other_coef_ref), custom_call_target="tpu_custom_call" | custom-call | flops 1200000000 | bytes 4320000 | tf_op jit(solution)/shard_map/compose/pallas_call | solution.py:546
  17.0 7.7 %all-to-all-start = ((bf16[16,272,128]{2,1,0:T(8,128)(2,1)}), bf16[16,272,128]{2,1,0:T(8,128)(2,1)S(1)}, u32[]{:S(2)}, u32[]{:S(2)}) async-start(bf16[16,272,128]{2,1,0:T(8,128)(2,1)} %compose.1), calls=%async_computation | async-start | bytes 2228224 | tf_op jit(solution)/shard_map/all_to_all | solution.py:556
  24.7 0.0 copy-start.2
  24.7 0.0 copy-start.4
  24.7 0.8 couple.1.coupling_ref
  25.5 0.6 copy-done.2
  26.1 0.1 copy-done.4
  26.2 7.4 %inner.1 = (bf16[2,13,128,1024]{3,2,1,0:T(8,128)(2,1)S(1)}, bf16[2,2,128,1024]{3,2,1,0:T(8,128)(2,1)S(1)}) custom-call(bf16[128,6144]{1,0:T(8,128)(2,1)S(1)} %bitcast.14, bf16[128,6144]{1,0:T(8,128)(2,1)S(1)} %bitcast.15, bf16[128,6144]{1,0:T(8,128)(2,1)S(1)} %bitcast.16, bf16[128,2048]{1,0:T(8,128)(2,1)S(1)} %bitcast.19, ...), custom_call_target="tpu_custom_call" | custom-call | flops 8000000000 | bytes 28800000 | tf_op jit(solution)/shard_map/inner/pallas_call | solution.py:569
  33.6 2.8 %copy-done.6 = bf16[2,13,128,1024]{3,2,1,0:T(8,128)(2,1)} copy-done((bf16[2,13,128,1024]{3,2,1,0:T(8,128)(2,1)}, bf16[2,13,128,1024]{3,2,1,0:T(8,128)(2,1)S(1)}, u32[]{:S(2)}) %copy-start.6) | copy-done | bytes 6815768
  36.4 1.0 copy-done.16
  37.4 4.3 %all-to-all-done.got_ref = bf16[16,272,128]{2,1,0:T(8,128)(2,1)S(1)} async-done(((bf16[16,272,128]{2,1,0:T(8,128)(2,1)}), bf16[16,272,128]{2,1,0:T(8,128)(2,1)S(1)}, u32[]{:S(2)}, u32[]{:S(2)}) %all-to-all-start) | async-done | bytes 1114144 | tf_op jit(solution)/shard_map/all_to_all | solution.py:556
  41.7 0.3 scan.1
  42.0 21.7 %all_to_all.20.got_ref = bf16[16,272,128]{2,1,0:T(8,128)(2,1)S(1)} all-to-all(bf16[16,272,128]{2,1,0:T(8,128)(2,1)S(1)} %scan.1), channel_id=1, replica_groups={{0,2,4,6,8,10,12,14,16,18,20,22,24,26,28,30},{1,3,5,7,9,11,13,15,17,19,..., dimensions={0} | all-to-all | bytes 2228224 | tf_op jit(solution)/shard_map/all_to_all | solution.py:605
  63.8 0.7 spread.1
  64.5 0.0 copy-start.10
  64.5 2.0 %collective-permute-start.3 = (bf16[8,528,128]{2,1,0:T(8,128)(2,1)S(1)}, bf16[8,528,128]{2,1,0:T(8,128)(2,1)S(1)}, u32[]{:S(2)}, u32[]{:S(2)}) collective-permute-start(bf16[8,528,128]{2,1,0:T(8,128)(2,1)S(1)} %get-tuple-element.47), channel_id=1, source_target_pairs={{0,1},{1,0},{2,3},{3,2},{4,5},{5,4},{6,7},{7,6},{8,9},{9,8},{10,11... | collective-permute-start | bytes 3244040 | tf_op jit(solution)/shard_map/ppermute | solution.py:619
  66.5 2.5 %sense.2 = (bf16[1,24,128,128]{3,2,1,0:T(8,128)(2,1)S(1)}, bf16[2,16,3072]{2,1,0:T(8,128)(2,1)S(1)}, f32[96,128]{1,0:T(8,128)S(1)}, f32[32,128]{1,0:T(8,128)S(1)}) custom-call(bf16[2,13,128,1024]{3,2,1,0:T(8,128)(2,1)S(1)} %copy-done.7, bf16[16,6144]{1,0:T(8,128)(2,1)S(1)} %collective-permute-done.halo_ref, f32[4,6144]{1,0:T(4,128)S(1)} %copy-done.5, ...), custom_call_target="tpu_custom_call" | custom-call | flops 3000000000 | bytes 10800000 | tf_op jit(solution)/shard_map/sense/pallas_call | solution.py:624
  69.0 0.9 copy-done.14
  69.9 0.0 collective-permute-done.3.state_ref.other_ref
  69.9 2.5 %sense.3 = (bf16[1,24,128,128]{3,2,1,0:T(8,128)(2,1)S(1)}, bf16[2,16,3072]{2,1,0:T(8,128)(2,1)S(1)}, f32[96,128]{1,0:T(8,128)S(1)}, f32[32,128]{1,0:T(8,128)S(1)}) custom-call(bf16[2,13,128,1024]{3,2,1,0:T(8,128)(2,1)S(1)} %copy-done.7, bf16[16,6144]{1,0:T(8,128)(2,1)S(1)} %collective-permute-done.halo_ref, f32[4,6144]{1,0:T(4,128)S(1)} %copy-done.5, ...), custom_call_target="tpu_custom_call" | custom-call | flops 3000000000 | bytes 10800000 | tf_op jit(solution)/shard_map/sense/pallas_call | solution.py:624
  72.4 0.9 copy-done.12
  73.3 0.1 collective-permute-start.4
  73.4 1.1 %collective-permute-done.4.far_ref = f32[96,128]{1,0:T(8,128)S(1)} collective-permute-done((f32[96,128]{1,0:T(8,128)S(1)}, f32[96,128]{1,0:T(8,128)S(1)}, u32[]{:S(2)}, u32[]{:S(2)}) %collective-permute-start.4) | collective-permute-done | bytes 49184 | tf_op jit(solution)/shard_map/ppermute | solution.py:646
  74.5 0.8 pack.1
  75.3 3.6 %all-to-all-start.2 = ((bf16[16,96,128]{2,1,0:T(8,128)(2,1)}), bf16[16,96,128]{2,1,0:T(8,128)(2,1)S(1)}, u32[]{:S(2)}, u32[]{:S(2)}) async-start(bf16[16,96,128]{2,1,0:T(8,128)(2,1)} %pack.1), calls=%async_computation.2 | async-start | bytes 786432 | tf_op jit(solution)/shard_map/all_to_all | solution.py:713
  78.8 2.1 %collective-permute-start.5 = (bf16[2,16,3072]{2,1,0:T(8,128)(2,1)S(1)}, bf16[2,16,3072]{2,1,0:T(8,128)(2,1)S(1)}, u32[]{:S(2)}, u32[]{:S(2)}) collective-permute-start(bf16[2,16,3072]{2,1,0:T(8,128)(2,1)S(1)} %get-tuple-element.54), channel_id=1, source_target_pairs={{1,0},{2,1},{3,2},{4,3},{5,4},{6,5},{7,6},{8,7},{9,8},{10,9},{11,1... | collective-permute-start | bytes 589832 | tf_op jit(solution)/shard_map/ppermute | solution.py:652
  80.9 7.7 %all-to-all-done.2.pieces_ref = bf16[16,96,128]{2,1,0:T(8,128)(2,1)S(1)} async-done(((bf16[16,96,128]{2,1,0:T(8,128)(2,1)}), bf16[16,96,128]{2,1,0:T(8,128)(2,1)S(1)}, u32[]{:S(2)}, u32[]{:S(2)}) %all-to-all-start.2) | async-done | bytes 393248 | tf_op jit(solution)/shard_map/all_to_all | solution.py:713
  88.6 0.8 fold.1
  89.4 8.2 %all-to-all-start.3 = ((bf16[8,160,128]{2,1,0:T(8,128)(2,1)}), bf16[8,160,128]{2,1,0:T(8,128)(2,1)S(1)}, u32[]{:S(2)}, u32[]{:S(2)}) async-start(bf16[8,160,128]{2,1,0:T(8,128)(2,1)} %fold.1), calls=%async_computation.3 | async-start | bytes 655360 | tf_op jit(solution)/shard_map/all_to_all | solution.py:724
  97.6 1.2 %copy-done.17 = bf16[2,2,128,1024]{3,2,1,0:T(8,128)(2,1)S(1)} copy-done((bf16[2,2,128,1024]{3,2,1,0:T(8,128)(2,1)S(1)}, bf16[2,2,128,1024]{3,2,1,0:T(8,128)(2,1)}, u32[]{:S(2)}) %copy-start.17) | copy-done | bytes 1048600
  98.8 1.6 %readout.1 = bf16[128,2048]{1,0:T(8,128)(2,1)} custom-call(s32[1]{0:T(128)} %bitcast.6.place_ref, bf16[2,2,128,1024]{3,2,1,0:T(8,128)(2,1)S(1)} %copy-done.17, f32[2,128,32]{2,1,0:T(8,128)S(1)} %copy-done.20, bf16[8,528,128]{2,1,0:T(8,128)(2,1)S(1)} %copy-done.11, bf16[8,528,128]{2,1,0:T(8,128)(2,1)S(1)} %collective-permute-done.3.state_ref.other_ref), custom_call_target="tpu_custom_call" | custom-call | flops 3000000000 | bytes 10800000 | tf_op jit(solution)/shard_map/readout/pallas_call | solution.py:661
  100.4 0.0 collective-permute-done.5.rim_own_ref.rim_other_ref
  100.4 3.1 %unroll.1 = bf16[128,6144]{1,0:T(8,128)(2,1)} custom-call(s32[1]{0:T(128)} %bitcast.6.place_ref, bf16[1,24,128,128]{3,2,1,0:T(8,128)(2,1)S(1)} %copy-done.15, bf16[1,24,128,128]{3,2,1,0:T(8,128)(2,1)S(1)} %copy-done.13, f32[4,6144]{1,0:T(4,128)S(1)} %copy-done.5, bf16[2,16,3072]{2,1,0:T(8,128)(2,1)S(1)} %collective-permute-done.5.rim_own_ref.rim_other_ref, ...), custom_call_target="tpu_custom_call" | custom-call | flops 4000000000 | bytes 14400000 | tf_op jit(solution)/shard_map/unroll/pallas_call | solution.py:681
  103.6 5.2 %all-to-all-done.3.pieces_ref = bf16[8,160,128]{2,1,0:T(8,128)(2,1)S(1)} async-done(((bf16[8,160,128]{2,1,0:T(8,128)(2,1)}), bf16[8,160,128]{2,1,0:T(8,128)(2,1)S(1)}, u32[]{:S(2)}, u32[]{:S(2)}) %all-to-all-start.3) | async-done | bytes 327712 | tf_op jit(solution)/shard_map/all_to_all | solution.py:724
  108.8 3.2 %collective-permute-start.6 = (f32[160,128]{1,0:T(8,128)S(1)}, f32[160,128]{1,0:T(8,128)S(1)}, u32[]{:S(2)}, u32[]{:S(2)}) collective-permute-start(f32[160,128]{1,0:T(8,128)S(1)} %total.1.own_ref), channel_id=1, source_target_pairs={{0,1},{1,0},{2,3},{3,2},{4,5},{5,4},{6,7},{7,6},{8,9},{9,8},{10,11... | collective-permute-start | bytes 245768 | tf_op jit(solution)/shard_map/ppermute | solution.py:736
  112.0 0.9 collective-permute-done.6.other_ref
  112.9 0.7 assemble.1
  (33 shorter events, 0.1 us)
Async XLA Ops:
  1.6 7.1 %collective-permute-start = (bf16[16,6144]{1,0:T(8,128)(2,1)S(1)}, bf16[16,6144]{1,0:T(8,128)(2,1)S(1)}, u32[]{:S(2)}, u32[]{:S(2)}) collective-permute-start(bf16[16,6144]{1,0:T(8,128)(2,1)S(1)} %slice_bitcast_fusion), channel_id=1, source_target_pairs={{0,1},{1,2},{2,3},{3,4},{4,5},{5,6},{6,7},{7,8},{8,9},{9,10},{10,1... | collective-permute-start | bytes 589832 | tf_op jit(solution)/shard_map/ppermute | solution.py:515
  6.8 1.9 %copy-start.1 = (bf16[1,128,6144]{2,1,0:T(8,128)(2,1)S(1)}, bf16[1,128,6144]{2,1,0:T(8,128)(2,1)}, u32[]{:S(2)}) copy-start(bf16[1,128,6144]{2,1,0:T(8,128)(2,1)} %param.7) | copy-start | bytes 4718596
  6.8 1.9 %copy-start.3 = (bf16[1,128,2048]{2,1,0:T(8,128)(2,1)S(1)}, bf16[1,128,2048]{2,1,0:T(8,128)(2,1)}, u32[]{:S(2)}) copy-start(bf16[1,128,2048]{2,1,0:T(8,128)(2,1)} %param.13) | copy-start | bytes 1572868
  6.8 1.9 %copy-start.5 = (f32[4,6144]{1,0:T(4,128)S(1)}, f32[4,6144]{1,0:T(4,128)}, u32[]{:S(2)}) copy-start(f32[4,6144]{1,0:T(4,128)} %weight_ref.11) | copy-start | bytes 294916
  7.7 4.6 %copy-start.18 = (f32[2,128,32]{2,1,0:T(8,128)}, f32[2,128,32]{2,1,0:T(8,128)S(1)}, u32[]{:S(2)}) copy-start(f32[2,128,32]{2,1,0:T(8,128)S(1)} %get-tuple-element.36.column_ref) | copy-start | bytes 98308
  11.7 3.6 %collective-permute-start.1 = (bf16[8,512,128]{2,1,0:T(8,128)(2,1)S(1)}, bf16[8,512,128]{2,1,0:T(8,128)(2,1)S(1)}, u32[]{:S(2)}, u32[]{:S(2)}) collective-permute-start(bf16[8,512,128]{2,1,0:T(8,128)(2,1)S(1)} %elements.3), channel_id=1, source_target_pairs={{0,1},{1,0},{2,3},{3,2},{4,5},{5,4},{6,7},{7,6},{8,9},{9,8},{10,11... | collective-permute-start | bytes 3145736 | tf_op jit(solution)/shard_map/ppermute | solution.py:543
  11.8 3.5 %collective-permute-start.2 = (f32[48,128]{1,0:T(8,128)S(1)}, f32[48,128]{1,0:T(8,128)S(1)}, u32[]{:S(2)}, u32[]{:S(2)}) collective-permute-start(f32[48,128]{1,0:T(8,128)S(1)} %get-tuple-element.37.own_coef_ref), channel_id=1, source_target_pairs={{0,1},{1,0},{2,3},{3,2},{4,5},{5,4},{6,7},{7,6},{8,9},{9,8},{10,11... | collective-permute-start | bytes 73736 | tf_op jit(solution)/shard_map/ppermute | solution.py:528
  15.3 1.6 %copy-start.8 = (bf16[8,512,128]{2,1,0:T(8,128)(2,1)}, bf16[8,512,128]{2,1,0:T(8,128)(2,1)S(1)}, u32[]{:S(2)}) copy-start(bf16[8,512,128]{2,1,0:T(8,128)(2,1)S(1)} %elements.2.own_ref) | copy-start | bytes 3145732
  17.0 24.7 %all-to-all-start = ((bf16[16,272,128]{2,1,0:T(8,128)(2,1)}), bf16[16,272,128]{2,1,0:T(8,128)(2,1)S(1)}, u32[]{:S(2)}, u32[]{:S(2)}) async-start(bf16[16,272,128]{2,1,0:T(8,128)(2,1)} %compose.1), calls=%async_computation | async-start | bytes 2228224 | tf_op jit(solution)/shard_map/all_to_all | solution.py:556
  24.7 1.4 %copy-start.2 = (bf16[1,128,6144]{2,1,0:T(8,128)(2,1)S(1)}, bf16[1,128,6144]{2,1,0:T(8,128)(2,1)}, u32[]{:S(2)}) copy-start(bf16[1,128,6144]{2,1,0:T(8,128)(2,1)} %param.7) | copy-start | bytes 4718596
  24.7 1.5 %copy-start.4 = (bf16[1,128,2048]{2,1,0:T(8,128)(2,1)S(1)}, bf16[1,128,2048]{2,1,0:T(8,128)(2,1)}, u32[]{:S(2)}) copy-start(bf16[1,128,2048]{2,1,0:T(8,128)(2,1)} %param.13) | copy-start | bytes 1572868
  26.2 15.5 %copy-start = (f32[16,128,128]{2,1,0:T(8,128)S(1)}, f32[16,128,128]{2,1,0:T(8,128)}, u32[]{:S(2)}) copy-start(f32[16,128,128]{2,1,0:T(8,128)} %param.9) | copy-start | bytes 3145732
  33.6 2.8 %copy-start.6 = (bf16[2,13,128,1024]{3,2,1,0:T(8,128)(2,1)}, bf16[2,13,128,1024]{3,2,1,0:T(8,128)(2,1)S(1)}, u32[]{:S(2)}) copy-start(bf16[2,13,128,1024]{3,2,1,0:T(8,128)(2,1)S(1)} %get-tuple-element.43.in_ref) | copy-start | bytes 20447236
  36.4 1.0 copy-start.16
  41.7 22.1 %copy-start.9 = (bf16[8,512,128]{2,1,0:T(8,128)(2,1)S(1)}, bf16[8,512,128]{2,1,0:T(8,128)(2,1)}, u32[]{:S(2)}) copy-start(bf16[8,512,128]{2,1,0:T(8,128)(2,1)} %copy-done.8) | copy-start | bytes 3145732
  42.0 24.5 %copy-start.7 = (bf16[2,13,128,1024]{3,2,1,0:T(8,128)(2,1)S(1)}, bf16[2,13,128,1024]{3,2,1,0:T(8,128)(2,1)}, u32[]{:S(2)}) copy-start(bf16[2,13,128,1024]{3,2,1,0:T(8,128)(2,1)} %copy-done.6) | copy-start | bytes 20447236
  63.8 2.7 %copy-start.19 = (f32[2,128,32]{2,1,0:T(8,128)S(1)}, f32[2,128,32]{2,1,0:T(8,128)}, u32[]{:S(2)}) copy-start(f32[2,128,32]{2,1,0:T(8,128)} %copy-done.18) | copy-start | bytes 98308
  64.5 4.5 %copy-start.10 = (bf16[8,528,128]{2,1,0:T(8,128)(2,1)}, bf16[8,528,128]{2,1,0:T(8,128)(2,1)S(1)}, u32[]{:S(2)}) copy-start(bf16[8,528,128]{2,1,0:T(8,128)(2,1)S(1)} %get-tuple-element.45.state_ref.own_ref) | copy-start | bytes 3244036
  64.5 5.4 %collective-permute-start.3 = (bf16[8,528,128]{2,1,0:T(8,128)(2,1)S(1)}, bf16[8,528,128]{2,1,0:T(8,128)(2,1)S(1)}, u32[]{:S(2)}, u32[]{:S(2)}) collective-permute-start(bf16[8,528,128]{2,1,0:T(8,128)(2,1)S(1)} %get-tuple-element.47), channel_id=1, source_target_pairs={{0,1},{1,0},{2,3},{3,2},{4,5},{5,4},{6,7},{7,6},{8,9},{9,8},{10,11... | collective-permute-start | bytes 3244040 | tf_op jit(solution)/shard_map/ppermute | solution.py:619
  69.0 0.9 copy-start.14
  72.4 0.9 copy-start.12
  73.3 1.2 %collective-permute-start.4 = (f32[96,128]{1,0:T(8,128)S(1)}, f32[96,128]{1,0:T(8,128)S(1)}, u32[]{:S(2)}, u32[]{:S(2)}) collective-permute-start(f32[96,128]{1,0:T(8,128)S(1)} %get-tuple-element.49), channel_id=1, source_target_pairs={{0,1},{1,0},{2,3},{3,2},{4,5},{5,4},{6,7},{7,6},{8,9},{9,8},{10,11... | collective-permute-start | bytes 147464 | tf_op jit(solution)/shard_map/ppermute | solution.py:646
  75.3 13.3 %all-to-all-start.2 = ((bf16[16,96,128]{2,1,0:T(8,128)(2,1)}), bf16[16,96,128]{2,1,0:T(8,128)(2,1)S(1)}, u32[]{:S(2)}, u32[]{:S(2)}) async-start(bf16[16,96,128]{2,1,0:T(8,128)(2,1)} %pack.1), calls=%async_computation.2 | async-start | bytes 786432 | tf_op jit(solution)/shard_map/all_to_all | solution.py:713
  78.8 21.6 %collective-permute-start.5 = (bf16[2,16,3072]{2,1,0:T(8,128)(2,1)S(1)}, bf16[2,16,3072]{2,1,0:T(8,128)(2,1)S(1)}, u32[]{:S(2)}, u32[]{:S(2)}) collective-permute-start(bf16[2,16,3072]{2,1,0:T(8,128)(2,1)S(1)} %get-tuple-element.54), channel_id=1, source_target_pairs={{1,0},{2,1},{3,2},{4,3},{5,4},{6,5},{7,6},{8,7},{9,8},{10,9},{11,1... | collective-permute-start | bytes 589832 | tf_op jit(solution)/shard_map/ppermute | solution.py:652
  88.6 9.0 %copy-start.11 = (bf16[8,528,128]{2,1,0:T(8,128)(2,1)S(1)}, bf16[8,528,128]{2,1,0:T(8,128)(2,1)}, u32[]{:S(2)}) copy-start(bf16[8,528,128]{2,1,0:T(8,128)(2,1)} %copy-done.10) | copy-start | bytes 3244036
  88.6 9.0 %copy-start.20 = (f32[2,128,32]{2,1,0:T(8,128)S(1)}, f32[2,128,32]{2,1,0:T(8,128)}, u32[]{:S(2)}) copy-start(f32[2,128,32]{2,1,0:T(8,128)} %copy-done.18) | copy-start | bytes 98308
  89.4 19.3 %all-to-all-start.3 = ((bf16[8,160,128]{2,1,0:T(8,128)(2,1)}), bf16[8,160,128]{2,1,0:T(8,128)(2,1)S(1)}, u32[]{:S(2)}, u32[]{:S(2)}) async-start(bf16[8,160,128]{2,1,0:T(8,128)(2,1)} %fold.1), calls=%async_computation.3 | async-start | bytes 655360 | tf_op jit(solution)/shard_map/all_to_all | solution.py:724
  97.6 1.2 %copy-start.17 = (bf16[2,2,128,1024]{3,2,1,0:T(8,128)(2,1)S(1)}, bf16[2,2,128,1024]{3,2,1,0:T(8,128)(2,1)}, u32[]{:S(2)}) copy-start(bf16[2,2,128,1024]{3,2,1,0:T(8,128)(2,1)} %copy-done.16) | copy-start | bytes 3145732
  98.8 1.6 %copy-start.13 = (bf16[1,24,128,128]{3,2,1,0:T(8,128)(2,1)S(1)}, bf16[1,24,128,128]{3,2,1,0:T(8,128)(2,1)}, u32[]{:S(2)}) copy-start(bf16[1,24,128,128]{3,2,1,0:T(8,128)(2,1)} %copy-done.12) | copy-start | bytes 2359300
  98.8 1.6 %copy-start.15 = (bf16[1,24,128,128]{3,2,1,0:T(8,128)(2,1)S(1)}, bf16[1,24,128,128]{3,2,1,0:T(8,128)(2,1)}, u32[]{:S(2)}) copy-start(bf16[1,24,128,128]{3,2,1,0:T(8,128)(2,1)} %copy-done.14) | copy-start | bytes 2359300
  108.8 4.1 %collective-permute-start.6 = (f32[160,128]{1,0:T(8,128)S(1)}, f32[160,128]{1,0:T(8,128)S(1)}, u32[]{:S(2)}, u32[]{:S(2)}) collective-permute-start(f32[160,128]{1,0:T(8,128)S(1)} %total.1.own_ref), channel_id=1, source_target_pairs={{0,1},{1,0},{2,3},{3,2},{4,5},{5,4},{6,7},{7,6},{8,9},{9,8},{10,11... | collective-permute-start | bytes 245768 | tf_op jit(solution)/shard_map/ppermute | solution.py:736

commit v5 on v4

--- a/solution.py
+++ b/solution.py
@@ -132,17 +132,18 @@
             made.append(active)
         query, key, value = made
         column = picker(column_ref, half, side)
-        query = query.astype(BF).astype(F32)
-        key = key.astype(BF).astype(F32)
-        left = jnp.concatenate(
-            [(key * column(0)).astype(BF), (key * column(1)).astype(BF)], axis=1
+        value = value.astype(BF).astype(F32)
+        right = jnp.concatenate([(value * column(0)).astype(BF), (value * column(1)).astype(BF)], axis=1)
+        both = dot(key.astype(BF), right, (0, 0)).astype(BF)
+        element_ref[side, 0:DK] = both[:, :DK]
+        element_ref[side, DK : 2 * DK] = both[:, DK:]
+        upstream = u_ref[:, pl.ds(pl.multiple_of(half * (HALF * DK) + side * DK, DK), DK)].astype(F32)
+        right = jnp.concatenate(
+            [(upstream * column(2)).astype(BF), (upstream * column(3)).astype(BF)], axis=1
         )
-        element_ref[side, 0 : 2 * DK] = dot(left, value.astype(BF), (0, 0)).astype(BF)
-        left = jnp.concatenate(
-            [(query * column(2)).astype(BF), (query * column(3)).astype(BF)], axis=1
-        )
-        upstream = u_ref[:, pl.ds(pl.multiple_of(half * (HALF * DK) + side * DK, DK), DK)]
-        element_ref[side, 2 * DK : 4 * DK] = dot(left, upstream, (0, 0)).astype(BF)
+        both = dot(query.astype(BF), right, (0, 0)).astype(BF)
+        element_ref[side, 2 * DK : 3 * DK] = both[:, :DK]
+        element_ref[side, 3 * DK : 4 * DK] = both[:, DK:]
 
 
 def compose_kernel(own_ref, other_ref, own_coef_ref, other_coef_ref, out_ref):
@@ -375,6 +376,7 @@
         grads.append(memory_col * a + tail_col * b)
         a, b = along_rows(key, adjoint)
         grads.append(memory_col * a + tail_col * b)
+        rims = []
         for part in range(3):
             grad = grads[part]
             if part < 2:
@@ -397,9 +399,9 @@
                 tap_ref[slot_row : slot_row + 1, :] = jnp.sum(moved * rows, axis=0, keepdims=True)
                 lead = moved[0:8] * weights[tap : tap + 1]
                 rim = lead if rim is None else rim + lead
-            rim_ref[1, :, part * width + side * DK : part * width + (side + 1) * DK] = jnp.concatenate(
-                [jnp.zeros_like(rim), rim], axis=0
-            ).astype(BF)
+            rims.append(rim[5:8])
+        rims.append(jnp.zeros((7, DK), F32))
+        rim_ref[1, :, cols] = jnp.concatenate(rims, axis=0).astype(BF)
 
 
 def readout_kernel(
@@ -431,6 +433,7 @@
 
     for side in range(width // DK):
         cols = slice(side * DK, (side + 1) * DK)
+        rims = jnp.where(owned, rim_own_ref[0, :, cols], rim_other_ref[0, :, cols]).astype(F32)
         for part in range(3):
             at = pl.ds(pl.multiple_of(part * section + block * width + side * DK, DK), DK)
             slot = side * 3 + part
@@ -441,9 +444,8 @@
             total = grad * weights[3:4]
             for tap in range(3):
                 total = total + pad_ref[3 - tap : 3 - tap + tokens, there] * weights[tap : tap + 1]
-            near = slice(part * width + side * DK, part * width + (side + 1) * DK)
-            rim = jnp.where(owned, rim_own_ref[0, :, near], rim_other_ref[0, :, near]).astype(F32)
-            total = jnp.concatenate([total[: tokens - 16], total[tokens - 16 :] + rim], axis=0)
+            rim = rims[3 * part : 3 * part + 3]
+            total = jnp.concatenate([total[: tokens - 3], total[tokens - 3 :] + rim], axis=0)
             grad_ref[:, at] = total.astype(BF)
 
 
@@ -625,7 +627,7 @@
             functools.partial(sense_kernel, mine),
             out_shape=(
                 shape((half_blocks, 3 * SIDES, tokens, DK), BF),
-                shape((2, 16, channels // 2), BF),
+                shape((2, 16, HALF * DK), BF),
                 shape((12 * HALF, DK), F32),
                 shape((4 * HALF, DK), F32),
             ),
@@ -688,8 +690,8 @@
                     pl.BlockSpec((1, 3 * SIDES, tokens, DK), lambda i, b: (own_at(i, b), 0, 0, 0)),
                     pl.BlockSpec((1, 3 * SIDES, tokens, DK), lambda i, b: (other_at(i, b), 0, 0, 0)),
                     whole(4, channels),
-                    pl.BlockSpec((1, 16, 3 * width), lambda i, b: (1, 0, own_at(i, b))),
-                    pl.BlockSpec((1, 16, 3 * width), lambda i, b: (0, 0, other_at(i, b))),
+                    pl.BlockSpec((1, 16, width), lambda i, b: (1, 0, own_at(i, b))),
+                    pl.BlockSpec((1, 16, width), lambda i, b: (0, 0, other_at(i, b))),
                 ],
                 out_specs=whole(tokens, channels),
                 scratch_shapes=[pltpu.VMEM((tokens + 8, 3 * SIDES * DK), F32)],

time: 114 us -> 113 us (level)
  Pallas kernels: 29.6 us -> 28.3 us
    pallas_call x2, Pallas kernels: 6.02 us -> 4.71 us  [elements(): pl.pallas_call(functools.partial(element_kernel, mine), out_shape=shape((...]
  transfers between devices with their start and end apart: 10 -> 10, of which waited for: 6 -> 6; matrix products, arithmetic and copies ran while one was open for 1% -> 1% of each run, Pallas kernels for 18% -> 17%
where the time goes in v5:
time: 113 us; the launch traced here: 112 us
  starting transfers between devices  31.9 us (28%)
  Pallas kernels  28.3 us (25%)
  blocking collectives  21.7 us (19%)
  waiting for transfers between devices  20.2 us (18%)
  local copies, waits for them, and re-layouts  8.49 us (8%)
    all_to_all x1, blocking collectives, local(): states = lax.all_to_all(back, 'seq', 0, 0, axis_index_groups=groups)  21.7 us
    all_to_all x1, starting transfers between devices, local(): pieces = lax.all_to_all(spread_sums, 'dp', 0, 0)  8.18 us
    all_to_all x1, starting transfers between devices, local(): got = lax.all_to_all(payload, 'seq', 0, 0, axis_index_groups=groups)  7.74 us
    all_to_all x1, waiting for transfers between devices, local(): pieces = lax.all_to_all(spread_taps, 'seq', 0, 0, axis_index_groups=groups)  7.71 us
    unnamed x42, local copies, waits for them, and re-layouts  7.54 us
    pallas_call x1, Pallas kernels, local(): pl.pallas_call(inner_kernel, out_shape=(shape((blocks, 13, tokens, width)...  7.37 us
    all_to_all x1, waiting for transfers between devices, local(): pieces = lax.all_to_all(spread_sums, 'dp', 0, 0)  5.15 us
    pallas_call x2, Pallas kernels, sense(): pl.pallas_call(functools.partial(sense_kernel, mine), out_shape=(shape((h...  4.91 us
  transfers between devices with their start and end apart: 10, of which 6 were waited for; matrix products, arithmetic and copies ran while one was open for 1% of the time, Pallas kernels for 17%

profile of v5, /device:TPU:1, one launch (start us, length us, event | category | flops | bytes accessed | tf_op | source)
XLA Modules:
  0.0 112.2 jit_solution(12588008277876523312)
XLA Ops:
  0.6 0.9 slice_bitcast_fusion
  1.6 4.5 %collective-permute-start = (bf16[16,6144]{1,0:T(8,128)(2,1)S(1)}, bf16[16,6144]{1,0:T(8,128)(2,1)S(1)}, u32[]{:S(2)}, u32[]{:S(2)}) collective-permute-start(bf16[16,6144]{1,0:T(8,128)(2,1)S(1)} %slice_bitcast_fusion), channel_id=1, source_target_pairs={{0,1},{1,2},{2,3},{3,4},{4,5},{5,6},{6,7},{7,8},{8,9},{9,10},{10,1... | collective-permute-start | bytes 589832 | tf_op jit(solution)/shard_map/ppermute | solution.py:517
  6.1 0.7 pad_maximum_fusion.gate_ref
  6.8 0.9 tables.1
  7.7 1.0 collective-permute-done.halo_ref
  8.7 2.4 %elements.3 = bf16[8,512,128]{2,1,0:T(8,128)(2,1)S(1)} custom-call(bf16[128,6144]{1,0:T(8,128)(2,1)S(1)} %bitcast.12, bf16[128,2048]{1,0:T(8,128)(2,1)S(1)} %bitcast.17, bf16[16,6144]{1,0:T(8,128)(2,1)S(1)} %collective-permute-done.halo_ref, f32[4,6144]{1,0:T(4,128)S(1)} %copy-done.5, f32[2,128,32]{2,1,0:T(8,128)S(1)} %get-tuple-element.36.column_ref), custom_call_target="tpu_custom_call" | custom-call | flops 3400000000 | bytes 12240000 | tf_op jit(solution)/shard_map/elements/pallas_call | solution.py:533
  11.1 0.1 collective-permute-start.1
  11.2 0.5 collective-permute-start.2
  11.7 2.4 %elements.2.own_ref = bf16[8,512,128]{2,1,0:T(8,128)(2,1)S(1)} custom-call(bf16[128,6144]{1,0:T(8,128)(2,1)S(1)} %bitcast.13, bf16[128,2048]{1,0:T(8,128)(2,1)S(1)} %bitcast.18, bf16[16,6144]{1,0:T(8,128)(2,1)S(1)} %collective-permute-done.halo_ref, f32[4,6144]{1,0:T(4,128)S(1)} %copy-done.5, f32[2,128,32]{2,1,0:T(8,128)S(1)} %get-tuple-element.36.column_ref), custom_call_target="tpu_custom_call" | custom-call | flops 3400000000 | bytes 12240000 | tf_op jit(solution)/shard_map/elements/pallas_call | solution.py:533
  14.0 0.0 collective-permute-done.2.other_coef_ref
  14.0 0.0 collective-permute-done.1.other_ref
  14.1 1.6 %compose.1 = bf16[16,272,128]{2,1,0:T(8,128)(2,1)} custom-call(bf16[8,512,128]{2,1,0:T(8,128)(2,1)S(1)} %elements.2.own_ref, bf16[8,512,128]{2,1,0:T(8,128)(2,1)S(1)} %collective-permute-done.1.other_ref, f32[48,128]{1,0:T(8,128)S(1)} %get-tuple-element.37.own_coef_ref, f32[48,128]{1,0:T(8,128)S(1)} %collective-permute-done.2.other_coef_ref), custom_call_target="tpu_custom_call" | custom-call | flops 1200000000 | bytes 4320000 | tf_op jit(solution)/shard_map/compose/pallas_call | solution.py:548
  15.6 7.7 %all-to-all-start = ((bf16[16,272,128]{2,1,0:T(8,128)(2,1)}), bf16[16,272,128]{2,1,0:T(8,128)(2,1)S(1)}, u32[]{:S(2)}, u32[]{:S(2)}) async-start(bf16[16,272,128]{2,1,0:T(8,128)(2,1)} %compose.1), calls=%async_computation | async-start | bytes 2228224 | tf_op jit(solution)/shard_map/all_to_all | solution.py:558
  23.4 0.0 copy-start.2
  23.4 0.0 copy-start.4
  23.4 0.8 couple.1.coupling_ref
  24.2 0.6 copy-done.2
  24.8 0.1 copy-done.4
  24.9 7.4 %inner.1 = (bf16[2,13,128,1024]{3,2,1,0:T(8,128)(2,1)S(1)}, bf16[2,2,128,1024]{3,2,1,0:T(8,128)(2,1)S(1)}) custom-call(bf16[128,6144]{1,0:T(8,128)(2,1)S(1)} %bitcast.14, bf16[128,6144]{1,0:T(8,128)(2,1)S(1)} %bitcast.15, bf16[128,6144]{1,0:T(8,128)(2,1)S(1)} %bitcast.16, bf16[128,2048]{1,0:T(8,128)(2,1)S(1)} %bitcast.19, ...), custom_call_target="tpu_custom_call" | custom-call | flops 8000000000 | bytes 28800000 | tf_op jit(solution)/shard_map/inner/pallas_call | solution.py:571
  32.3 2.8 %copy-done.6 = bf16[2,13,128,1024]{3,2,1,0:T(8,128)(2,1)} copy-done((bf16[2,13,128,1024]{3,2,1,0:T(8,128)(2,1)}, bf16[2,13,128,1024]{3,2,1,0:T(8,128)(2,1)S(1)}, u32[]{:S(2)}) %copy-start.6) | copy-done | bytes 6815768
  35.1 1.0 copy-done.16
  36.1 4.3 %all-to-all-done.got_ref = bf16[16,272,128]{2,1,0:T(8,128)(2,1)S(1)} async-done(((bf16[16,272,128]{2,1,0:T(8,128)(2,1)}), bf16[16,272,128]{2,1,0:T(8,128)(2,1)S(1)}, u32[]{:S(2)}, u32[]{:S(2)}) %all-to-all-start) | async-done | bytes 1114144 | tf_op jit(solution)/shard_map/all_to_all | solution.py:558
  40.4 0.3 scan.1
  40.7 21.7 %all_to_all.20.got_ref = bf16[16,272,128]{2,1,0:T(8,128)(2,1)S(1)} all-to-all(bf16[16,272,128]{2,1,0:T(8,128)(2,1)S(1)} %scan.1), channel_id=1, replica_groups={{0,2,4,6,8,10,12,14,16,18,20,22,24,26,28,30},{1,3,5,7,9,11,13,15,17,19,..., dimensions={0} | all-to-all | bytes 2228224 | tf_op jit(solution)/shard_map/all_to_all | solution.py:607
  62.5 0.7 spread.1
  63.2 0.0 copy-start.10
  63.2 2.0 %collective-permute-start.3 = (bf16[8,528,128]{2,1,0:T(8,128)(2,1)S(1)}, bf16[8,528,128]{2,1,0:T(8,128)(2,1)S(1)}, u32[]{:S(2)}, u32[]{:S(2)}) collective-permute-start(bf16[8,528,128]{2,1,0:T(8,128)(2,1)S(1)} %get-tuple-element.47), channel_id=1, source_target_pairs={{0,1},{1,0},{2,3},{3,2},{4,5},{5,4},{6,7},{7,6},{8,9},{9,8},{10,11... | collective-permute-start | bytes 3244040 | tf_op jit(solution)/shard_map/ppermute | solution.py:621
  65.2 2.5 %sense.2 = (bf16[1,24,128,128]{3,2,1,0:T(8,128)(2,1)S(1)}, bf16[2,16,1024]{2,1,0:T(8,128)(2,1)S(1)}, f32[96,128]{1,0:T(8,128)S(1)}, f32[32,128]{1,0:T(8,128)S(1)}) custom-call(bf16[2,13,128,1024]{3,2,1,0:T(8,128)(2,1)S(1)} %copy-done.7, bf16[16,6144]{1,0:T(8,128)(2,1)S(1)} %collective-permute-done.halo_ref, f32[4,6144]{1,0:T(4,128)S(1)} %copy-done.5, ...), custom_call_target="tpu_custom_call" | custom-call | flops 3000000000 | bytes 10800000 | tf_op jit(solution)/shard_map/sense/pallas_call | solution.py:626
  67.7 0.9 copy-done.14
  68.6 0.0 collective-permute-done.3.state_ref.other_ref
  68.6 2.4 %sense.3 = (bf16[1,24,128,128]{3,2,1,0:T(8,128)(2,1)S(1)}, bf16[2,16,1024]{2,1,0:T(8,128)(2,1)S(1)}, f32[96,128]{1,0:T(8,128)S(1)}, f32[32,128]{1,0:T(8,128)S(1)}) custom-call(bf16[2,13,128,1024]{3,2,1,0:T(8,128)(2,1)S(1)} %copy-done.7, bf16[16,6144]{1,0:T(8,128)(2,1)S(1)} %collective-permute-done.halo_ref, f32[4,6144]{1,0:T(4,128)S(1)} %copy-done.5, ...), custom_call_target="tpu_custom_call" | custom-call | flops 3000000000 | bytes 10800000 | tf_op jit(solution)/shard_map/sense/pallas_call | solution.py:626
  71.0 0.9 copy-done.12
  71.9 0.1 collective-permute-start.4
  72.0 1.1 %collective-permute-done.4.far_ref = f32[96,128]{1,0:T(8,128)S(1)} collective-permute-done((f32[96,128]{1,0:T(8,128)S(1)}, f32[96,128]{1,0:T(8,128)S(1)}, u32[]{:S(2)}, u32[]{:S(2)}) %collective-permute-start.4) | collective-permute-done | bytes 49184 | tf_op jit(solution)/shard_map/ppermute | solution.py:648
  73.2 0.8 pack.1
  74.0 3.6 %all-to-all-start.2 = ((bf16[16,96,128]{2,1,0:T(8,128)(2,1)}), bf16[16,96,128]{2,1,0:T(8,128)(2,1)S(1)}, u32[]{:S(2)}, u32[]{:S(2)}) async-start(bf16[16,96,128]{2,1,0:T(8,128)(2,1)} %pack.1), calls=%async_computation.2 | async-start | bytes 786432 | tf_op jit(solution)/shard_map/all_to_all | solution.py:715
  77.5 2.1 %collective-permute-start.5 = (bf16[2,16,1024]{2,1,0:T(8,128)(2,1)S(1)}, bf16[2,16,1024]{2,1,0:T(8,128)(2,1)S(1)}, u32[]{:S(2)}, u32[]{:S(2)}) collective-permute-start(bf16[2,16,1024]{2,1,0:T(8,128)(2,1)S(1)} %get-tuple-element.54), channel_id=1, source_target_pairs={{1,0},{2,1},{3,2},{4,3},{5,4},{6,5},{7,6},{8,7},{9,8},{10,9},{11,1... | collective-permute-start | bytes 196616 | tf_op jit(solution)/shard_map/ppermute | solution.py:654
  79.6 7.7 %all-to-all-done.2.pieces_ref = bf16[16,96,128]{2,1,0:T(8,128)(2,1)S(1)} async-done(((bf16[16,96,128]{2,1,0:T(8,128)(2,1)}), bf16[16,96,128]{2,1,0:T(8,128)(2,1)S(1)}, u32[]{:S(2)}, u32[]{:S(2)}) %all-to-all-start.2) | async-done | bytes 393248 | tf_op jit(solution)/shard_map/all_to_all | solution.py:715
  87.3 0.8 fold.1
  88.1 8.2 %all-to-all-start.3 = ((bf16[8,160,128]{2,1,0:T(8,128)(2,1)}), bf16[8,160,128]{2,1,0:T(8,128)(2,1)S(1)}, u32[]{:S(2)}, u32[]{:S(2)}) async-start(bf16[8,160,128]{2,1,0:T(8,128)(2,1)} %fold.1), calls=%async_computation.3 | async-start | bytes 655360 | tf_op jit(solution)/shard_map/all_to_all | solution.py:726
  96.3 1.2 %copy-done.17 = bf16[2,2,128,1024]{3,2,1,0:T(8,128)(2,1)S(1)} copy-done((bf16[2,2,128,1024]{3,2,1,0:T(8,128)(2,1)S(1)}, bf16[2,2,128,1024]{3,2,1,0:T(8,128)(2,1)}, u32[]{:S(2)}) %copy-start.17) | copy-done | bytes 1048600
  97.5 1.6 %readout.1 = bf16[128,2048]{1,0:T(8,128)(2,1)} custom-call(s32[1]{0:T(128)} %bitcast.6.place_ref, bf16[2,2,128,1024]{3,2,1,0:T(8,128)(2,1)S(1)} %copy-done.17, f32[2,128,32]{2,1,0:T(8,128)S(1)} %copy-done.20, bf16[8,528,128]{2,1,0:T(8,128)(2,1)S(1)} %copy-done.11, bf16[8,528,128]{2,1,0:T(8,128)(2,1)S(1)} %collective-permute-done.3.state_ref.other_ref), custom_call_target="tpu_custom_call" | custom-call | flops 3000000000 | bytes 10800000 | tf_op jit(solution)/shard_map/readout/pallas_call | solution.py:663
  99.1 0.0 collective-permute-done.5.rim_own_ref.rim_other_ref
  99.1 3.2 %unroll.1 = bf16[128,6144]{1,0:T(8,128)(2,1)} custom-call(s32[1]{0:T(128)} %bitcast.6.place_ref, bf16[1,24,128,128]{3,2,1,0:T(8,128)(2,1)S(1)} %copy-done.15, bf16[1,24,128,128]{3,2,1,0:T(8,128)(2,1)S(1)} %copy-done.13, f32[4,6144]{1,0:T(4,128)S(1)} %copy-done.5, bf16[2,16,1024]{2,1,0:T(8,128)(2,1)S(1)} %collective-permute-done.5.rim_own_ref.rim_other_ref, ...), custom_call_target="tpu_custom_call" | custom-call | flops 4000000000 | bytes 14400000 | tf_op jit(solution)/shard_map/unroll/pallas_call | solution.py:683
  102.3 5.2 %all-to-all-done.3.pieces_ref = bf16[8,160,128]{2,1,0:T(8,128)(2,1)S(1)} async-done(((bf16[8,160,128]{2,1,0:T(8,128)(2,1)}), bf16[8,160,128]{2,1,0:T(8,128)(2,1)S(1)}, u32[]{:S(2)}, u32[]{:S(2)}) %all-to-all-start.3) | async-done | bytes 327712 | tf_op jit(solution)/shard_map/all_to_all | solution.py:726
  107.5 3.2 %collective-permute-start.6 = (f32[160,128]{1,0:T(8,128)S(1)}, f32[160,128]{1,0:T(8,128)S(1)}, u32[]{:S(2)}, u32[]{:S(2)}) collective-permute-start(f32[160,128]{1,0:T(8,128)S(1)} %total.1.own_ref), channel_id=1, source_target_pairs={{0,1},{1,0},{2,3},{3,2},{4,5},{5,4},{6,7},{7,6},{8,9},{9,8},{10,11... | collective-permute-start | bytes 245768 | tf_op jit(solution)/shard_map/ppermute | solution.py:738
  110.6 0.9 collective-permute-done.6.other_ref
  111.6 0.7 assemble.1
  (33 shorter events, 0.1 us)
Async XLA Ops:
  1.6 7.1 %collective-permute-start = (bf16[16,6144]{1,0:T(8,128)(2,1)S(1)}, bf16[16,6144]{1,0:T(8,128)(2,1)S(1)}, u32[]{:S(2)}, u32[]{:S(2)}) collective-permute-start(bf16[16,6144]{1,0:T(8,128)(2,1)S(1)} %slice_bitcast_fusion), channel_id=1, source_target_pairs={{0,1},{1,2},{2,3},{3,4},{4,5},{5,6},{6,7},{7,8},{8,9},{9,10},{10,1... | collective-permute-start | bytes 589832 | tf_op jit(solution)/shard_map/ppermute | solution.py:517
  6.8 1.9 %copy-start.1 = (bf16[1,128,6144]{2,1,0:T(8,128)(2,1)S(1)}, bf16[1,128,6144]{2,1,0:T(8,128)(2,1)}, u32[]{:S(2)}) copy-start(bf16[1,128,6144]{2,1,0:T(8,128)(2,1)} %param.7) | copy-start | bytes 4718596
  6.8 1.9 %copy-start.3 = (bf16[1,128,2048]{2,1,0:T(8,128)(2,1)S(1)}, bf16[1,128,2048]{2,1,0:T(8,128)(2,1)}, u32[]{:S(2)}) copy-start(bf16[1,128,2048]{2,1,0:T(8,128)(2,1)} %param.13) | copy-start | bytes 1572868
  6.8 1.9 %copy-start.5 = (f32[4,6144]{1,0:T(4,128)S(1)}, f32[4,6144]{1,0:T(4,128)}, u32[]{:S(2)}) copy-start(f32[4,6144]{1,0:T(4,128)} %weight_ref.11) | copy-start | bytes 294916
  7.7 3.9 %copy-start.18 = (f32[2,128,32]{2,1,0:T(8,128)}, f32[2,128,32]{2,1,0:T(8,128)S(1)}, u32[]{:S(2)}) copy-start(f32[2,128,32]{2,1,0:T(8,128)S(1)} %get-tuple-element.36.column_ref) | copy-start | bytes 98308
  11.1 3.0 %collective-permute-start.1 = (bf16[8,512,128]{2,1,0:T(8,128)(2,1)S(1)}, bf16[8,512,128]{2,1,0:T(8,128)(2,1)S(1)}, u32[]{:S(2)}, u32[]{:S(2)}) collective-permute-start(bf16[8,512,128]{2,1,0:T(8,128)(2,1)S(1)} %elements.3), channel_id=1, source_target_pairs={{0,1},{1,0},{2,3},{3,2},{4,5},{5,4},{6,7},{7,6},{8,9},{9,8},{10,11... | collective-permute-start | bytes 3145736 | tf_op jit(solution)/shard_map/ppermute | solution.py:545
  11.2 2.9 %collective-permute-start.2 = (f32[48,128]{1,0:T(8,128)S(1)}, f32[48,128]{1,0:T(8,128)S(1)}, u32[]{:S(2)}, u32[]{:S(2)}) collective-permute-start(f32[48,128]{1,0:T(8,128)S(1)} %get-tuple-element.37.own_coef_ref), channel_id=1, source_target_pairs={{0,1},{1,0},{2,3},{3,2},{4,5},{5,4},{6,7},{7,6},{8,9},{9,8},{10,11... | collective-permute-start | bytes 73736 | tf_op jit(solution)/shard_map/ppermute | solution.py:530
  14.0 1.6 %copy-start.8 = (bf16[8,512,128]{2,1,0:T(8,128)(2,1)}, bf16[8,512,128]{2,1,0:T(8,128)(2,1)S(1)}, u32[]{:S(2)}) copy-start(bf16[8,512,128]{2,1,0:T(8,128)(2,1)S(1)} %elements.2.own_ref) | copy-start | bytes 3145732
  15.6 24.7 %all-to-all-start = ((bf16[16,272,128]{2,1,0:T(8,128)(2,1)}), bf16[16,272,128]{2,1,0:T(8,128)(2,1)S(1)}, u32[]{:S(2)}, u32[]{:S(2)}) async-start(bf16[16,272,128]{2,1,0:T(8,128)(2,1)} %compose.1), calls=%async_computation | async-start | bytes 2228224 | tf_op jit(solution)/shard_map/all_to_all | solution.py:558
  23.4 1.4 %copy-start.2 = (bf16[1,128,6144]{2,1,0:T(8,128)(2,1)S(1)}, bf16[1,128,6144]{2,1,0:T(8,128)(2,1)}, u32[]{:S(2)}) copy-start(bf16[1,128,6144]{2,1,0:T(8,128)(2,1)} %param.7) | copy-start | bytes 4718596
  23.4 1.5 %copy-start.4 = (bf16[1,128,2048]{2,1,0:T(8,128)(2,1)S(1)}, bf16[1,128,2048]{2,1,0:T(8,128)(2,1)}, u32[]{:S(2)}) copy-start(bf16[1,128,2048]{2,1,0:T(8,128)(2,1)} %param.13) | copy-start | bytes 1572868
  24.9 15.5 %copy-start = (f32[16,128,128]{2,1,0:T(8,128)S(1)}, f32[16,128,128]{2,1,0:T(8,128)}, u32[]{:S(2)}) copy-start(f32[16,128,128]{2,1,0:T(8,128)} %param.9) | copy-start | bytes 3145732
  32.3 2.8 %copy-start.6 = (bf16[2,13,128,1024]{3,2,1,0:T(8,128)(2,1)}, bf16[2,13,128,1024]{3,2,1,0:T(8,128)(2,1)S(1)}, u32[]{:S(2)}) copy-start(bf16[2,13,128,1024]{3,2,1,0:T(8,128)(2,1)S(1)} %get-tuple-element.43.in_ref) | copy-start | bytes 20447236
  35.1 1.0 copy-start.16
  40.4 22.1 %copy-start.9 = (bf16[8,512,128]{2,1,0:T(8,128)(2,1)S(1)}, bf16[8,512,128]{2,1,0:T(8,128)(2,1)}, u32[]{:S(2)}) copy-start(bf16[8,512,128]{2,1,0:T(8,128)(2,1)} %copy-done.8) | copy-start | bytes 3145732
  40.7 24.5 %copy-start.7 = (bf16[2,13,128,1024]{3,2,1,0:T(8,128)(2,1)S(1)}, bf16[2,13,128,1024]{3,2,1,0:T(8,128)(2,1)}, u32[]{:S(2)}) copy-start(bf16[2,13,128,1024]{3,2,1,0:T(8,128)(2,1)} %copy-done.6) | copy-start | bytes 20447236
  62.5 2.7 %copy-start.19 = (f32[2,128,32]{2,1,0:T(8,128)S(1)}, f32[2,128,32]{2,1,0:T(8,128)}, u32[]{:S(2)}) copy-start(f32[2,128,32]{2,1,0:T(8,128)} %copy-done.18) | copy-start | bytes 98308
  63.2 4.5 %copy-start.10 = (bf16[8,528,128]{2,1,0:T(8,128)(2,1)}, bf16[8,528,128]{2,1,0:T(8,128)(2,1)S(1)}, u32[]{:S(2)}) copy-start(bf16[8,528,128]{2,1,0:T(8,128)(2,1)S(1)} %get-tuple-element.45.state_ref.own_ref) | copy-start | bytes 3244036
  63.2 5.4 %collective-permute-start.3 = (bf16[8,528,128]{2,1,0:T(8,128)(2,1)S(1)}, bf16[8,528,128]{2,1,0:T(8,128)(2,1)S(1)}, u32[]{:S(2)}, u32[]{:S(2)}) collective-permute-start(bf16[8,528,128]{2,1,0:T(8,128)(2,1)S(1)} %get-tuple-element.47), channel_id=1, source_target_pairs={{0,1},{1,0},{2,3},{3,2},{4,5},{5,4},{6,7},{7,6},{8,9},{9,8},{10,11... | collective-permute-start | bytes 3244040 | tf_op jit(solution)/shard_map/ppermute | solution.py:621
  67.7 0.9 copy-start.14
  71.0 0.9 copy-start.12
  71.9 1.2 %collective-permute-start.4 = (f32[96,128]{1,0:T(8,128)S(1)}, f32[96,128]{1,0:T(8,128)S(1)}, u32[]{:S(2)}, u32[]{:S(2)}) collective-permute-start(f32[96,128]{1,0:T(8,128)S(1)} %get-tuple-element.49), channel_id=1, source_target_pairs={{0,1},{1,0},{2,3},{3,2},{4,5},{5,4},{6,7},{7,6},{8,9},{9,8},{10,11... | collective-permute-start | bytes 147464 | tf_op jit(solution)/shard_map/ppermute | solution.py:648
  74.0 13.3 %all-to-all-start.2 = ((bf16[16,96,128]{2,1,0:T(8,128)(2,1)}), bf16[16,96,128]{2,1,0:T(8,128)(2,1)S(1)}, u32[]{:S(2)}, u32[]{:S(2)}) async-start(bf16[16,96,128]{2,1,0:T(8,128)(2,1)} %pack.1), calls=%async_computation.2 | async-start | bytes 786432 | tf_op jit(solution)/shard_map/all_to_all | solution.py:715
  77.5 21.6 %collective-permute-start.5 = (bf16[2,16,1024]{2,1,0:T(8,128)(2,1)S(1)}, bf16[2,16,1024]{2,1,0:T(8,128)(2,1)S(1)}, u32[]{:S(2)}, u32[]{:S(2)}) collective-permute-start(bf16[2,16,1024]{2,1,0:T(8,128)(2,1)S(1)} %get-tuple-element.54), channel_id=1, source_target_pairs={{1,0},{2,1},{3,2},{4,3},{5,4},{6,5},{7,6},{8,7},{9,8},{10,9},{11,1... | collective-permute-start | bytes 196616 | tf_op jit(solution)/shard_map/ppermute | solution.py:654
  87.3 9.0 %copy-start.11 = (bf16[8,528,128]{2,1,0:T(8,128)(2,1)S(1)}, bf16[8,528,128]{2,1,0:T(8,128)(2,1)}, u32[]{:S(2)}) copy-start(bf16[8,528,128]{2,1,0:T(8,128)(2,1)} %copy-done.10) | copy-start | bytes 3244036
  87.3 9.0 %copy-start.20 = (f32[2,128,32]{2,1,0:T(8,128)S(1)}, f32[2,128,32]{2,1,0:T(8,128)}, u32[]{:S(2)}) copy-start(f32[2,128,32]{2,1,0:T(8,128)} %copy-done.18) | copy-start | bytes 98308
  88.1 19.3 %all-to-all-start.3 = ((bf16[8,160,128]{2,1,0:T(8,128)(2,1)}), bf16[8,160,128]{2,1,0:T(8,128)(2,1)S(1)}, u32[]{:S(2)}, u32[]{:S(2)}) async-start(bf16[8,160,128]{2,1,0:T(8,128)(2,1)} %fold.1), calls=%async_computation.3 | async-start | bytes 655360 | tf_op jit(solution)/shard_map/all_to_all | solution.py:726
  96.3 1.2 %copy-start.17 = (bf16[2,2,128,1024]{3,2,1,0:T(8,128)(2,1)S(1)}, bf16[2,2,128,1024]{3,2,1,0:T(8,128)(2,1)}, u32[]{:S(2)}) copy-start(bf16[2,2,128,1024]{3,2,1,0:T(8,128)(2,1)} %copy-done.16) | copy-start | bytes 3145732
  97.5 1.6 %copy-start.13 = (bf16[1,24,128,128]{3,2,1,0:T(8,128)(2,1)S(1)}, bf16[1,24,128,128]{3,2,1,0:T(8,128)(2,1)}, u32[]{:S(2)}) copy-start(bf16[1,24,128,128]{3,2,1,0:T(8,128)(2,1)} %copy-done.12) | copy-start | bytes 2359300
  97.5 1.6 %copy-start.15 = (bf16[1,24,128,128]{3,2,1,0:T(8,128)(2,1)S(1)}, bf16[1,24,128,128]{3,2,1,0:T(8,128)(2,1)}, u32[]{:S(2)}) copy-start(bf16[1,24,128,128]{3,2,1,0:T(8,128)(2,1)} %copy-done.14) | copy-start | bytes 2359300
  107.5 4.1 %collective-permute-start.6 = (f32[160,128]{1,0:T(8,128)S(1)}, f32[160,128]{1,0:T(8,128)S(1)}, u32[]{:S(2)}, u32[]{:S(2)}) collective-permute-start(f32[160,128]{1,0:T(8,128)S(1)} %total.1.own_ref), channel_id=1, source_target_pairs={{0,1},{1,0},{2,3},{3,2},{4,5},{5,4},{6,7},{7,6},{8,9},{9,8},{10,11... | collective-permute-start | bytes 245768 | tf_op jit(solution)/shard_map/ppermute | solution.py:738

commit v6 on v5

--- a/solution.py
+++ b/solution.py
@@ -94,7 +94,7 @@
             decay = jnp.exp(jnp.minimum(to_column(row, eye) - row, 0.0))
             maps.append(jnp.where(causal, decay, 0.0).astype(BF))
         rated = dot(maps[0], maps[1], (1, 0)) * gate_ref[2 * heads + h : 2 * heads + h + 1, :]
-        coupling_ref[h] = rated.astype(BF)
+        coupling_ref[h] = rated
 
 
 def extend(ext_ref, slot, halo, own):
@@ -312,7 +312,7 @@
         query, key, value = made
         upstream = u_ref[:, cols]
         out_ref[0, 3, :, cols] = upstream
-        coupling = coupling_ref[side].astype(F32)
+        coupling = coupling_ref[side]
         scores = (dot(query, key, (1, 1)) * coupling).astype(BF)
         sense = (dot(upstream, value, (1, 1)) * coupling).astype(BF)
         grads = (
@@ -559,7 +559,7 @@
 
     coupling = pl.pallas_call(
         couple_kernel,
-        out_shape=shape((heads, tokens, tokens), BF),
+        out_shape=shape((heads, tokens, tokens), F32),
         compiler_params=SHARED,
         name="couple",
         cost_estimate=pl.CostEstimate(flops=3500000000, transcendentals=0, bytes_accessed=12600000),

time: 113 us -> 113 us (level)
  no operation moved by 1% of the time
where the time goes in v6:
time: 113 us; the launch traced here: 112 us
  starting transfers between devices  31.9 us (28%)
  Pallas kernels  28.2 us (25%)
  blocking collectives  21.7 us (19%)
  waiting for transfers between devices  20.2 us (18%)
  local copies, waits for them, and re-layouts  8.49 us (8%)
    all_to_all x1, blocking collectives, local(): states = lax.all_to_all(back, 'seq', 0, 0, axis_index_groups=groups)  21.7 us
    all_to_all x1, starting transfers between devices, local(): pieces = lax.all_to_all(spread_sums, 'dp', 0, 0)  8.18 us
    all_to_all x1, starting transfers between devices, local(): got = lax.all_to_all(payload, 'seq', 0, 0, axis_index_groups=groups)  7.74 us
    all_to_all x1, waiting for transfers between devices, local(): pieces = lax.all_to_all(spread_taps, 'seq', 0, 0, axis_index_groups=groups)  7.71 us
    unnamed x42, local copies, waits for them, and re-layouts  7.55 us
    pallas_call x1, Pallas kernels, local(): pl.pallas_call(inner_kernel, out_shape=(shape((blocks, 13, tokens, width)...  7.34 us
    all_to_all x1, waiting for transfers between devices, local(): pieces = lax.all_to_all(spread_sums, 'dp', 0, 0)  5.15 us
    pallas_call x2, Pallas kernels, sense(): pl.pallas_call(functools.partial(sense_kernel, mine), out_shape=(shape((h...  4.91 us
  transfers between devices with their start and end apart: 10, of which 6 were waited for; matrix products, arithmetic and copies ran while one was open for 1% of the time, Pallas kernels for 17%

profile of v6, /device:TPU:1, one launch (start us, length us, event | category | flops | bytes accessed | tf_op | source)
XLA Modules:
  0.0 112.2 jit_solution(10314237319026349031)
XLA Ops:
  0.6 0.9 slice_bitcast_fusion
  1.6 4.5 %collective-permute-start = (bf16[16,6144]{1,0:T(8,128)(2,1)S(1)}, bf16[16,6144]{1,0:T(8,128)(2,1)S(1)}, u32[]{:S(2)}, u32[]{:S(2)}) collective-permute-start(bf16[16,6144]{1,0:T(8,128)(2,1)S(1)} %slice_bitcast_fusion), channel_id=1, source_target_pairs={{0,1},{1,2},{2,3},{3,4},{4,5},{5,6},{6,7},{7,8},{8,9},{9,10},{10,1... | collective-permute-start | bytes 589832 | tf_op jit(solution)/shard_map/ppermute | solution.py:517
  6.1 0.7 pad_maximum_fusion.gate_ref
  6.8 0.9 tables.1
  7.7 1.0 collective-permute-done.halo_ref
  8.7 2.4 %elements.3 = bf16[8,512,128]{2,1,0:T(8,128)(2,1)S(1)} custom-call(bf16[128,6144]{1,0:T(8,128)(2,1)S(1)} %bitcast.12, bf16[128,2048]{1,0:T(8,128)(2,1)S(1)} %bitcast.17, bf16[16,6144]{1,0:T(8,128)(2,1)S(1)} %collective-permute-done.halo_ref, f32[4,6144]{1,0:T(4,128)S(1)} %copy-done.5, f32[2,128,32]{2,1,0:T(8,128)S(1)} %get-tuple-element.36.column_ref), custom_call_target="tpu_custom_call" | custom-call | flops 3400000000 | bytes 12240000 | tf_op jit(solution)/shard_map/elements/pallas_call | solution.py:533
  11.1 0.1 collective-permute-start.1
  11.2 0.5 collective-permute-start.2
  11.7 2.4 %elements.2.own_ref = bf16[8,512,128]{2,1,0:T(8,128)(2,1)S(1)} custom-call(bf16[128,6144]{1,0:T(8,128)(2,1)S(1)} %bitcast.13, bf16[128,2048]{1,0:T(8,128)(2,1)S(1)} %bitcast.18, bf16[16,6144]{1,0:T(8,128)(2,1)S(1)} %collective-permute-done.halo_ref, f32[4,6144]{1,0:T(4,128)S(1)} %copy-done.5, f32[2,128,32]{2,1,0:T(8,128)S(1)} %get-tuple-element.36.column_ref), custom_call_target="tpu_custom_call" | custom-call | flops 3400000000 | bytes 12240000 | tf_op jit(solution)/shard_map/elements/pallas_call | solution.py:533
  14.0 0.0 collective-permute-done.2.other_coef_ref
  14.0 0.0 collective-permute-done.1.other_ref
  14.1 1.6 %compose.1 = bf16[16,272,128]{2,1,0:T(8,128)(2,1)} custom-call(bf16[8,512,128]{2,1,0:T(8,128)(2,1)S(1)} %elements.2.own_ref, bf16[8,512,128]{2,1,0:T(8,128)(2,1)S(1)} %collective-permute-done.1.other_ref, f32[48,128]{1,0:T(8,128)S(1)} %get-tuple-element.37.own_coef_ref, f32[48,128]{1,0:T(8,128)S(1)} %collective-permute-done.2.other_coef_ref), custom_call_target="tpu_custom_call" | custom-call | flops 1200000000 | bytes 4320000 | tf_op jit(solution)/shard_map/compose/pallas_call | solution.py:548
  15.6 7.7 %all-to-all-start = ((bf16[16,272,128]{2,1,0:T(8,128)(2,1)}), bf16[16,272,128]{2,1,0:T(8,128)(2,1)S(1)}, u32[]{:S(2)}, u32[]{:S(2)}) async-start(bf16[16,272,128]{2,1,0:T(8,128)(2,1)} %compose.1), calls=%async_computation | async-start | bytes 2228224 | tf_op jit(solution)/shard_map/all_to_all | solution.py:558
  23.4 0.0 copy-start.2
  23.4 0.0 copy-start.4
  23.4 0.8 couple.1.coupling_ref
  24.2 0.6 copy-done.2
  24.8 0.1 copy-done.4
  24.9 7.3 %inner.1 = (bf16[2,13,128,1024]{3,2,1,0:T(8,128)(2,1)S(1)}, bf16[2,2,128,1024]{3,2,1,0:T(8,128)(2,1)S(1)}) custom-call(bf16[128,6144]{1,0:T(8,128)(2,1)S(1)} %bitcast.14, bf16[128,6144]{1,0:T(8,128)(2,1)S(1)} %bitcast.15, bf16[128,6144]{1,0:T(8,128)(2,1)S(1)} %bitcast.16, bf16[128,2048]{1,0:T(8,128)(2,1)S(1)} %bitcast.19, ...), custom_call_target="tpu_custom_call" | custom-call | flops 8000000000 | bytes 28800000 | tf_op jit(solution)/shard_map/inner/pallas_call | solution.py:571
  32.3 2.8 %copy-done.6 = bf16[2,13,128,1024]{3,2,1,0:T(8,128)(2,1)} copy-done((bf16[2,13,128,1024]{3,2,1,0:T(8,128)(2,1)}, bf16[2,13,128,1024]{3,2,1,0:T(8,128)(2,1)S(1)}, u32[]{:S(2)}) %copy-start.6) | copy-done | bytes 6815768
  35.0 1.0 copy-done.16
  36.0 4.3 %all-to-all-done.got_ref = bf16[16,272,128]{2,1,0:T(8,128)(2,1)S(1)} async-done(((bf16[16,272,128]{2,1,0:T(8,128)(2,1)}), bf16[16,272,128]{2,1,0:T(8,128)(2,1)S(1)}, u32[]{:S(2)}, u32[]{:S(2)}) %all-to-all-start) | async-done | bytes 1114144 | tf_op jit(solution)/shard_map/all_to_all | solution.py:558
  40.4 0.3 scan.1
  40.7 21.7 %all_to_all.20.got_ref = bf16[16,272,128]{2,1,0:T(8,128)(2,1)S(1)} all-to-all(bf16[16,272,128]{2,1,0:T(8,128)(2,1)S(1)} %scan.1), channel_id=1, replica_groups={{0,2,4,6,8,10,12,14,16,18,20,22,24,26,28,30},{1,3,5,7,9,11,13,15,17,19,..., dimensions={0} | all-to-all | bytes 2228224 | tf_op jit(solution)/shard_map/all_to_all | solution.py:607
  62.5 0.7 spread.1
  63.2 0.0 copy-start.10
  63.2 2.0 %collective-permute-start.3 = (bf16[8,528,128]{2,1,0:T(8,128)(2,1)S(1)}, bf16[8,528,128]{2,1,0:T(8,128)(2,1)S(1)}, u32[]{:S(2)}, u32[]{:S(2)}) collective-permute-start(bf16[8,528,128]{2,1,0:T(8,128)(2,1)S(1)} %get-tuple-element.47), channel_id=1, source_target_pairs={{0,1},{1,0},{2,3},{3,2},{4,5},{5,4},{6,7},{7,6},{8,9},{9,8},{10,11... | collective-permute-start | bytes 3244040 | tf_op jit(solution)/shard_map/ppermute | solution.py:621
  65.2 2.5 %sense.2 = (bf16[1,24,128,128]{3,2,1,0:T(8,128)(2,1)S(1)}, bf16[2,16,1024]{2,1,0:T(8,128)(2,1)S(1)}, f32[96,128]{1,0:T(8,128)S(1)}, f32[32,128]{1,0:T(8,128)S(1)}) custom-call(bf16[2,13,128,1024]{3,2,1,0:T(8,128)(2,1)S(1)} %copy-done.7, bf16[16,6144]{1,0:T(8,128)(2,1)S(1)} %collective-permute-done.halo_ref, f32[4,6144]{1,0:T(4,128)S(1)} %copy-done.5, ...), custom_call_target="tpu_custom_call" | custom-call | flops 3000000000 | bytes 10800000 | tf_op jit(solution)/shard_map/sense/pallas_call | solution.py:626
  67.7 0.9 copy-done.14
  68.6 0.0 collective-permute-done.3.state_ref.other_ref
  68.6 2.4 %sense.3 = (bf16[1,24,128,128]{3,2,1,0:T(8,128)(2,1)S(1)}, bf16[2,16,1024]{2,1,0:T(8,128)(2,1)S(1)}, f32[96,128]{1,0:T(8,128)S(1)}, f32[32,128]{1,0:T(8,128)S(1)}) custom-call(bf16[2,13,128,1024]{3,2,1,0:T(8,128)(2,1)S(1)} %copy-done.7, bf16[16,6144]{1,0:T(8,128)(2,1)S(1)} %collective-permute-done.halo_ref, f32[4,6144]{1,0:T(4,128)S(1)} %copy-done.5, ...), custom_call_target="tpu_custom_call" | custom-call | flops 3000000000 | bytes 10800000 | tf_op jit(solution)/shard_map/sense/pallas_call | solution.py:626
  71.0 0.9 copy-done.12
  71.9 0.1 collective-permute-start.4
  72.0 1.1 %collective-permute-done.4.far_ref = f32[96,128]{1,0:T(8,128)S(1)} collective-permute-done((f32[96,128]{1,0:T(8,128)S(1)}, f32[96,128]{1,0:T(8,128)S(1)}, u32[]{:S(2)}, u32[]{:S(2)}) %collective-permute-start.4) | collective-permute-done | bytes 49184 | tf_op jit(solution)/shard_map/ppermute | solution.py:648
  73.2 0.8 pack.1
  74.0 3.6 %all-to-all-start.2 = ((bf16[16,96,128]{2,1,0:T(8,128)(2,1)}), bf16[16,96,128]{2,1,0:T(8,128)(2,1)S(1)}, u32[]{:S(2)}, u32[]{:S(2)}) async-start(bf16[16,96,128]{2,1,0:T(8,128)(2,1)} %pack.1), calls=%async_computation.2 | async-start | bytes 786432 | tf_op jit(solution)/shard_map/all_to_all | solution.py:715
  77.5 2.1 %collective-permute-start.5 = (bf16[2,16,1024]{2,1,0:T(8,128)(2,1)S(1)}, bf16[2,16,1024]{2,1,0:T(8,128)(2,1)S(1)}, u32[]{:S(2)}, u32[]{:S(2)}) collective-permute-start(bf16[2,16,1024]{2,1,0:T(8,128)(2,1)S(1)} %get-tuple-element.54), channel_id=1, source_target_pairs={{1,0},{2,1},{3,2},{4,3},{5,4},{6,5},{7,6},{8,7},{9,8},{10,9},{11,1... | collective-permute-start | bytes 196616 | tf_op jit(solution)/shard_map/ppermute | solution.py:654
  79.6 7.7 %all-to-all-done.2.pieces_ref = bf16[16,96,128]{2,1,0:T(8,128)(2,1)S(1)} async-done(((bf16[16,96,128]{2,1,0:T(8,128)(2,1)}), bf16[16,96,128]{2,1,0:T(8,128)(2,1)S(1)}, u32[]{:S(2)}, u32[]{:S(2)}) %all-to-all-start.2) | async-done | bytes 393248 | tf_op jit(solution)/shard_map/all_to_all | solution.py:715
  87.3 0.8 fold.1
  88.1 8.2 %all-to-all-start.3 = ((bf16[8,160,128]{2,1,0:T(8,128)(2,1)}), bf16[8,160,128]{2,1,0:T(8,128)(2,1)S(1)}, u32[]{:S(2)}, u32[]{:S(2)}) async-start(bf16[8,160,128]{2,1,0:T(8,128)(2,1)} %fold.1), calls=%async_computation.3 | async-start | bytes 655360 | tf_op jit(solution)/shard_map/all_to_all | solution.py:726
  96.3 1.2 %copy-done.17 = bf16[2,2,128,1024]{3,2,1,0:T(8,128)(2,1)S(1)} copy-done((bf16[2,2,128,1024]{3,2,1,0:T(8,128)(2,1)S(1)}, bf16[2,2,128,1024]{3,2,1,0:T(8,128)(2,1)}, u32[]{:S(2)}) %copy-start.17) | copy-done | bytes 1048600
  97.5 1.6 %readout.1 = bf16[128,2048]{1,0:T(8,128)(2,1)} custom-call(s32[1]{0:T(128)} %bitcast.6.place_ref, bf16[2,2,128,1024]{3,2,1,0:T(8,128)(2,1)S(1)} %copy-done.17, f32[2,128,32]{2,1,0:T(8,128)S(1)} %copy-done.20, bf16[8,528,128]{2,1,0:T(8,128)(2,1)S(1)} %copy-done.11, bf16[8,528,128]{2,1,0:T(8,128)(2,1)S(1)} %collective-permute-done.3.state_ref.other_ref), custom_call_target="tpu_custom_call" | custom-call | flops 3000000000 | bytes 10800000 | tf_op jit(solution)/shard_map/readout/pallas_call | solution.py:663
  99.1 0.0 collective-permute-done.5.rim_own_ref.rim_other_ref
  99.1 3.2 %unroll.1 = bf16[128,6144]{1,0:T(8,128)(2,1)} custom-call(s32[1]{0:T(128)} %bitcast.6.place_ref, bf16[1,24,128,128]{3,2,1,0:T(8,128)(2,1)S(1)} %copy-done.15, bf16[1,24,128,128]{3,2,1,0:T(8,128)(2,1)S(1)} %copy-done.13, f32[4,6144]{1,0:T(4,128)S(1)} %copy-done.5, bf16[2,16,1024]{2,1,0:T(8,128)(2,1)S(1)} %collective-permute-done.5.rim_own_ref.rim_other_ref, ...), custom_call_target="tpu_custom_call" | custom-call | flops 4000000000 | bytes 14400000 | tf_op jit(solution)/shard_map/unroll/pallas_call | solution.py:683
  102.3 5.2 %all-to-all-done.3.pieces_ref = bf16[8,160,128]{2,1,0:T(8,128)(2,1)S(1)} async-done(((bf16[8,160,128]{2,1,0:T(8,128)(2,1)}), bf16[8,160,128]{2,1,0:T(8,128)(2,1)S(1)}, u32[]{:S(2)}, u32[]{:S(2)}) %all-to-all-start.3) | async-done | bytes 327712 | tf_op jit(solution)/shard_map/all_to_all | solution.py:726
  107.5 3.2 %collective-permute-start.6 = (f32[160,128]{1,0:T(8,128)S(1)}, f32[160,128]{1,0:T(8,128)S(1)}, u32[]{:S(2)}, u32[]{:S(2)}) collective-permute-start(f32[160,128]{1,0:T(8,128)S(1)} %total.1.own_ref), channel_id=1, source_target_pairs={{0,1},{1,0},{2,3},{3,2},{4,5},{5,4},{6,7},{7,6},{8,9},{9,8},{10,11... | collective-permute-start | bytes 245768 | tf_op jit(solution)/shard_map/ppermute | solution.py:738
  110.6 0.9 collective-permute-done.6.other_ref
  111.6 0.7 assemble.1
  (33 shorter events, 0.1 us)
Async XLA Ops:
  1.6 7.1 %collective-permute-start = (bf16[16,6144]{1,0:T(8,128)(2,1)S(1)}, bf16[16,6144]{1,0:T(8,128)(2,1)S(1)}, u32[]{:S(2)}, u32[]{:S(2)}) collective-permute-start(bf16[16,6144]{1,0:T(8,128)(2,1)S(1)} %slice_bitcast_fusion), channel_id=1, source_target_pairs={{0,1},{1,2},{2,3},{3,4},{4,5},{5,6},{6,7},{7,8},{8,9},{9,10},{10,1... | collective-permute-start | bytes 589832 | tf_op jit(solution)/shard_map/ppermute | solution.py:517
  6.8 1.9 %copy-start.1 = (bf16[1,128,6144]{2,1,0:T(8,128)(2,1)S(1)}, bf16[1,128,6144]{2,1,0:T(8,128)(2,1)}, u32[]{:S(2)}) copy-start(bf16[1,128,6144]{2,1,0:T(8,128)(2,1)} %param.7) | copy-start | bytes 4718596
  6.8 1.9 %copy-start.3 = (bf16[1,128,2048]{2,1,0:T(8,128)(2,1)S(1)}, bf16[1,128,2048]{2,1,0:T(8,128)(2,1)}, u32[]{:S(2)}) copy-start(bf16[1,128,2048]{2,1,0:T(8,128)(2,1)} %param.13) | copy-start | bytes 1572868
  6.8 1.9 %copy-start.5 = (f32[4,6144]{1,0:T(4,128)S(1)}, f32[4,6144]{1,0:T(4,128)}, u32[]{:S(2)}) copy-start(f32[4,6144]{1,0:T(4,128)} %weight_ref.11) | copy-start | bytes 294916
  7.7 3.9 %copy-start.18 = (f32[2,128,32]{2,1,0:T(8,128)}, f32[2,128,32]{2,1,0:T(8,128)S(1)}, u32[]{:S(2)}) copy-start(f32[2,128,32]{2,1,0:T(8,128)S(1)} %get-tuple-element.36.column_ref) | copy-start | bytes 98308
  11.1 3.0 %collective-permute-start.1 = (bf16[8,512,128]{2,1,0:T(8,128)(2,1)S(1)}, bf16[8,512,128]{2,1,0:T(8,128)(2,1)S(1)}, u32[]{:S(2)}, u32[]{:S(2)}) collective-permute-start(bf16[8,512,128]{2,1,0:T(8,128)(2,1)S(1)} %elements.3), channel_id=1, source_target_pairs={{0,1},{1,0},{2,3},{3,2},{4,5},{5,4},{6,7},{7,6},{8,9},{9,8},{10,11... | collective-permute-start | bytes 3145736 | tf_op jit(solution)/shard_map/ppermute | solution.py:545
  11.2 2.9 %collective-permute-start.2 = (f32[48,128]{1,0:T(8,128)S(1)}, f32[48,128]{1,0:T(8,128)S(1)}, u32[]{:S(2)}, u32[]{:S(2)}) collective-permute-start(f32[48,128]{1,0:T(8,128)S(1)} %get-tuple-element.37.own_coef_ref), channel_id=1, source_target_pairs={{0,1},{1,0},{2,3},{3,2},{4,5},{5,4},{6,7},{7,6},{8,9},{9,8},{10,11... | collective-permute-start | bytes 73736 | tf_op jit(solution)/shard_map/ppermute | solution.py:530
  14.0 1.6 %copy-start.8 = (bf16[8,512,128]{2,1,0:T(8,128)(2,1)}, bf16[8,512,128]{2,1,0:T(8,128)(2,1)S(1)}, u32[]{:S(2)}) copy-start(bf16[8,512,128]{2,1,0:T(8,128)(2,1)S(1)} %elements.2.own_ref) | copy-start | bytes 3145732
  15.6 24.7 %all-to-all-start = ((bf16[16,272,128]{2,1,0:T(8,128)(2,1)}), bf16[16,272,128]{2,1,0:T(8,128)(2,1)S(1)}, u32[]{:S(2)}, u32[]{:S(2)}) async-start(bf16[16,272,128]{2,1,0:T(8,128)(2,1)} %compose.1), calls=%async_computation | async-start | bytes 2228224 | tf_op jit(solution)/shard_map/all_to_all | solution.py:558
  23.4 1.4 %copy-start.2 = (bf16[1,128,6144]{2,1,0:T(8,128)(2,1)S(1)}, bf16[1,128,6144]{2,1,0:T(8,128)(2,1)}, u32[]{:S(2)}) copy-start(bf16[1,128,6144]{2,1,0:T(8,128)(2,1)} %param.7) | copy-start | bytes 4718596
  23.4 1.5 %copy-start.4 = (bf16[1,128,2048]{2,1,0:T(8,128)(2,1)S(1)}, bf16[1,128,2048]{2,1,0:T(8,128)(2,1)}, u32[]{:S(2)}) copy-start(bf16[1,128,2048]{2,1,0:T(8,128)(2,1)} %param.13) | copy-start | bytes 1572868
  24.9 15.5 %copy-start = (f32[16,128,128]{2,1,0:T(8,128)S(1)}, f32[16,128,128]{2,1,0:T(8,128)}, u32[]{:S(2)}) copy-start(f32[16,128,128]{2,1,0:T(8,128)} %param.9) | copy-start | bytes 3145732
  32.2 2.8 %copy-start.6 = (bf16[2,13,128,1024]{3,2,1,0:T(8,128)(2,1)}, bf16[2,13,128,1024]{3,2,1,0:T(8,128)(2,1)S(1)}, u32[]{:S(2)}) copy-start(bf16[2,13,128,1024]{3,2,1,0:T(8,128)(2,1)S(1)} %get-tuple-element.43.in_ref) | copy-start | bytes 20447236
  35.0 1.0 copy-start.16
  40.4 22.1 %copy-start.9 = (bf16[8,512,128]{2,1,0:T(8,128)(2,1)S(1)}, bf16[8,512,128]{2,1,0:T(8,128)(2,1)}, u32[]{:S(2)}) copy-start(bf16[8,512,128]{2,1,0:T(8,128)(2,1)} %copy-done.8) | copy-start | bytes 3145732
  40.7 24.5 %copy-start.7 = (bf16[2,13,128,1024]{3,2,1,0:T(8,128)(2,1)S(1)}, bf16[2,13,128,1024]{3,2,1,0:T(8,128)(2,1)}, u32[]{:S(2)}) copy-start(bf16[2,13,128,1024]{3,2,1,0:T(8,128)(2,1)} %copy-done.6) | copy-start | bytes 20447236
  62.5 2.7 %copy-start.19 = (f32[2,128,32]{2,1,0:T(8,128)S(1)}, f32[2,128,32]{2,1,0:T(8,128)}, u32[]{:S(2)}) copy-start(f32[2,128,32]{2,1,0:T(8,128)} %copy-done.18) | copy-start | bytes 98308
  63.2 4.5 %copy-start.10 = (bf16[8,528,128]{2,1,0:T(8,128)(2,1)}, bf16[8,528,128]{2,1,0:T(8,128)(2,1)S(1)}, u32[]{:S(2)}) copy-start(bf16[8,528,128]{2,1,0:T(8,128)(2,1)S(1)} %get-tuple-element.45.state_ref.own_ref) | copy-start | bytes 3244036
  63.2 5.4 %collective-permute-start.3 = (bf16[8,528,128]{2,1,0:T(8,128)(2,1)S(1)}, bf16[8,528,128]{2,1,0:T(8,128)(2,1)S(1)}, u32[]{:S(2)}, u32[]{:S(2)}) collective-permute-start(bf16[8,528,128]{2,1,0:T(8,128)(2,1)S(1)} %get-tuple-element.47), channel_id=1, source_target_pairs={{0,1},{1,0},{2,3},{3,2},{4,5},{5,4},{6,7},{7,6},{8,9},{9,8},{10,11... | collective-permute-start | bytes 3244040 | tf_op jit(solution)/shard_map/ppermute | solution.py:621
  67.7 0.9 copy-start.14
  71.0 0.9 copy-start.12
  71.9 1.2 %collective-permute-start.4 = (f32[96,128]{1,0:T(8,128)S(1)}, f32[96,128]{1,0:T(8,128)S(1)}, u32[]{:S(2)}, u32[]{:S(2)}) collective-permute-start(f32[96,128]{1,0:T(8,128)S(1)} %get-tuple-element.49), channel_id=1, source_target_pairs={{0,1},{1,0},{2,3},{3,2},{4,5},{5,4},{6,7},{7,6},{8,9},{9,8},{10,11... | collective-permute-start | bytes 147464 | tf_op jit(solution)/shard_map/ppermute | solution.py:648
  74.0 13.3 %all-to-all-start.2 = ((bf16[16,96,128]{2,1,0:T(8,128)(2,1)}), bf16[16,96,128]{2,1,0:T(8,128)(2,1)S(1)}, u32[]{:S(2)}, u32[]{:S(2)}) async-start(bf16[16,96,128]{2,1,0:T(8,128)(2,1)} %pack.1), calls=%async_computation.2 | async-start | bytes 786432 | tf_op jit(solution)/shard_map/all_to_all | solution.py:715
  77.5 21.6 %collective-permute-start.5 = (bf16[2,16,1024]{2,1,0:T(8,128)(2,1)S(1)}, bf16[2,16,1024]{2,1,0:T(8,128)(2,1)S(1)}, u32[]{:S(2)}, u32[]{:S(2)}) collective-permute-start(bf16[2,16,1024]{2,1,0:T(8,128)(2,1)S(1)} %get-tuple-element.54), channel_id=1, source_target_pairs={{1,0},{2,1},{3,2},{4,3},{5,4},{6,5},{7,6},{8,7},{9,8},{10,9},{11,1... | collective-permute-start | bytes 196616 | tf_op jit(solution)/shard_map/ppermute | solution.py:654
  87.3 9.0 %copy-start.11 = (bf16[8,528,128]{2,1,0:T(8,128)(2,1)S(1)}, bf16[8,528,128]{2,1,0:T(8,128)(2,1)}, u32[]{:S(2)}) copy-start(bf16[8,528,128]{2,1,0:T(8,128)(2,1)} %copy-done.10) | copy-start | bytes 3244036
  87.3 9.0 %copy-start.20 = (f32[2,128,32]{2,1,0:T(8,128)S(1)}, f32[2,128,32]{2,1,0:T(8,128)}, u32[]{:S(2)}) copy-start(f32[2,128,32]{2,1,0:T(8,128)} %copy-done.18) | copy-start | bytes 98308
  88.1 19.3 %all-to-all-start.3 = ((bf16[8,160,128]{2,1,0:T(8,128)(2,1)}), bf16[8,160,128]{2,1,0:T(8,128)(2,1)S(1)}, u32[]{:S(2)}, u32[]{:S(2)}) async-start(bf16[8,160,128]{2,1,0:T(8,128)(2,1)} %fold.1), calls=%async_computation.3 | async-start | bytes 655360 | tf_op jit(solution)/shard_map/all_to_all | solution.py:726
  96.3 1.2 %copy-start.17 = (bf16[2,2,128,1024]{3,2,1,0:T(8,128)(2,1)S(1)}, bf16[2,2,128,1024]{3,2,1,0:T(8,128)(2,1)}, u32[]{:S(2)}) copy-start(bf16[2,2,128,1024]{3,2,1,0:T(8,128)(2,1)} %copy-done.16) | copy-start | bytes 3145732
  97.5 1.6 %copy-start.13 = (bf16[1,24,128,128]{3,2,1,0:T(8,128)(2,1)S(1)}, bf16[1,24,128,128]{3,2,1,0:T(8,128)(2,1)}, u32[]{:S(2)}) copy-start(bf16[1,24,128,128]{3,2,1,0:T(8,128)(2,1)} %copy-done.12) | copy-start | bytes 2359300
  97.5 1.6 %copy-start.15 = (bf16[1,24,128,128]{3,2,1,0:T(8,128)(2,1)S(1)}, bf16[1,24,128,128]{3,2,1,0:T(8,128)(2,1)}, u32[]{:S(2)}) copy-start(bf16[1,24,128,128]{3,2,1,0:T(8,128)(2,1)} %copy-done.14) | copy-start | bytes 2359300
  107.5 4.1 %collective-permute-start.6 = (f32[160,128]{1,0:T(8,128)S(1)}, f32[160,128]{1,0:T(8,128)S(1)}, u32[]{:S(2)}, u32[]{:S(2)}) collective-permute-start(f32[160,128]{1,0:T(8,128)S(1)} %total.1.own_ref), channel_id=1, source_target_pairs={{0,1},{1,0},{2,3},{3,2},{4,5},{5,4},{6,7},{7,6},{8,9},{9,8},{10,11... | collective-permute-start | bytes 245768 | tf_op jit(solution)/shard_map/ppermute | solution.py:738
